TPU v7x, 32 devices: a whole 2x2x4 slice. The times are simulated.
32 devices in a mesh: cam: 4 (over y, x), batch: 8 (over z, core).
Axes of the slice: x: 2, y: 2, z: 4, core: 2. Of those that a mesh axis runs over, the one named last changes fastest.
Arguments:
- images: bfloat16 [4, 4, 256, 2, 9, 512], P('cam', None, 'batch'), may hold values from -6 to 6
- trajectory: bfloat16 [1024, 16, 512], P(('cam', 'batch')), may hold values from -6 to 6
- view_mask: int32 [1024, 4], P(('cam', 'batch')), may hold values from 0 to 1, as said below
- timesteps: int32 [1024], P(('cam', 'batch')), may hold values from 0 to 999
- out_grad: bfloat16 [1024, 8, 512], P(('cam', 'batch')), may hold values from -6 to 6
- encoder_weight: float32 [4, 512, 2, 4608], P('cam', 'batch'), may hold values from -0.09375 to 0.09375
- encoder_affine: float32 [4, 512, 4], P('cam', 'batch'), may hold values from -0.9 to 1.75
- block_convs: float32 [512, 2, 2560], P('batch'), may hold values from -0.125 to 0.125
- film_weight: float32 [512, 2, 1152], P('batch'), may hold values from -0.1875 to 0.1875
- skip_weight: float32 [512, 512], P('batch'), may hold values from -0.25 to 0.25
- down_weight: float32 [512, 1536], P('batch'), may hold values from -0.15625 to 0.15625
- block_affine: float32 [512, 10], P('batch'), may hold values from -0.9 to 1.75
- first_encoder: float32 [4, 512, 2, 4608], P('cam', 'batch'), may hold values from -40 to 40
- first_affine: float32 [4, 512, 4], P('cam', 'batch'), may hold values from -40 to 40
- first_convs: float32 [512, 2, 2560], P('batch'), may hold values from -384 to 384
- first_film: float32 [512, 2, 1152], P('batch'), may hold values from -384 to 384
- first_skip: float32 [512, 512], P('batch'), may hold values from -384 to 384
- first_down: float32 [512, 1536], P('batch'), may hold values from -384 to 384
- first_block: float32 [512, 10], P('batch'), may hold values from -384 to 384
- second_encoder: float32 [4, 512, 2, 4608], P('cam', 'batch'), may hold values from 46.08 to 184.32
- second_affine: float32 [4, 512, 4], P('cam', 'batch'), may hold values from 46.08 to 184.32
- second_convs: float32 [512, 2, 2560], P('batch'), may hold values from 4096 to 16384
- second_film: float32 [512, 2, 1152], P('batch'), may hold values from 4096 to 16384
- second_skip: float32 [512, 512], P('batch'), may hold values from 4096 to 16384
- second_down: float32 [512, 1536], P('batch'), may hold values from 4096 to 16384
- second_block: float32 [512, 10], P('batch'), may hold values from 4096 to 16384
Outputs:
- block_output: bfloat16 [1024, 8, 512], P(('cam', 'batch'))
- trajectory_grad: float32 [1024, 16, 512], P(('cam', 'batch'))
- images_grad: float32 [4, 4, 256, 2, 9, 512], P('cam', None, 'batch')
- next_encoder: float32 [4, 512, 2, 4608], P('cam', 'batch')
- next_affine: float32 [4, 512, 4], P('cam', 'batch')
- next_convs: float32 [512, 2, 2560], P('batch')
- next_film: float32 [512, 2, 1152], P('batch')
- next_skip: float32 [512, 512], P('batch')
- next_down: float32 [512, 1536], P('batch')
- next_block: float32 [512, 10], P('batch')
- mean_encoder: float32 [4, 512, 2, 4608], P('cam', 'batch')
- mean_affine: float32 [4, 512, 4], P('cam', 'batch')
- mean_convs: float32 [512, 2, 2560], P('batch')
- mean_film: float32 [512, 2, 1152], P('batch')
- mean_skip: float32 [512, 512], P('batch')
- mean_down: float32 [512, 1536], P('batch')
- mean_block: float32 [512, 10], P('batch')
- square_encoder: float32 [4, 512, 2, 4608], P('cam', 'batch')
- square_affine: float32 [4, 512, 4], P('cam', 'batch')
- square_convs: float32 [512, 2, 2560], P('batch')
- square_film: float32 [512, 2, 1152], P('batch')
- square_skip: float32 [512, 512], P('batch')
- square_down: float32 [512, 1536], P('batch')
- square_block: float32 [512, 10], P('batch')
Inputs may be any that keep to these rules, and one draw needn't show every extreme that they name: `view_mask`: every sample has at least one present view.
All inputs are finite; a program needn't handle non-finite values.
Results may differ from a plain program's by a relative error of at most 0.012.
Values may be sent and summed in bfloat16 or wider, within the bound.
A program may use at most 384 MiB of HBM per device.

v0:
```python
import math

import jax
import jax.numpy as jnp
from jax import lax
from jax.sharding import PartitionSpec as P

TEMB = 128
GROUPS = 8
STEP = 5


norm_eps = 1e-05
beta_first = 0.5
beta_second = 0.5
adam_eps = 1e-08
rate_matrix = 0.02
rate_vector = 0.2
decay_matrix = 0.01


def mish(tensor):
    return tensor * jnp.tanh(jax.nn.softplus(tensor))


def group_norm(tensor, groups):
    tensor_shape = tensor.shape
    grouped = tensor.reshape(tensor_shape[0], -1, groups, tensor_shape[-1] // groups)
    centred = grouped - jnp.mean(grouped, axis=(1, 3), keepdims=True)
    variance = jnp.mean(centred * centred, axis=(1, 3), keepdims=True)
    return (centred * lax.rsqrt(variance + norm_eps)).reshape(tensor_shape)


def time_embed(steps_given, embed_width):
    half_width = embed_width // 2
    frequency = jnp.exp(
        jnp.arange(half_width, dtype=jnp.float32) * (-math.log(10000.0) / (half_width - 1))
    )
    argument = steps_given.astype(jnp.float32)[:, None] * frequency[None, :]
    return jnp.concatenate([jnp.sin(argument), jnp.cos(argument)], axis=1)


def grid_columns(padded):
    return jnp.concatenate(
        [
            padded[:, step_row : step_row + 3, step_column : step_column + 3]
            for step_row in range(3)
            for step_column in range(3)
        ],
        axis=-1,
    )


def grid_back(grad_columns):
    span_width = grad_columns.shape[-1] // 9
    running = jnp.zeros((grad_columns.shape[0], 5, 5, span_width), jnp.float32)
    for step_row in range(3):
        for step_column in range(3):
            offset = (3 * step_row + step_column) * span_width
            segment = grad_columns[..., offset : offset + span_width]
            running = running + jnp.pad(
                segment, ((0, 0), (step_row, 2 - step_row), (step_column, 2 - step_column), (0, 0))
            )
    return running[:, 1:4, 1:4]


def line_columns(padded, length_all):
    return jnp.concatenate(
        [padded[:, offset : offset + length_all] for offset in range(5)], axis=-1
    )


def line_back(grad_columns, length_all):
    span_width = grad_columns.shape[-1] // 5
    running = jnp.zeros((grad_columns.shape[0], length_all + 4, span_width), jnp.float32)
    for offset in range(5):
        segment = grad_columns[..., offset * span_width : (offset + 1) * span_width]
        running = running + jnp.pad(segment, ((0, 0), (offset, 4 - offset), (0, 0)))
    return running[:, 2 : 2 + length_all]


def apply_rows(columns, weight):
    return lax.dot_general(
        columns, weight, (((columns.ndim - 1,), (1,)), ((), ())), preferred_element_type=jnp.float32
    )


def apply_back(gradient, weight):
    return lax.dot_general(
        gradient,
        weight,
        (((gradient.ndim - 1,), (0,)), ((), ())),
        preferred_element_type=jnp.float32,
    )


def weight_grad(gradient, columns):
    flat_grad = gradient.reshape(-1, gradient.shape[-1])
    flat_columns = columns.reshape(-1, columns.shape[-1])
    return lax.dot_general(
        flat_grad, flat_columns, (((0,), (0,)), ((), ())), preferred_element_type=jnp.float32
    )


def adamw(weight, gradient, moment_one, moment_two, step_rate, weight_decay):
    mean_new = beta_first * moment_one + (1.0 - beta_first) * gradient
    square_new = beta_second * moment_two + (1.0 - beta_second) * gradient * gradient
    mean_hat = mean_new / (1.0 - beta_first**STEP)
    square_hat = square_new / (1.0 - beta_second**STEP)
    weight_new = weight - step_rate * (
        mean_hat / (jnp.sqrt(square_hat) + adam_eps) + weight_decay * weight
    )
    return (weight_new, mean_new, square_new)


def shards(
    images,
    trajectory,
    view_mask,
    timesteps,
    out_grad,
    encoder_weight,
    encoder_affine,
    block_convs,
    film_weight,
    skip_weight,
    down_weight,
    block_affine,
    first_encoder,
    first_affine,
    first_convs,
    first_film,
    first_skip,
    first_down,
    first_block,
    second_encoder,
    second_affine,
    second_convs,
    second_film,
    second_skip,
    second_down,
    second_block,
):
    samples = trajectory.shape[0]
    frames = trajectory.shape[1]
    channels = trajectory.shape[2]
    cameras = images.shape[1]
    observe = images.shape[3]
    groups_encoder = channels // 16
    encoder_full, affine_full, convs_full, film_full, skip_full, down_full, block_full = (
        lax.all_gather(encoder_weight[0].astype(jnp.bfloat16), "batch", axis=0, tiled=True),
        lax.all_gather(encoder_affine[0].astype(jnp.bfloat16), "batch", axis=0, tiled=True),
        lax.all_gather(block_convs.astype(jnp.bfloat16), "batch", axis=0, tiled=True),
        lax.all_gather(film_weight.astype(jnp.bfloat16), "batch", axis=0, tiled=True),
        lax.all_gather(skip_weight.astype(jnp.bfloat16), "batch", axis=0, tiled=True),
        lax.all_gather(down_weight.astype(jnp.bfloat16), "batch", axis=0, tiled=True),
        lax.all_gather(block_affine.astype(jnp.bfloat16), "batch", axis=0, tiled=True),
    )
    encoder_gains = affine_full.astype(jnp.float32)
    block_gains = block_full.astype(jnp.float32)
    pictures = images.reshape(-1, 3, 3, channels)
    picture_values = pictures.astype(jnp.float32)
    columns_one = grid_columns(jnp.pad(pictures, ((0, 0), (1, 1), (1, 1), (0, 0))))
    section_one = apply_rows(columns_one, encoder_full[:, 0])

    def first_piece(tensor, scale_gain, offset):
        return jax.nn.silu(group_norm(tensor, groups_encoder) * scale_gain + offset)

    active_one, back_one = jax.vjp(
        first_piece, section_one, encoder_gains[:, 0], encoder_gains[:, 1]
    )
    active_low = active_one.astype(jnp.bfloat16)
    columns_two = grid_columns(jnp.pad(active_low, ((0, 0), (1, 1), (1, 1), (0, 0))))
    section_two = apply_rows(columns_two, encoder_full[:, 1])

    def second_piece(tensor, scale_gain, offset, residual):
        return jnp.mean(
            jax.nn.silu(group_norm(tensor, groups_encoder) * scale_gain + offset + residual),
            axis=(1, 2),
        )

    pooled, back_two = jax.vjp(
        second_piece, section_two, encoder_gains[:, 2], encoder_gains[:, 3], picture_values
    )
    outgoing = pooled.astype(jnp.bfloat16).reshape(1, cameras, samples, observe, channels)
    arrived = lax.all_to_all(outgoing, "cam", split_axis=1, concat_axis=0, tiled=True)
    present = view_mask.astype(jnp.float32)
    embedded = time_embed(timesteps, TEMB)

    def condition_piece(view_values):
        weighted = jnp.sum(jnp.transpose(present)[:, :, None, None] * view_values, axis=0)
        pooled_views = weighted / jnp.sum(present, axis=1)[:, None, None]
        return mish(jnp.concatenate([pooled_views.reshape(samples, -1), embedded], axis=1))

    condition, back_condition = jax.vjp(condition_piece, arrived[:, 0].astype(jnp.float32))
    condition_low = condition.astype(jnp.bfloat16)
    film_out = (
        jnp.einsum("sk,ojk->sjo", condition_low, film_full, preferred_element_type=jnp.float32)
        + jnp.transpose(block_gains[:, 6:8])[None]
    )
    columns_a = line_columns(jnp.pad(trajectory, ((0, 0), (2, 2), (0, 0))), frames)
    hidden_a = apply_rows(columns_a, convs_full[:, 0]) + block_gains[:, 4]

    def middle_piece(tensor, scale_gain, offset, film_scale, film_shift):
        return (
            mish(group_norm(tensor, GROUPS) * scale_gain + offset) * film_scale[:, None, :]
            + film_shift[:, None, :]
        )

    middle, back_middle = jax.vjp(
        middle_piece, hidden_a, block_gains[:, 0], block_gains[:, 1], film_out[:, 0], film_out[:, 1]
    )
    middle_low = middle.astype(jnp.bfloat16)
    columns_b = line_columns(jnp.pad(middle_low, ((0, 0), (2, 2), (0, 0))), frames)
    hidden_b = apply_rows(columns_b, convs_full[:, 1]) + block_gains[:, 5]
    skip_term = apply_rows(trajectory, skip_full)

    def output_piece(tensor, scale_gain, offset, skip_value, skip_bias):
        return mish(group_norm(tensor, GROUPS) * scale_gain + offset) + skip_value + skip_bias

    summed, back_output = jax.vjp(
        output_piece, hidden_b, block_gains[:, 2], block_gains[:, 3], skip_term, block_gains[:, 8]
    )
    summed_low = summed.astype(jnp.bfloat16)
    pairs = summed_low.reshape(samples, frames // 2, 2, channels)
    even_part = pairs[:, :, 0]
    odd_part = pairs[:, :, 1]
    odd_before = jnp.pad(odd_part, ((0, 0), (1, 0), (0, 0)))[:, :-1]
    columns_down = jnp.concatenate([odd_before, even_part, odd_part], axis=-1)
    block_output = (apply_rows(columns_down, down_full) + block_gains[:, 9]).astype(jnp.bfloat16)
    down_bias_grad = jnp.sum(out_grad.astype(jnp.float32), axis=(0, 1))
    down_grad = weight_grad(out_grad, columns_down)
    down_columns_grad = apply_back(out_grad, down_full)
    tap_before = down_columns_grad[..., :channels]
    tap_even = down_columns_grad[..., channels : 2 * channels]
    tap_odd = down_columns_grad[..., 2 * channels :]
    odd_grad = tap_odd + jnp.pad(tap_before[:, 1:], ((0, 0), (0, 1), (0, 0)))
    summed_grad = jnp.stack([tap_even, odd_grad], axis=2).reshape(samples, frames, channels)
    hidden_b_grad, gain_two_grad, offset_two_grad, skip_grad_term, skip_bias_grad = back_output(
        summed_grad
    )
    skip_low = skip_grad_term.astype(jnp.bfloat16)
    skip_grad = weight_grad(skip_low, trajectory)
    trajectory_skip = apply_back(skip_low, skip_full)
    conv_b_bias = jnp.sum(hidden_b_grad, axis=(0, 1))
    hidden_b_low = hidden_b_grad.astype(jnp.bfloat16)
    conv_b_grad = weight_grad(hidden_b_low, columns_b)
    middle_grad = line_back(apply_back(hidden_b_low, convs_full[:, 1]), frames)
    hidden_a_grad, gain_one_grad, offset_one_grad, scale_grad, shift_grad = back_middle(middle_grad)
    conv_a_bias = jnp.sum(hidden_a_grad, axis=(0, 1))
    hidden_a_low = hidden_a_grad.astype(jnp.bfloat16)
    conv_a_grad = weight_grad(hidden_a_low, columns_a)
    trajectory_grad = (
        line_back(apply_back(hidden_a_low, convs_full[:, 0]), frames) + trajectory_skip
    )
    film_out_grad = jnp.stack([scale_grad, shift_grad], axis=1)
    film_bias_grad = jnp.sum(film_out_grad, axis=0)
    film_low = film_out_grad.astype(jnp.bfloat16)
    film_grad = jnp.einsum(
        "sjo,sk->ojk", film_low, condition_low, preferred_element_type=jnp.float32
    )
    condition_grad = jnp.einsum(
        "sjo,ojk->sk", film_low, film_full, preferred_element_type=jnp.float32
    )
    (views_grad,) = back_condition(condition_grad)
    returned = lax.all_to_all(
        views_grad.astype(jnp.bfloat16)[:, None], "cam", split_axis=0, concat_axis=1, tiled=True
    )
    pooled_grad = returned.reshape(-1, channels).astype(jnp.float32)
    section_two_grad, gain_four_grad, offset_four_grad, image_skip = back_two(pooled_grad)
    section_two_low = section_two_grad.astype(jnp.bfloat16)
    weight_two_grad = weight_grad(section_two_low, columns_two)
    active_grad = grid_back(apply_back(section_two_low, encoder_full[:, 1]))
    section_one_grad, gain_three_grad, offset_three_grad = back_one(active_grad)
    section_one_low = section_one_grad.astype(jnp.bfloat16)
    weight_one_grad = weight_grad(section_one_low, columns_one)
    images_grad = (grid_back(apply_back(section_one_low, encoder_full[:, 0])) + image_skip).reshape(
        images.shape
    )
    encoder_grad = jnp.stack([weight_one_grad, weight_two_grad], axis=1)
    affine_grad = jnp.stack(
        [gain_three_grad, offset_three_grad, gain_four_grad, offset_four_grad], axis=1
    )
    convs_grad = jnp.stack([conv_a_grad, conv_b_grad], axis=1)
    block_grad = jnp.stack(
        [
            gain_one_grad,
            offset_one_grad,
            gain_two_grad,
            offset_two_grad,
            conv_a_bias,
            conv_b_bias,
            film_bias_grad[0],
            film_bias_grad[1],
            skip_bias_grad,
            down_bias_grad,
        ],
        axis=1,
    )
    convs_total, film_total, skip_total, down_total, block_total = (
        lax.psum(convs_grad.astype(jnp.bfloat16), "cam").astype(jnp.float32),
        lax.psum(film_grad.astype(jnp.bfloat16), "cam").astype(jnp.float32),
        lax.psum(skip_grad.astype(jnp.bfloat16), "cam").astype(jnp.float32),
        lax.psum(down_grad.astype(jnp.bfloat16), "cam").astype(jnp.float32),
        lax.psum(block_grad.astype(jnp.bfloat16), "cam").astype(jnp.float32),
    )
    encoder_share, affine_share, convs_share, film_share, skip_share, down_share, block_share = (
        lax.psum_scatter(encoder_grad, "batch", scatter_dimension=0, tiled=True),
        lax.psum_scatter(affine_grad, "batch", scatter_dimension=0, tiled=True),
        lax.psum_scatter(convs_total, "batch", scatter_dimension=0, tiled=True),
        lax.psum_scatter(film_total, "batch", scatter_dimension=0, tiled=True),
        lax.psum_scatter(skip_total, "batch", scatter_dimension=0, tiled=True),
        lax.psum_scatter(down_total, "batch", scatter_dimension=0, tiled=True),
        lax.psum_scatter(block_total, "batch", scatter_dimension=0, tiled=True),
    )
    upd_encoder = adamw(
        encoder_weight,
        encoder_share[None],
        first_encoder,
        second_encoder,
        rate_matrix,
        decay_matrix,
    )
    upd_affine = adamw(
        encoder_affine, affine_share[None], first_affine, second_affine, rate_vector, 0.0
    )
    upd_convs = adamw(
        block_convs, convs_share, first_convs, second_convs, rate_matrix, decay_matrix
    )
    upd_film = adamw(film_weight, film_share, first_film, second_film, rate_matrix, decay_matrix)
    upd_skip = adamw(skip_weight, skip_share, first_skip, second_skip, rate_matrix, decay_matrix)
    upd_down = adamw(down_weight, down_share, first_down, second_down, rate_matrix, decay_matrix)
    upd_block = adamw(block_affine, block_share, first_block, second_block, rate_vector, 0.0)
    return (
        block_output,
        trajectory_grad,
        images_grad,
        upd_encoder[0],
        upd_affine[0],
        upd_convs[0],
        upd_film[0],
        upd_skip[0],
        upd_down[0],
        upd_block[0],
        upd_encoder[1],
        upd_affine[1],
        upd_convs[1],
        upd_film[1],
        upd_skip[1],
        upd_down[1],
        upd_block[1],
        upd_encoder[2],
        upd_affine[2],
        upd_convs[2],
        upd_film[2],
        upd_skip[2],
        upd_down[2],
        upd_block[2],
    )


def solution(mesh):
    return jax.shard_map(
        shards,
        mesh=mesh,
        in_specs=(
            P("cam", None, "batch", None, None, None),
            P(("cam", "batch"), None, None),
            P(("cam", "batch"), None),
            P(("cam", "batch")),
            P(("cam", "batch"), None, None),
            P("cam", "batch", None, None),
            P("cam", "batch", None),
            P("batch", None, None),
            P("batch", None, None),
            P("batch", None),
            P("batch", None),
            P("batch", None),
            P("cam", "batch", None, None),
            P("cam", "batch", None),
            P("batch", None, None),
            P("batch", None, None),
            P("batch", None),
            P("batch", None),
            P("batch", None),
            P("cam", "batch", None, None),
            P("cam", "batch", None),
            P("batch", None, None),
            P("batch", None, None),
            P("batch", None),
            P("batch", None),
            P("batch", None),
        ),
        out_specs=(
            P(("cam", "batch"), None, None),
            P(("cam", "batch"), None, None),
            P("cam", None, "batch", None, None, None),
            P("cam", "batch", None, None),
            P("cam", "batch", None),
            P("batch", None, None),
            P("batch", None, None),
            P("batch", None),
            P("batch", None),
            P("batch", None),
            P("cam", "batch", None, None),
            P("cam", "batch", None),
            P("batch", None, None),
            P("batch", None, None),
            P("batch", None),
            P("batch", None),
            P("batch", None),
            P("cam", "batch", None, None),
            P("cam", "batch", None),
            P("batch", None, None),
            P("batch", None, None),
            P("batch", None),
            P("batch", None),
            P("batch", None),
        ),
        check_vma=False,
    )
```

profile of v0, /device:TPU:0, one launch (start us, length us, event | category | flops | bytes accessed | tf_op | source)
XLA Modules:
  0.0 1125.9 jit_solution(247833370392999757)
XLA Ops:
  16.7 15.8 %all-gather.2 = bf16[8,64,10]{1,2,0:T(8,128)(2,1)S(1)} all-gather(bf16[1,64,10]{1,2,0:T(8,128)(2,1)S(1)} %convert_bitcast_fusion), channel_id=1, replica_groups=mesh['cam'=4,'batch'=8] {'batch'}, dimensions={0}, use_global_device_ids=true | all-gather | bytes 11520 | tf_op jit(solution)/shard_map/all_gather | solution.py:157
  42.8 6.6 concatenate.44
  49.4 6.6 copy.344
  56.1 15.2 %all-gather.1 = bf16[1,512,4]{2,0,1:T(2,128)(2,1)S(1)} all-gather(bf16[1,64,4]{2,0,1:T(2,128)(2,1)S(1)} %copy.339), channel_id=3, replica_groups=mesh['cam'=4,'batch'=8] {'batch'}, dimensions={1}, use_global_device_ids=true | all-gather | bytes 4608 | tf_op jit(solution)/shard_map/all_gather | solution.py:152
  72.9 18.6 %all_gather.26 = bf16[512,512]{1,0:T(8,128)(2,1)} all-gather(bf16[64,512]{1,0:T(8,128)(2,1)S(1)} %convert_element_type.234), channel_id=1, replica_groups=mesh['cam'=4,'batch'=8] {'batch'}, dimensions={0}, use_global_device_ids=true | all-gather | bytes 589824 | tf_op jit(solution)/shard_map/all_gather | solution.py:155
  109.8 7.2 constant_dynamic-update-slice_fusion.12
  118.7 23.1 %reshape.418 = f32[256,9,32,16]{3,2,0,1:T(8,128)} reshape(f32[1,4,32,2,9,512]{5,3,2,1,4,0:T(2,128)} %copy.344) | data formatting | bytes 9437184 | tf_op jit(solution)/shard_map/convert_element_type | solution.py:162
  141.8 23.2 %copy.345 = f32[256,9,32,16]{0,2,3,1:T(8,128)} copy(f32[256,9,32,16]{3,2,0,1:T(8,128)} %reshape.418) | data formatting | bytes 9437184 | tf_op jit(solution)/shard_map/convert_element_type | solution.py:162
  200.3 21.6 %fusion.135 = (f32[256,32]{0,1:T(8,128)S(1)}, f32[256,9,32,16]{0,2,3,1:T(8,128)S(1)}) fusion(bf16[32,16,4608]{2,1,0:T(8,128)(2,1)S(1)} %bitcast.254, bf16[256,9,4608]{2,0,1:T(8,128)(2,1)} %constant_dynamic-update-slice_fusion.1), kind=kOutput, calls=%fused_computation.321 | convolution fusion | flops 10872807424 | bytes 30703616 | tf_op jit(solution)/shard_map/dot_general | solution.py:83
  255.8 21.0 %fusion.136 = (f32[256,32]{0,1:T(8,128)S(1)}, f32[256,9,32,16]{0,2,3,1:T(8,128)S(1)}) fusion(bf16[256,9,4608,1]{2,0,3,1:T(8,128)(2,1)} %bitcast.24, bf16[32,16,4608]{2,1,0:T(8,128)(2,1)S(1)} %bitcast.253), kind=kOutput, calls=%fused_computation.322 | convolution fusion | flops 10872807424 | bytes 30703616 | tf_op jit(solution)/shard_map/dot_general | solution.py:83
  369.7 18.0 %psum.39 = bf16[512,10]{0,1:T(8,128)(2,1)S(1)} all-reduce(bf16[512,10]{0,1:T(8,128)(2,1)S(1)} %stack.105), channel_id=1, replica_groups=mesh['cam'=4,'batch'=8] {'cam'}, use_global_device_ids=true, to_apply=%region_53.55 | all-reduce | flops 5120 | bytes 20480 | tf_op jit(solution)/shard_map/psum | solution.py:305
  396.1 8.7 multiply_reduce_fusion
  415.9 20.7 %fusion.11 = f32[256,3,3,4608]{3,0,2,1:T(8,128)} fusion(bf16[256,3,3,512]{0,3,2,1:T(8,128)(2,1)S(1)} %bitcast.255, bf16[512,2,4608]{2,0,1:T(8,128)(2,1)} %bitcast.248), kind=kOutput, calls=%fused_computation.52 | convolution fusion | flops 10871635968 | bytes 49545216 | tf_op jit(solution)/shard_map/dot_general | solution.py:89
  436.6 29.6 %fusion.129 = (f32[256,3,3,512]{3,0,2,1:T(8,128)}, f32[256,3,3,512]{3,0,2,1:T(8,128)}, f32[256,3,3,512]{3,0,2,1:T(8,128)}, f32[256,3,3,512]{3,0,2,1:T(8,128)}, f...) fusion(f32[256,3,3,4608]{3,0,2,1:T(8,128)} %fusion.11), kind=kLoop, calls=%fused_computation.315 | loop fusion | bytes 84934656 | tf_op jit(solution)/shard_map/slice | solution.py:60
  466.3 7.9 pad_add_fusion.1
  476.6 9.8 multiply_reduce_fusion.1
  487.4 69.2 %all-reduce.41.cloned.1.call-done = (bf16[512,2,1152]{0,2,1:T(8,128)(2,1)}, bf16[512,1536]{0,1:T(8,128)(2,1)}, bf16[512,2,2560]{2,0,1:T(8,128)(2,1)}, bf16[512,512]{1,0:T(8,128)(2,1)}) async-done(((bf16[512,2,1152]{0,2,1:T(8,128)(2,1)}, bf16[512,1536]{0,1:T(8,128)(2,1)}, bf16[512,2,2560]{2,0,1:T(8,128)(2,1)}, bf16[512,512]{1,0:T(8,128)(2,1)}), (bf16[512,2,1152]{0,2,1:T(8,128)(2,1)}, ...) | async-done | bytes 9699344 | tf_op jit(solution)/shard_map/psum | solution.py:302
  558.8 7.3 copy.373
  569.3 7.9 convert_element_type.249
  588.8 6.8 multiply_reduce_fusion.2
  606.8 14.5 %convolution_bitcast_fusion = f32[512,1,4608]{2,0,1:T(8,128)S(1)} fusion(bf16[256,3,3,512]{0,3,2,1:T(8,128)(2,1)S(1)} %bitcast.256, bf16[256,3,3,4608]{3,0,2,1:T(8,128)(2,1)} %fusion.33), kind=kOutput, calls=%fused_computation.21 | convolution fusion | flops 10871635968 | bytes 33030144 | tf_op jit(solution)/shard_map/dot_general | solution.py:100
  621.3 15.2 %convolution_bitcast_fusion.1 = f32[512,1,4608]{2,0,1:T(8,128)S(1)} fusion(bf16[256,3,3,512]{0,3,2,1:T(8,128)(2,1)} %bitcast.257, bf16[256,3,3,4608]{3,0,2,1:T(8,128)(2,1)} %get-tuple-element.260), kind=kOutput, calls=%fused_computation.22 | convolution fusion | flops 10871635968 | bytes 33030144 | tf_op jit(solution)/shard_map/dot_general | solution.py:100
  636.5 6.8 pad_maximum_fusion
  645.2 7.3 copy.360
  668.5 20.4 %fusion.9 = f32[256,3,3,4608]{3,0,2,1:T(8,128)} fusion(bf16[256,3,3,512]{0,3,2,1:T(8,128)(2,1)S(1)} %bitcast.258, bf16[512,2,4608]{2,0,1:T(8,128)(2,1)} %bitcast.249), kind=kOutput, calls=%fused_computation.50 | convolution fusion | flops 10871635968 | bytes 49545216 | tf_op jit(solution)/shard_map/dot_general | solution.py:89
  688.9 28.6 %fusion.128 = (f32[256,3,3,512]{3,0,2,1:T(8,128)}, f32[256,3,3,512]{3,0,2,1:T(8,128)}, f32[256,3,3,512]{3,0,2,1:T(8,128)}, f32[256,3,3,512]{3,0,2,1:T(8,128)}, f...) fusion(f32[256,3,3,4608]{3,0,2,1:T(8,128)} %fusion.9), kind=kLoop, calls=%fused_computation.314 | loop fusion | bytes 84934656 | tf_op jit(solution)/shard_map/slice | solution.py:60
  717.5 12.0 %pad_add_fusion = f32[256,5,5,512]{3,0,2,1:T(8,128)} fusion(f32[256,3,3,512]{3,0,2,1:T(8,128)} %get-tuple-element.237, f32[256,3,3,512]{3,0,2,1:T(8,128)} %get-tuple-element.238, f32[256,3,3,512]{3,0,2,1:T(8,128)} %get-tuple-element.230), kind=kLoop, calls=%fused_computation.19 | loop fusion | flops 6553600 | bytes 27262976 | tf_op jit(solution)/shard_map/add | solution.py:61
  731.0 11.9 %fusion.8 = f32[256,3,3,512]{3,0,2,1:T(8,128)} fusion(f32[256,3,3,512]{3,0,2,1:T(8,128)S(1)} %copy-done.5, f32[256,3,3,512]{3,0,2,1:T(8,128)S(1)} %copy-done.6, f32[256,3,3,512]{3,0,2,1:T(8,128)} %get-tuple-element.233, f32[256,3,3,512]{3,0,2,1:T(8,128)} %get-tuple-element.234, f32[256,3,3,512]{3,0,2,1:T(8,128)} %get-tuple-element.235, ...), kind=kLoop, calls=%fused_computation.37 | loop fusion | flops 23592960 | bytes 45355008 | tf_op jit(solution)/shard_map/add | solution.py:277
  742.9 7.2 reshape.417
  766.0 38.4 %reduce-scatter.21.cloned.1.call-done = f32[64,1536]{1,0:T(8,128)} async-done(((f32[512,1536]{1,0:T(8,128)}), f32[64,1536]{1,0:T(8,128)}) %reduce-scatter.21.cloned.1.call-update) | async-done | bytes 393232 | tf_op jit(solution)/shard_map/reduce_scatter | solution.py:313
  806.8 108.4 %reduce-scatter.15.cloned.1.call-done = f32[64,2,2560]{2,0,1:T(8,128)} async-done(((f32[512,2,2560]{2,0,1:T(8,128)}), f32[64,2,2560]{2,0,1:T(8,128)}) %reduce-scatter.15.cloned.1.call-update) | async-done | bytes 1310736 | tf_op jit(solution)/shard_map/reduce_scatter | solution.py:310
  924.7 179.1 %reduce-scatter.13.cloned.1.call-done = f32[64,2,4608]{2,0,1:T(8,128)} async-done(((f32[512,2,4608]{2,0,1:T(8,128)}), f32[64,2,4608]{2,0,1:T(8,128)}) %reduce-scatter.13.cloned.1.call-update) | async-done | bytes 2359312 | tf_op jit(solution)/shard_map/reduce_scatter | solution.py:308
  (495 shorter events, 314.6 us)
Async XLA Ops:
  7.2 26.6 %copy-start.20 = (bf16[1,4,32,2,9,512]{5,3,4,2,1,0:T(2,128)(2,1)S(1)}, bf16[1,4,32,2,9,512]{5,3,4,2,1,0:T(2,128)(2,1)}, u32[]{:S(2)}) copy-start(bf16[1,4,32,2,9,512]{5,3,4,2,1,0:T(2,128)(2,1)} %param.27) | copy-start | bytes 7077892
  7.2 171.6 %all-gather.12.cloned.1.call-start = ((), (), s32[]{:S(2)}) async-start(), calls=%async_computation.10 | async-start | bytes 1769472 | tf_op jit(solution)/shard_map/all_gather | solution.py:156
  9.2 175.4 %all-gather.8.cloned.1.call-start = ((), (), s32[]{:S(2)}) async-start(), calls=%async_computation.8 | async-start | bytes 5898240 | tf_op jit(solution)/shard_map/all_gather | solution.py:153
  11.6 182.3 %all-gather.14.cloned.1.call-start = ((), (), s32[]{:S(2)}) async-start(), calls=%async_computation.14 | async-start | bytes 10616832 | tf_op jit(solution)/shard_map/all_gather | solution.py:151
  14.7 284.6 %all-gather.10.cloned.1.call-start = ((), (), s32[]{:S(2)}) async-start(), calls=%async_computation.9 | async-start | bytes 2654208 | tf_op jit(solution)/shard_map/all_gather | solution.py:154
  42.8 67.0 %copy-start = (bf16[256,3,3,512]{3,0,2,1:T(8,128)(2,1)}, bf16[256,3,3,512]{3,0,2,1:T(8,128)(2,1)S(1)}, u32[]{:S(2)}) copy-start(bf16[256,3,3,512]{3,0,2,1:T(8,128)(2,1)S(1)} %reshape.408) | copy-start | bytes 7077892
  49.4 42.1 %copy-start.10 = (bf16[32,16,512]{2,1,0:T(8,128)(2,1)S(1)}, bf16[32,16,512]{2,1,0:T(8,128)(2,1)}, u32[]{:S(2)}) copy-start(bf16[32,16,512]{2,1,0:T(8,128)(2,1)} %param.28) | copy-start | bytes 1572868
  72.2 25.8 %copy-start.79 = (f32[512]{0:T(512)}, f32[512]{0:T(512)S(1)}, u32[]{:S(2)}) copy-start(f32[512]{0:T(512)S(1)} %get-tuple-element.191) | copy-start | bytes 6148
  72.2 173.8 %copy-start.69 = (f32[512]{0:T(512)}, f32[512]{0:T(512)S(1)}, u32[]{:S(2)}) copy-start(f32[512]{0:T(512)S(1)} %get-tuple-element.194) | copy-start | bytes 6148
  72.2 173.8 %copy-start.73 = (f32[512]{0:T(512)}, f32[512]{0:T(512)S(1)}, u32[]{:S(2)}) copy-start(f32[512]{0:T(512)S(1)} %get-tuple-element.193) | copy-start | bytes 6148
  72.4 205.0 %copy-start.62 = (f32[32,16]{0,1:T(8,128)}, f32[32,16]{0,1:T(8,128)S(1)}, u32[]{:S(2)}) copy-start(f32[32,16]{0,1:T(8,128)S(1)} %copy.342) | copy-start | bytes 6148
  72.9 204.5 %copy-start.67 = (f32[32,16]{0,1:T(8,128)}, f32[32,16]{0,1:T(8,128)S(1)}, u32[]{:S(2)}) copy-start(f32[32,16]{0,1:T(8,128)S(1)} %copy.343) | copy-start | bytes 6148
  141.8 23.3 %copy-start.17 = (bf16[256,3,3,512]{3,0,2,1:T(8,128)(2,1)S(1)}, bf16[256,3,3,512]{3,0,2,1:T(8,128)(2,1)}, u32[]{:S(2)}) copy-start(bf16[256,3,3,512]{3,0,2,1:T(8,128)(2,1)} %get-tuple-element.261) | copy-start | bytes 7077892
  189.6 103.6 %copy-start.64 = (f32[32,8]{1,0:T(8,128)}, f32[32,8]{1,0:T(8,128)S(1)}, u32[]{:S(2)}) copy-start(f32[32,8]{1,0:T(8,128)S(1)} %reduce_sum.461) | copy-start | bytes 3076
  255.7 21.6 %slice-start.6 = ((s8[4718592]{0:T(1024)(128)(4,1)}), s8[4194304]{0:T(1024)(128)(4,1)S(1)}, s32[]{:S(2)}) async-start(s8[4718592]{0:T(1024)(128)(4,1)} %bitcast.235), calls=%async_computation.26 | async-start | bytes 8388608
  255.7 21.6 %slice-start.7 = ((s8[4718592]{0:T(1024)(128)(4,1)}), s8[524288]{0:T(1024)(128)(4,1)S(1)}, s32[]{:S(2)}) async-start(s8[4718592]{0:T(1024)(128)(4,1)} %bitcast.235), calls=%async_computation.27 | async-start | bytes 1048576
  281.0 20.7 %copy-start.71 = (f32[512,1]{0,1:T(1,128)S(1)}, f32[512,1]{0,1:T(1,128)}, u32[]{:S(2)}) copy-start(f32[512,1]{0,1:T(1,128)} %get-tuple-element.283) | copy-start | bytes 6148
  281.0 20.7 %copy-start.77 = (f32[512,1]{0,1:T(1,128)S(1)}, f32[512,1]{0,1:T(1,128)}, u32[]{:S(2)}) copy-start(f32[512,1]{0,1:T(1,128)} %get-tuple-element.282) | copy-start | bytes 6148
  289.2 9.5 all-to-all-start
  292.9 263.7 %all-reduce.41.cloned.1.call-start = ((), (), s32[]{:S(2)}) async-start(), calls=%async_computation.19 | async-start | bytes 19398656 | tf_op jit(solution)/shard_map/psum | solution.py:302
  348.1 21.3 %copy-start.18 = (f32[32,16,512]{2,1,0:T(8,128)}, f32[32,16,512]{2,1,0:T(8,128)S(1)}, u32[]{:S(2)}) copy-start(f32[32,16,512]{2,1,0:T(8,128)S(1)} %get-tuple-element.223) | copy-start | bytes 3145732
  365.9 22.9 %all-to-all-start.1 = ((bf16[4,1,32,2,512]{4,3,2,1,0:T(2,128)(2,1)}), bf16[4,1,32,2,512]{4,3,2,1,0:T(2,128)(2,1)S(1)}, u32[]{:S(2)}, u32[]{:S(2)}) async-start(bf16[4,1,32,2,512]{4,3,2,1,0:T(2,128)(2,1)} %multiply_convert_fusion.1), calls=%async_computation.1 | async-start | bytes 524288 | tf_op jit(solution)/shard_map/all_to_all | solution.py:266
  369.3 297.3 %reduce-scatter.23.cloned.1.call-start = ((), (), s32[]{:S(2)}) async-start(), calls=%async_computation.17 | async-start | bytes 294912
  388.6 367.9 %reduce-scatter.19.cloned.1.call-start = ((), (), s32[]{:S(2)}) async-start(), calls=%async_computation.15 | async-start | bytes 294912
  487.3 270.7 %reduce-scatter.17.cloned.1.call-start = ((), (), s32[]{:S(2)}) async-start(), calls=%async_computation.13 | async-start | bytes 1179648 | tf_op jit(solution)/shard_map/reduce_scatter | solution.py:312
  558.7 203.1 %all-reduce.39.cloned.1.call-start = ((), (), s32[]{:S(2)}) async-start(), calls=%async_computation.18 | async-start | bytes 9437184
  566.1 238.3 %reduce-scatter.21.cloned.1.call-start = ((), (), s32[]{:S(2)}) async-start(), calls=%async_computation.16 | async-start | bytes 3538944 | tf_op jit(solution)/shard_map/reduce_scatter | solution.py:313
  569.3 346.0 %reduce-scatter.15.cloned.1.call-start = ((), (), s32[]{:S(2)}) async-start(), calls=%async_computation.12 | async-start | bytes 11796480 | tf_op jit(solution)/shard_map/reduce_scatter | solution.py:310
  577.2 526.6 %reduce-scatter.13.cloned.1.call-start = ((), (), s32[]{:S(2)}) async-start(), calls=%async_computation.11 | async-start | bytes 21233664 | tf_op jit(solution)/shard_map/reduce_scatter | solution.py:308
  756.5 47.9 %copy-start.36 = (f32[64,1536]{1,0:T(8,128)S(1)}, f32[64,1536]{1,0:T(8,128)}, u32[]{:S(2)}) copy-start(f32[64,1536]{1,0:T(8,128)} %param.37) | copy-start | bytes 1179652
  756.5 158.8 %copy-start.27 = (f32[64,2,2560]{2,1,0:T(2,128)S(1)}, f32[64,2,2560]{2,1,0:T(2,128)}, u32[]{:S(2)}) copy-start(f32[64,2,2560]{2,1,0:T(2,128)} %param.34) | copy-start | bytes 3932164
  918.5 185.3 %copy-start.26 = (f32[1,64,2,4608]{3,2,1,0:T(2,128)S(1)}, f32[1,64,2,4608]{3,2,1,0:T(2,128)}, u32[]{:S(2)}) copy-start(f32[1,64,2,4608]{3,2,1,0:T(2,128)} %param.32) | copy-start | bytes 7077892
  (100 other events, 599.9 us)
Sparse Core Ops, SparseCore 0:
  10.3 27.9 all-gather.11
  40.4 61.6 all-gather.7
  104.3 89.4 all-gather.13
  195.9 30.0 all-gather.9
  361.0 195.5 all-reduce.40
  559.2 30.6 reduce-scatter.22
  592.8 28.4 reduce-scatter.18
  624.2 30.4 reduce-scatter.16
  657.0 104.7 all-reduce.38
  764.0 40.3 reduce-scatter.20
  806.7 108.4 reduce-scatter.14
  917.5 186.3 reduce-scatter.12
where the time goes:
time: 1140 us; the launch traced here: 1130 us
  waiting for transfers between devices  407 us (36%)
  local copies, waits for them, and re-layouts  314 us (28%)
  matrix products  158 us (14%)
  other arithmetic  155 us (14%)
  blocking collectives  67.5 us (6%)
  between operations  16.9 us (1%)
    reduce_scatter x1, waiting for transfers between devices, shards(): lax.psum_scatter(encoder_grad, 'batch', scatter_dimension=0, tiled=True)  179 us
    reduce_scatter x1, waiting for transfers between devices, shards(): lax.psum_scatter(convs_total, 'batch', scatter_dimension=0, tiled=True)  108 us
    unnamed x284, local copies, waits for them, and re-layouts  91.2 us
    psum x1, waiting for transfers between devices, shards(): lax.psum(film_grad.astype(jnp.bfloat16), 'cam').astype(jnp.float32)  69.2 us
    slice x2, local copies, waits for them, and re-layouts, grid_back(): segment = grad_columns[..., offset:offset + span_width]  58.2 us
    dot_general x6, matrix products, apply_rows(): lax.dot_general(columns, weight, (((columns.ndim - 1,), (1,)), ((), ())),...  56.7 us
    convert_element_type x3, local copies, waits for them, and re-layouts, shards(): picture_values = pictures.astype(jnp.float32)  52.8 us
    dot_general x6, matrix products, apply_back(): lax.dot_general(gradient, weight, (((gradient.ndim - 1,), (0,)), ((), ())...  51.9 us
  transfers between devices with their start and end apart: 14, of which 7 were waited for; matrix products, arithmetic and copies ran while one was open for 48% of the time, Pallas kernels for 0%

commit v1 on v0

v1 whole, which is shorter than its diff:
```python
import functools
import math

import jax
import jax.numpy as jnp
from jax import lax
from jax.experimental import pallas as pl
from jax.experimental.pallas import tpu as pltpu
from jax.sharding import PartitionSpec as P

TEMB = 128
GROUPS = 8
STEP = 5

norm_eps = 1e-05
beta_first = 0.5
beta_second = 0.5
adam_eps = 1e-08
rate_matrix = 0.02
rate_vector = 0.2
decay_matrix = 0.01

CH = 512
BLK = 128
ENC_GROUP = 16
f32 = jnp.float32
bf16 = jnp.bfloat16
VMEM_BYTES = 60 * 1024 * 1024

NT = (((1,), (1,)), ((), ()))
NN = (((1,), (0,)), ((), ()))
TN = (((0,), (0,)), ((), ()))


def dot(a, b, dims=NN):
    return lax.dot_general(a, b, dims, preferred_element_type=f32)


def group_ones(width, group):
    rows = lax.broadcasted_iota(jnp.int32, (width, width), 0) // group
    cols = lax.broadcasted_iota(jnp.int32, (width, width), 1) // group
    return jnp.where(rows == cols, 1.0, 0.0).astype(bf16)


def group_sum(v, ones):
    high = v.astype(bf16)
    rest = v - high.astype(f32)
    middle = rest.astype(bf16)
    low = (rest - middle.astype(f32)).astype(bf16)
    return dot(high, ones) + dot(middle, ones) + dot(low, ones)


def sigmoid(v):
    return 1.0 / (1.0 + jnp.exp(-v))


def mish_pair(v):
    e = jnp.exp(jnp.minimum(v, 20.0))
    n = e * (e + 2.0)
    inv = 1.0 / (n + 2.0)
    t = n * inv
    return v * t, t + v * (4.0 * e * (1.0 + e)) * inv * inv


def mish_value(v):
    e = jnp.exp(jnp.minimum(v, 20.0))
    n = e * (e + 2.0)
    return v * (n / (n + 2.0))


def span(i):
    return range(max(0, 1 - i), min(2, 3 - i) + 1)


def enc_fwd_kernel(x_ref, w1_ref, w2_ref, aff_ref, z1_ref, r1_ref, a_ref, z2_ref, r2_ref, feat_ref):
    ones = group_ones(BLK, ENC_GROUP)
    inv_n = 1.0 / (9 * ENC_GROUP)

    def conv_norm(src_ref, w_ref, z_ref, r_ref, j):
        wrows = pl.ds(pl.multiple_of(j * BLK, BLK), BLK)
        total = None
        lanes = [pl.ds(pl.multiple_of(p * CH + j * BLK, BLK), BLK) for p in range(9)]
        for p in range(9):
            r, c = divmod(p, 3)
            bs = span(c)
            acc = None
            for a in span(r):
                start = (3 * (r + a - 1) + c + bs[0] - 1) * CH
                wstart = (3 * a + bs[0]) * CH
                wide = len(bs) * CH
                part = dot(src_ref[:, start : start + wide], w_ref[wrows, wstart : wstart + wide], NT)
                acc = part if acc is None else acc + part
            z_ref[:, lanes[p]] = acc
            total = acc if total is None else total + acc
        mean = group_sum(total, ones) * inv_n
        var = None
        for p in range(9):
            centred = z_ref[:, lanes[p]] - mean
            sq = centred * centred
            var = sq if var is None else var + sq
        rstd = lax.rsqrt(group_sum(var, ones) * inv_n + norm_eps)
        r_ref[:, wrows] = rstd
        return wrows, lanes, mean, rstd

    def first(j, carry):
        wrows, lanes, mean, rstd = conv_norm(x_ref, w1_ref, z1_ref, r1_ref, j)
        gain, offset = aff_ref[0:1, wrows], aff_ref[1:2, wrows]
        for p in range(9):
            z = (z1_ref[:, lanes[p]] - mean) * rstd
            z1_ref[:, lanes[p]] = z
            u = z * gain + offset
            a_ref[:, lanes[p]] = (u * sigmoid(u)).astype(bf16)
        return carry

    def second(j, carry):
        wrows, lanes, mean, rstd = conv_norm(a_ref, w2_ref, z2_ref, r2_ref, j)
        gain, offset = aff_ref[2:3, wrows], aff_ref[3:4, wrows]
        total = None
        for p in range(9):
            z = (z2_ref[:, lanes[p]] - mean) * rstd
            z2_ref[:, lanes[p]] = z
            u = z * gain + offset + x_ref[:, lanes[p]].astype(f32)
            act = u * sigmoid(u)
            total = act if total is None else total + act
        feat_ref[:, wrows] = (total * (1.0 / 9.0)).astype(bf16)
        return carry

    lax.fori_loop(0, CH // BLK, first, 0)
    lax.fori_loop(0, CH // BLK, second, 0)


def enc_bwd_kernel(
    x_ref, a_ref, w1_ref, w2_ref, z1_ref, r1_ref, z2_ref, r2_ref, aff_ref, gp_ref,
    dw1_ref, dw2_ref, ig_ref, ag_ref, g_ref, gt_ref, da_ref, pos_ref,
):
    rows = x_ref.shape[0]
    ones = group_ones(BLK, ENC_GROUP)
    inv_n = 1.0 / (9 * ENC_GROUP)

    def norm_back(du_ref, z_ref, r_ref, j, gain, row):
        wrows = pl.ds(pl.multiple_of(j * BLK, BLK), BLK)
        lanes = [pl.ds(pl.multiple_of(p * CH + j * BLK, BLK), BLK) for p in range(9)]
        s0 = jnp.zeros((rows, BLK), f32)
        s1 = jnp.zeros((rows, BLK), f32)
        for p in range(9):
            du = du_ref[:, lanes[p]]
            s0 = s0 + du
            s1 = s1 + du * z_ref[:, lanes[p]]
        ag_ref[row : row + 1, wrows] = jnp.sum(s1, axis=0, keepdims=True)
        ag_ref[row + 1 : row + 2, wrows] = jnp.sum(s0, axis=0, keepdims=True)
        m0 = group_sum(s0 * gain, ones) * inv_n
        m1 = group_sum(s1 * gain, ones) * inv_n
        rstd = r_ref[:, wrows]
        for p in range(9):
            dv = (du_ref[:, lanes[p]] * gain - m0 - z_ref[:, lanes[p]] * m1) * rstd
            g_ref[:, lanes[p]] = dv.astype(bf16)
            gt_ref[wrows, p * rows : (p + 1) * rows] = jnp.transpose(dv).astype(bf16)

    def weight_back(src_ref, dw_ref):
        for p in range(9):
            pos_ref[p * rows : (p + 1) * rows, :] = src_ref[:, p * CH : (p + 1) * CH]
        for a in range(3):
            for b in range(3):
                r_lo, r_hi = max(0, 1 - a), min(2, 3 - a)
                c_lo, c_hi = max(0, 1 - b), min(2, 3 - b)
                if b == 1:
                    runs = [(3 * r_lo, 3 * (r_hi - r_lo + 1))]
                else:
                    runs = [(3 * r + c_lo, c_hi - c_lo + 1) for r in range(r_lo, r_hi + 1)]
                shift = 3 * (a - 1) + b - 1
                for half in range(2):
                    hrows = slice(half * 256, half * 256 + 256)
                    acc = None
                    for p, n in runs:
                        part = dot(
                            gt_ref[hrows, p * rows : (p + n) * rows],
                            pos_ref[(p + shift) * rows : (p + shift + n) * rows, :],
                        )
                        acc = part if acc is None else acc + part
                    t = 3 * a + b
                    dw_ref[hrows, t * CH : (t + 1) * CH] = acc.astype(bf16)

    def input_back(w_ref, q):
        r, c = divmod(q, 3)
        acc = None
        for a in range(3):
            for b in range(3):
                pr, pc = r - a + 1, c - b + 1
                if 0 <= pr < 3 and 0 <= pc < 3:
                    p, t = 3 * pr + pc, 3 * a + b
                    part = dot(g_ref[:, p * CH : (p + 1) * CH], w_ref[:, t * CH : (t + 1) * CH])
                    acc = part if acc is None else acc + part
        return acc

    def second(j, carry):
        wrows = pl.ds(pl.multiple_of(j * BLK, BLK), BLK)
        gain, offset = aff_ref[2:3, wrows], aff_ref[3:4, wrows]
        pooled = gp_ref[:, wrows].astype(f32) * (1.0 / 9.0)
        for p in range(9):
            lanes = pl.ds(pl.multiple_of(p * CH + j * BLK, BLK), BLK)
            u = z2_ref[:, lanes] * gain + offset + x_ref[:, lanes].astype(f32)
            s = sigmoid(u)
            ig_ref[:, lanes] = pooled * (s * (1.0 + u * (1.0 - s)))
        norm_back(ig_ref, z2_ref, r2_ref, j, gain, 2)
        return carry

    lax.fori_loop(0, CH // BLK, second, 0)
    weight_back(a_ref, dw2_ref)
    for q in range(9):
        da_ref[:, q * CH : (q + 1) * CH] = input_back(w2_ref, q)

    def first(j, carry):
        wrows = pl.ds(pl.multiple_of(j * BLK, BLK), BLK)
        gain, offset = aff_ref[0:1, wrows], aff_ref[1:2, wrows]
        for p in range(9):
            lanes = pl.ds(pl.multiple_of(p * CH + j * BLK, BLK), BLK)
            u = z1_ref[:, lanes] * gain + offset
            s = sigmoid(u)
            da_ref[:, lanes] = da_ref[:, lanes] * (s * (1.0 + u * (1.0 - s)))
        norm_back(da_ref, z1_ref, r1_ref, j, gain, 0)
        return carry

    lax.fori_loop(0, CH // BLK, first, 0)
    weight_back(x_ref, dw1_ref)
    for q in range(9):
        ig_ref[:, q * CH : (q + 1) * CH] = ig_ref[:, q * CH : (q + 1) * CH] + input_back(w1_ref, q)


def temporal_kernel(
    traj_ref, og_ref, arr_ref, mask_ref, emb_ref, wa_ref, wb_ref, f0_ref, f1_ref, ws_ref, wd_ref, aff_ref,
    out_ref, tg_ref, dviews_ref, dwa_ref, dwb_ref, df0_ref, df1_ref, dws_ref, dwd_ref, ag_ref,
    pad_t, pad_m, pad_h, za_ref, zb_ref, sum_ref,
):
    ns = mask_ref.shape[0]
    rows = traj_ref.shape[0]
    nf = rows // ns
    edge = 2 * ns
    ones = group_ones(CH, CH // GROUPS)
    inv_n = 1.0 / (nf * (CH // GROUPS))
    aff = lambda i: aff_ref[i : i + 1, :]

    def frames(v):
        return v.reshape(nf, ns, CH)

    def fill(pad_ref, v):
        pad_ref[0:edge, :] = jnp.zeros((edge, CH), bf16)
        pad_ref[edge : edge + rows, :] = v
        pad_ref[edge + rows : edge + rows + edge, :] = jnp.zeros((edge, CH), bf16)

    def conv5(pad_ref, w_ref):
        acc = None
        for t in range(5):
            part = dot(pad_ref[t * ns : t * ns + rows, :], w_ref[:, t * CH : (t + 1) * CH], NT)
            acc = part if acc is None else acc + part
        return acc

    def conv5_back(pad_ref, w_ref):
        acc = None
        for t in range(5):
            part = dot(pad_ref[(4 - t) * ns : (4 - t) * ns + rows, :], w_ref[:, t * CH : (t + 1) * CH])
            acc = part if acc is None else acc + part
        return acc

    def norm(v):
        v = frames(v)
        mean = group_sum(jnp.sum(v, axis=0), ones) * inv_n
        centred = v - mean[None]
        rstd = lax.rsqrt(group_sum(jnp.sum(centred * centred, axis=0), ones) * inv_n + norm_eps)
        return centred * rstd[None], rstd

    def norm_back(du, z, rstd, gain):
        s0 = jnp.sum(du, axis=0)
        s1 = jnp.sum(du * z, axis=0)
        m0 = group_sum(s0 * gain, ones) * inv_n
        m1 = group_sum(s1 * gain, ones) * inv_n
        dv = (du * gain[None] - m0[None] - z * m1[None]) * rstd[None]
        return dv, jnp.sum(s1, axis=0, keepdims=True), jnp.sum(s0, axis=0, keepdims=True)

    mask = mask_ref[...]
    count = jnp.sum(mask, axis=1, keepdims=True)
    cams = arr_ref.shape[0]
    pooled = None
    for cam in range(cams):
        part = mask[:, cam : cam + 1] * arr_ref[cam].astype(f32)
        pooled = part if pooled is None else pooled + part
    pooled = pooled / count
    pm, pd = mish_pair(pooled)
    cond_v = pm.astype(bf16)
    cond_e = mish_value(emb_ref[...]).astype(bf16)
    width = cond_v.shape[1]
    film = []
    for i, w_ref in ((6, f0_ref), (7, f1_ref)):
        film.append(dot(cond_v, w_ref[:, :width], NT) + dot(cond_e, w_ref[:, width:], NT) + aff(i))
    scale, shift = film

    fill(pad_t, traj_ref[...])
    za, rstd_a = norm(conv5(pad_t, wa_ref) + aff(4))
    za_ref[...] = za.reshape(rows, CH)
    act_a = mish_value(za * aff(0)[None] + aff(1)[None])
    fill(pad_m, (act_a * scale[None] + shift[None]).astype(bf16).reshape(rows, CH))
    zb, rstd_b = norm(conv5(pad_m, wb_ref) + aff(5))
    zb_ref[...] = zb.reshape(rows, CH)
    skip = frames(dot(traj_ref[...], ws_ref[...], NT)) + aff(8)[None]
    summed = (mish_value(zb * aff(2)[None] + aff(3)[None]) + skip).astype(bf16)
    pairs = summed.reshape(nf // 2, 2, ns, CH)
    half = rows // 2
    sum_ref[0:ns, :] = jnp.zeros((ns, CH), bf16)
    sum_ref[ns : ns + half, :] = pairs[:, 1].reshape(half, CH)
    sum_ref[ns + half : ns + 2 * half, :] = pairs[:, 0].reshape(half, CH)
    taps = (0, ns + half, ns)
    out = None
    og = og_ref[...]
    dcols = []
    for t in range(3):
        cols = sum_ref[taps[t] : taps[t] + half, :]
        w = wd_ref[:, t * CH : (t + 1) * CH]
        part = dot(cols, w, NT)
        out = part if out is None else out + part
        dcols.append(dot(og, w).reshape(nf // 2, ns, CH))
        dwd_ref[:, t * CH : (t + 1) * CH] = dot(og, cols, TN).astype(bf16)
    out_ref[...] = (out + aff(9)).astype(bf16)
    ag_ref[9:10, :] = jnp.sum(og.astype(f32), axis=0, keepdims=True)

    before = jnp.concatenate([dcols[0][1:], jnp.zeros((1, ns, CH), f32)], axis=0)
    dsum = jnp.stack([dcols[1], dcols[2] + before], axis=1).reshape(nf, ns, CH)
    ag_ref[8:9, :] = jnp.sum(dsum, axis=(0, 1)).reshape(1, CH)
    dskip = dsum.astype(bf16).reshape(rows, CH)
    dws_ref[...] = dot(dskip, traj_ref[...], TN).astype(bf16)
    tg_ref[...] = dot(dskip, ws_ref[...])
    zb = frames(zb_ref[...])
    _, slope = mish_pair(zb * aff(2)[None] + aff(3)[None])
    dhb, ag_ref[2:3, :], ag_ref[3:4, :] = norm_back(dsum * slope, zb, rstd_b, aff(2))
    ag_ref[5:6, :] = jnp.sum(dhb, axis=(0, 1)).reshape(1, CH)
    fill(pad_h, dhb.astype(bf16).reshape(rows, CH))
    hb = pad_h[edge : edge + rows, :]
    for t in range(5):
        dwb_ref[:, t * CH : (t + 1) * CH] = dot(hb, pad_m[t * ns : t * ns + rows, :], TN).astype(bf16)
    dmid = frames(conv5_back(pad_h, wb_ref))
    za = frames(za_ref[...])
    act_a, slope = mish_pair(za * aff(0)[None] + aff(1)[None])
    dscale = jnp.sum(dmid * act_a, axis=0)
    dshift = jnp.sum(dmid, axis=0)
    dha, ag_ref[0:1, :], ag_ref[1:2, :] = norm_back(dmid * scale[None] * slope, za, rstd_a, aff(0))
    ag_ref[4:5, :] = jnp.sum(dha, axis=(0, 1)).reshape(1, CH)
    ag_ref[6:7, :] = jnp.sum(dscale, axis=0, keepdims=True)
    ag_ref[7:8, :] = jnp.sum(dshift, axis=0, keepdims=True)
    ag_ref[10:, :] = jnp.zeros((ag_ref.shape[0] - 10, CH), f32)
    fill(pad_h, dha.astype(bf16).reshape(rows, CH))
    ha = pad_h[edge : edge + rows, :]
    for t in range(5):
        dwa_ref[:, t * CH : (t + 1) * CH] = dot(ha, pad_t[t * ns : t * ns + rows, :], TN).astype(bf16)
    tg_ref[...] = tg_ref[...] + conv5_back(pad_h, wa_ref)

    dcond = None
    for grad, w_ref, dw_ref in ((dscale, f0_ref, df0_ref), (dshift, f1_ref, df1_ref)):
        low = grad.astype(bf16)
        dw_ref[:, :width] = dot(low, cond_v, TN).astype(bf16)
        dw_ref[:, width:] = dot(low, cond_e, TN).astype(bf16)
        part = dot(low, w_ref[:, :width])
        dcond = part if dcond is None else dcond + part
    dviews = dcond * pd / count
    for cam in range(cams):
        dviews_ref[cam] = (mask[:, cam : cam + 1] * dviews).astype(bf16)


def call(kernel, outs, scratch=(), cost=None):
    return pl.pallas_call(
        kernel,
        out_shape=[jax.ShapeDtypeStruct(s, d) for s, d in outs],
        scratch_shapes=list(scratch),
        compiler_params=pltpu.CompilerParams(vmem_limit_bytes=VMEM_BYTES),
        cost_estimate=cost,
    )


def time_embed(steps_given, embed_width):
    half_width = embed_width // 2
    frequency = jnp.exp(
        jnp.arange(half_width, dtype=jnp.float32) * (-math.log(10000.0) / (half_width - 1))
    )
    argument = steps_given.astype(jnp.float32)[:, None] * frequency[None, :]
    return jnp.concatenate([jnp.sin(argument), jnp.cos(argument)], axis=1)


def adamw(weight, gradient, moment_one, moment_two, step_rate, weight_decay):
    mean_new = beta_first * moment_one + (1.0 - beta_first) * gradient
    square_new = beta_second * moment_two + (1.0 - beta_second) * gradient * gradient
    mean_hat = mean_new / (1.0 - beta_first**STEP)
    square_hat = square_new / (1.0 - beta_second**STEP)
    weight_new = weight - step_rate * (
        mean_hat / (jnp.sqrt(square_hat) + adam_eps) + weight_decay * weight
    )
    return (weight_new, mean_new, square_new)


def shards(
    images, trajectory, view_mask, timesteps, out_grad,
    encoder_weight, encoder_affine, block_convs, film_weight, skip_weight, down_weight, block_affine,
    first_encoder, first_affine, first_convs, first_film, first_skip, first_down, first_block,
    second_encoder, second_affine, second_convs, second_film, second_skip, second_down, second_block,
):
    ns, nf, ch = trajectory.shape
    cams = images.shape[1]
    obs = images.shape[3]
    n_img = cams * images.shape[2] * obs
    cond = film_weight.shape[2]

    def gather(v):
        return lax.all_gather(v.astype(bf16), "batch", axis=0, tiled=True)

    w1 = gather(encoder_weight[0, :, 0])
    w2 = gather(encoder_weight[0, :, 1])
    enc_aff = jnp.pad(jnp.transpose(gather(encoder_affine[0])).astype(f32), ((0, 4), (0, 0)))
    wa = gather(block_convs[:, 0])
    wb = gather(block_convs[:, 1])
    f0 = gather(film_weight[:, 0])
    f1 = gather(film_weight[:, 1])
    ws = gather(skip_weight)
    wd = gather(down_weight)
    blk_aff = jnp.pad(jnp.transpose(gather(block_affine)).astype(f32), ((0, 6), (0, 0)))

    x = images.reshape(n_img, 9 * ch)
    wide = 9 * ch
    z1, r1, act, z2, r2, feat = call(
        enc_fwd_kernel,
        [((n_img, wide), f32), ((n_img, ch), f32), ((n_img, wide), bf16),
         ((n_img, wide), f32), ((n_img, ch), f32), ((n_img, ch), bf16)],
    )(x, w1, w2, enc_aff)

    outgoing = feat.reshape(1, cams, ns, obs * ch)
    arrived = lax.all_to_all(outgoing, "cam", split_axis=1, concat_axis=0, tiled=True)[:, 0]
    present = view_mask.astype(f32)
    embedded = time_embed(timesteps, TEMB)
    traj_fm = jnp.transpose(trajectory, (1, 0, 2)).reshape(nf * ns, ch)
    og_fm = jnp.transpose(out_grad, (1, 0, 2)).reshape(nf // 2 * ns, ch)
    rows = nf * ns
    (out_fm, tg_fm, dviews, dwa, dwb, df0, df1, dws, dwd, blk_grad) = call(
        temporal_kernel,
        [((rows // 2, ch), bf16), ((rows, ch), f32), ((cams, ns, obs * ch), bf16),
         ((ch, 5 * ch), bf16), ((ch, 5 * ch), bf16), ((ch, cond), bf16), ((ch, cond), bf16),
         ((ch, ch), bf16), ((ch, 3 * ch), bf16), ((16, ch), f32)],
        [pltpu.VMEM((rows + 4 * ns, ch), bf16)] * 3
        + [pltpu.VMEM((rows, ch), f32)] * 2
        + [pltpu.VMEM((rows + ns, ch), bf16)],
    )(traj_fm, og_fm, arrived, present, embedded, wa, wb, f0, f1, ws, wd, blk_aff)
    block_output = jnp.transpose(out_fm.reshape(nf // 2, ns, ch), (1, 0, 2))
    trajectory_grad = jnp.transpose(tg_fm.reshape(nf, ns, ch), (1, 0, 2))

    returned = lax.all_to_all(dviews[:, None], "cam", split_axis=0, concat_axis=1, tiled=True)
    gp = returned.reshape(n_img, ch)
    dw1, dw2, ig, aff_grad = call(
        enc_bwd_kernel,
        [((ch, wide), bf16), ((ch, wide), bf16), ((n_img, wide), f32), ((8, ch), f32)],
        [pltpu.VMEM((n_img, wide), bf16), pltpu.VMEM((ch, 9 * n_img), bf16),
         pltpu.VMEM((n_img, wide), f32), pltpu.VMEM((9 * n_img, ch), bf16)],
    )(x, act, w1, w2, z1, r1, z2, r2, enc_aff, gp)
    images_grad = ig.reshape(images.shape)

    def scatter(v):
        return lax.psum_scatter(v, "batch", scatter_dimension=0, tiled=True)

    def total(v):
        return scatter(lax.psum(v, "cam")).astype(f32)

    convs_share = jnp.stack([total(dwa), total(dwb)], axis=1)
    film_share = jnp.stack([total(df0), total(df1)], axis=1)
    skip_share = total(dws)
    down_share = total(dwd)
    block_share = scatter(lax.psum(jnp.transpose(blk_grad[:10]), "cam"))
    encoder_share = jnp.stack([scatter(dw1).astype(f32), scatter(dw2).astype(f32)], axis=1)
    affine_share = scatter(jnp.transpose(aff_grad[:4]))

    upd = (
        adamw(encoder_weight, encoder_share[None], first_encoder, second_encoder, rate_matrix, decay_matrix),
        adamw(encoder_affine, affine_share[None], first_affine, second_affine, rate_vector, 0.0),
        adamw(block_convs, convs_share, first_convs, second_convs, rate_matrix, decay_matrix),
        adamw(film_weight, film_share, first_film, second_film, rate_matrix, decay_matrix),
        adamw(skip_weight, skip_share, first_skip, second_skip, rate_matrix, decay_matrix),
        adamw(down_weight, down_share, first_down, second_down, rate_matrix, decay_matrix),
        adamw(block_affine, block_share, first_block, second_block, rate_vector, 0.0),
    )
    return (
        (block_output, trajectory_grad, images_grad)
        + tuple(u[0] for u in upd)
        + tuple(u[1] for u in upd)
        + tuple(u[2] for u in upd)
    )


def solution(mesh):
    sample = P(("cam", "batch"))
    params = (P("cam", "batch"), P("cam", "batch")) + (P("batch"),) * 5
    images_spec = P("cam", None, "batch")
    return jax.shard_map(
        shards,
        mesh=mesh,
        in_specs=(images_spec, sample, sample, sample, sample) + params * 3,
        out_specs=(sample, sample, images_spec) + params * 3,
        check_vma=False,
    )
```

time: 1140 us -> 766 us (0.67)
  local copies, waits for them, and re-layouts: 314 us -> 63.9 us
  matrix products: 158 us -> 0 us
  other arithmetic: 155 us -> 13.1 us
  Pallas kernels: 0 us -> 120 us
  waiting for transfers between devices: 407 us -> 476 us
    dot_general x21 -> x0, matrix products: 158 us -> none  [the longest x6 56.7 us: apply_rows(): lax.dot_general(columns, weight, (((columns.ndim - 1,), (1,)), ((), ())),...]
    all_gather x4 -> x7, waiting for transfers between devices: 4.29 us -> 139 us  [gather(): return lax.all_gather(v.astype(bf16), 'batch', axis=0, tiled=True)]
    pallas_call x0 -> x3, Pallas kernels: none -> 120 us  [the longest x1 51.8 us: shards(): call(enc_bwd_kernel, [((ch, wide), bf16), ((ch, wide), bf16), ((n_img, wi...]
    reduce_scatter x4 -> x8, waiting for transfers between devices: 326 us -> 240 us  [scatter(): return lax.psum_scatter(v, 'batch', scatter_dimension=0, tiled=True)]
    convert_element_type x10 -> x2, local copies, waits for them, and re-layouts: 72.9 us -> 0.8 us  [the longest x1 0.68 us: shards(): present = view_mask.astype(f32)]
    slice x10 -> x3, local copies, waits for them, and re-layouts: 69.1 us -> 2.69 us  [the longest x1 1.09 us: shards(): w2 = gather(encoder_weight[0, :, 1])]
    reduce_sum x29 -> x0, other arithmetic: 56.9 us -> none  [the longest x8 14.4 us: group_norm(): centred = grouped - jnp.mean(grouped, axis=(1, 3), keepdims=True)]
    unnamed x284 -> x76, local copies, waits for them, and re-layouts: 91.2 us -> 43.5 us
  transfers between devices with their start and end apart: 14 -> 20, of which waited for: 7 -> 15; matrix products, arithmetic and copies ran while one was open for 48% -> 8% of each run, Pallas kernels for 0% -> 13%
where the time goes in v1:
time: 766 us; the launch traced here: 756 us
  waiting for transfers between devices  476 us (62%)
  Pallas kernels  120 us (16%)
  local copies, waits for them, and re-layouts  63.9 us (8%)
  blocking collectives  59.1 us (8%)
  between operations  14.9 us (2%)
  other arithmetic  13.1 us (2%)
  starting transfers between devices  7.95 us (1%)
    reduce_scatter x8, waiting for transfers between devices, scatter(): return lax.psum_scatter(v, 'batch', scatter_dimension=0, tiled=True)  240 us
    all_gather x7, waiting for transfers between devices, gather(): return lax.all_gather(v.astype(bf16), 'batch', axis=0, tiled=True)  139 us
    psum x1, waiting for transfers between devices, total(): return scatter(lax.psum(v, 'cam')).astype(f32)  56.9 us
    pallas_call x1, Pallas kernels, shards(): call(enc_bwd_kernel, [((ch, wide), bf16), ((ch, wide), bf16), ((n_img, wi...  51.8 us
    all_gather x3, blocking collectives, gather(): return lax.all_gather(v.astype(bf16), 'batch', axis=0, tiled=True)  49.1 us
    pallas_call x1, Pallas kernels, shards(): call(enc_fwd_kernel, [((n_img, wide), f32), ((n_img, ch), f32), ((n_img,...  46.7 us
    unnamed x76, local copies, waits for them, and re-layouts  43.5 us
    unnamed x20, waiting for transfers between devices  35.6 us
  transfers between devices with their start and end apart: 20, of which 15 were waited for; matrix products, arithmetic and copies ran while one was open for 8% of the time, Pallas kernels for 13%

profile of v1, /device:TPU:0, one launch (start us, length us, event | category | flops | bytes accessed | tf_op | source)
XLA Modules:
  0.0 755.6 jit_solution(17705602691876363193)
XLA Ops:
  16.1 15.9 %all-gather.7 = bf16[8,64,10]{1,2,0:T(8,128)(2,1)S(1)} all-gather(bf16[1,64,10]{1,2,0:T(8,128)(2,1)S(1)} %convert_bitcast_fusion), channel_id=1, replica_groups=mesh['cam'=4,'batch'=8] {'batch'}, dimensions={0}, use_global_device_ids=true | all-gather | bytes 11520 | tf_op jit(solution)/shard_map/all_gather | solution.py:409
  32.2 15.1 %all-gather.2 = bf16[1,512,4]{2,0,1:T(2,128)(2,1)S(1)} all-gather(bf16[1,64,4]{2,0,1:T(2,128)(2,1)S(1)} %copy.154), channel_id=4, replica_groups=mesh['cam'=4,'batch'=8] {'batch'}, dimensions={1}, use_global_device_ids=true | all-gather | bytes 4608 | tf_op jit(solution)/shard_map/all_gather | solution.py:409
  50.3 2.7 copy.152
  53.0 3.8 copy.190
  58.9 8.1 %all-gather.20.cloned.1.call-done = bf16[1,512,1,4608]{3,1,2,0:T(8,128)(2,1)} async-done(((bf16[1,64,1,4608]{3,1,2,0:T(8,128)(2,1)}), bf16[1,512,1,4608]{3,1,2,0:T(8,128)(2,1)}) %all-gather.20.cloned.1.call-update) | async-done | bytes 4718608 | tf_op jit(solution)/shard_map/all_gather | solution.py:409
  67.1 52.8 %all-gather.18.cloned.1.call-done = bf16[1,512,1,4608]{3,1,2,0:T(8,128)(2,1)} async-done(((bf16[1,64,1,4608]{3,1,2,0:T(8,128)(2,1)}), bf16[1,512,1,4608]{3,1,2,0:T(8,128)(2,1)}) %all-gather.18.cloned.1.call-update) | async-done | bytes 4718608 | tf_op jit(solution)/shard_map/all_gather | solution.py:409
  119.8 46.7 %shard_map.433 = (f32[256,4608]{1,0:T(8,128)}, f32[256,512]{1,0:T(8,128)}, bf16[256,4608]{1,0:T(8,128)(2,1)}, f32[256,4608]{1,0:T(8,128)}, f32[256,512]{1,0:T(8,128)}, /*index=5*/bf16[256,512]{1,0:T(8,128)(2,1)}) custom-call(bf16[256,4608]{1,0:T(8,128)(2,1)} %bitcast.58, bf16[512,4608]{1,0:T(8,128)(2,1)} %bitcast.62, bf16[512,4608]{1,0:T(8,128)(2,1)} %bitcast.60, ...), custom_call_target="tpu_custom_call" | custom-call | tf_op jit(solution)/shard_map/pallas_call | solution.py:424
  168.3 3.7 all-to-all-start
  172.0 18.1 %all_gather.37.ws_ref = bf16[512,512]{1,0:T(8,128)(2,1)} all-gather(bf16[64,512]{1,0:T(8,128)(2,1)S(1)} %convert_element_type.80), channel_id=1, replica_groups=mesh['cam'=4,'batch'=8] {'batch'}, dimensions={0}, use_global_device_ids=true | all-gather | bytes 589824 | tf_op jit(solution)/shard_map/all_gather | solution.py:409
  190.1 6.9 all-gather.16.cloned.1.call-done.wd_ref
  197.0 35.7 %all-gather.24.cloned.1.call-done = bf16[512,1,2560]{2,0,1:T(8,128)(2,1)} async-done(((bf16[64,1,2560]{2,0,1:T(8,128)(2,1)}), bf16[512,1,2560]{2,0,1:T(8,128)(2,1)}) %all-gather.24.cloned.1.call-update) | async-done | bytes 2621456 | tf_op jit(solution)/shard_map/all_gather | solution.py:409
  232.7 35.1 %all-gather.22.cloned.1.call-done = bf16[512,1,2560]{2,0,1:T(8,128)(2,1)} async-done(((bf16[64,1,2560]{2,0,1:T(8,128)(2,1)}), bf16[512,1,2560]{2,0,1:T(8,128)(2,1)}) %all-gather.22.cloned.1.call-update) | async-done | bytes 2621456 | tf_op jit(solution)/shard_map/all_gather | solution.py:409
  268.6 21.7 %shard_map.434 = (bf16[256,512]{1,0:T(8,128)(2,1)}, f32[512,512]{1,0:T(8,128)}, bf16[4,32,1024]{2,1,0:T(8,128)(2,1)}, bf16[512,2560]{1,0:T(8,128)(2,1)}, bf16[51...) custom-call(bf16[512,512]{1,0:T(8,128)(2,1)} %bitcast.67, ...), custom_call_target="tpu_custom_call" | custom-call | tf_op jit(solution)/shard_map/pallas_call | solution.py:437
  293.6 3.7 all-to-all-start.1
  298.2 4.8 all-to-all-done.1
  303.9 51.8 %shard_map.435 = (bf16[512,4608]{1,0:T(8,128)(2,1)}, bf16[512,4608]{1,0:T(8,128)(2,1)}, f32[256,4608]{1,0:T(8,128)}, f32[8,512]{1,0:T(8,128)}) custom-call(bf16[256,4608]{1,0:T(8,128)(2,1)} %bitcast.59, bf16[256,4608]{1,0:T(8,128)(2,1)} %get-tuple-element.47.a_ref, bf16[512,4608]{1,0:T(8,128)(2,1)} %bitcast.63, bf16[512,4608]{1,0:T(8,128)(2,1)} %bitcast.61, ...), custom_call_target="tpu_custom_call" | custom-call | tf_op jit(solution)/shard_map/pallas_call | solution.py:451
  357.3 30.5 %reduce-scatter.25.cloned.1.call-done = bf16[64,1152]{1,0:T(8,128)(2,1)} async-done(((bf16[512,1152]{1,0:T(8,128)(2,1)}), bf16[64,1152]{1,0:T(8,128)(2,1)}) %reduce-scatter.25.cloned.1.call-update) | async-done | bytes 147472 | tf_op jit(solution)/shard_map/reduce_scatter | solution.py:460
  387.9 35.5 %reduce-scatter.29.cloned.1.call-done = bf16[64,1536]{1,0:T(8,128)(2,1)} async-done(((bf16[512,1536]{1,0:T(8,128)(2,1)}), bf16[64,1536]{1,0:T(8,128)(2,1)}) %reduce-scatter.29.cloned.1.call-update) | async-done | bytes 196624 | tf_op jit(solution)/shard_map/reduce_scatter | solution.py:460
  423.4 37.6 %reduce-scatter.19.cloned.1.call-done = bf16[64,2560]{1,0:T(8,128)(2,1)} async-done(((bf16[512,2560]{1,0:T(8,128)(2,1)}), bf16[64,2560]{1,0:T(8,128)(2,1)}) %reduce-scatter.19.cloned.1.call-update) | async-done | bytes 327696 | tf_op jit(solution)/shard_map/reduce_scatter | solution.py:460
  461.0 39.0 %reduce-scatter.21.cloned.1.call-done = bf16[64,2560]{1,0:T(8,128)(2,1)} async-done(((bf16[512,2560]{1,0:T(8,128)(2,1)}), bf16[64,2560]{1,0:T(8,128)(2,1)}) %reduce-scatter.21.cloned.1.call-update) | async-done | bytes 327696 | tf_op jit(solution)/shard_map/reduce_scatter | solution.py:460
  502.5 2.8 copy.226
  505.3 27.0 %reduce-scatter.33.cloned.1.call-done = f32[64,10]{1,0:T(8,128)} async-done(((f32[512,10]{1,0:T(8,128)}), f32[64,10]{1,0:T(8,128)}) %reduce-scatter.33.cloned.1.call-update) | async-done | bytes 2576
  533.1 10.0 %psum.62 = f32[64,10]{0,1:T(8,128)S(1)} all-reduce(f32[64,10]{0,1:T(8,128)S(1)} %copy.189), channel_id=1, replica_groups=mesh['cam'=4,'batch'=8] {'cam'}, use_global_device_ids=true, to_apply=%region_15.16 | all-reduce | flops 640 | bytes 5120 | tf_op jit(solution)/shard_map/psum | solution.py:469
  543.8 7.0 reshape.180
  550.9 10.3 %copy.176 = f32[1,4,32,2,9,512]{5,3,4,2,1,0:T(2,128)} copy(f32[1,4,32,2,9,512]{5,4,3,2,1,0:T(8,128)} %reshape.180) | data formatting | bytes 9437184
  565.0 56.9 %all-reduce.5.cloned.1.call-done = (bf16[64,2560]{1,0:T(8,128)(2,1)}, bf16[64,2560]{1,0:T(8,128)(2,1)}, bf16[64,1152]{1,0:T(8,128)(2,1)}, bf16[64,1152]{1,0:T(8,...) async-done(((bf16[64,2560]{1,0:T(8,128)(2,1)}, bf16[64,2560]{1,0:T(8,128)(2,1)}, bf16[64,1152]{1,0:T(8,128)(2,1)}, bf16[64,1152]{1,0:T(8,128)(2,1)}, ...) | async-done | bytes 1212432 | tf_op jit(solution)/shard_map/psum | solution.py:463
  636.9 42.2 %reduce-scatter.15.cloned.1.call-done = bf16[64,4608]{1,0:T(8,128)(2,1)} async-done(((bf16[512,4608]{1,0:T(8,128)(2,1)}), bf16[64,4608]{1,0:T(8,128)(2,1)}) %reduce-scatter.15.cloned.1.call-update) | async-done | bytes 589840 | tf_op jit(solution)/shard_map/reduce_scatter | solution.py:460
  679.1 55.5 %reduce-scatter.17.cloned.1.call-done = bf16[64,4608]{1,0:T(8,128)(2,1)} async-done(((bf16[512,4608]{1,0:T(8,128)(2,1)}), bf16[64,4608]{1,0:T(8,128)(2,1)}) %reduce-scatter.17.cloned.1.call-update) | async-done | bytes 589840 | tf_op jit(solution)/shard_map/reduce_scatter | solution.py:460
  734.6 4.3 multiply_subtract_fusion
  738.9 3.2 copy.177
  742.1 3.2 copy.180
  745.3 3.2 copy.183
  (143 shorter events, 45.7 us)
Async XLA Ops:
  7.2 59.9 %all-gather.20.cloned.1.call-start = ((), (), s32[]{:S(2)}) async-start(), calls=%async_computation.16 | async-start | bytes 5308416 | tf_op jit(solution)/shard_map/all_gather | solution.py:409
  10.4 109.4 %all-gather.18.cloned.1.call-start = ((), (), s32[]{:S(2)}) async-start(), calls=%async_computation.15 | async-start | bytes 5308416 | tf_op jit(solution)/shard_map/all_gather | solution.py:409
  11.2 178.9 %all-gather.28.cloned.1.call-start = ((), (), s32[]{:S(2)}) async-start(), calls=%async_computation.20 | async-start | bytes 1327104 | tf_op jit(solution)/shard_map/all_gather | solution.py:409
  12.0 178.1 %all-gather.26.cloned.1.call-start = ((), (), s32[]{:S(2)}) async-start(), calls=%async_computation.19 | async-start | bytes 1327104 | tf_op jit(solution)/shard_map/all_gather | solution.py:409
  12.6 19.6 %copy-start.9 = (f32[64,512]{1,0:T(8,128)S(1)}, f32[64,512]{1,0:T(8,128)}, u32[]{:S(2)}) copy-start(f32[64,512]{1,0:T(8,128)} %param.35) | copy-start | bytes 393220
  12.7 184.3 %all-gather.16.cloned.1.call-start = ((), (), s32[]{:S(2)}) async-start(), calls=%async_computation.12 | async-start | bytes 1769472 | tf_op jit(solution)/shard_map/all_gather | solution.py:409
  13.4 35.8 %copy-start.8 = (bf16[32,16,512]{2,1,0:T(8,128)(2,1)S(1)}, bf16[32,16,512]{2,1,0:T(8,128)(2,1)}, u32[]{:S(2)}) copy-start(bf16[32,16,512]{2,1,0:T(8,128)(2,1)} %param.27) | copy-start | bytes 1572868
  13.4 219.3 %all-gather.24.cloned.1.call-start = ((), (), s32[]{:S(2)}) async-start(), calls=%async_computation.18 | async-start | bytes 2949120 | tf_op jit(solution)/shard_map/all_gather | solution.py:409
  14.6 253.2 %all-gather.22.cloned.1.call-start = ((), (), s32[]{:S(2)}) async-start(), calls=%async_computation.17 | async-start | bytes 2949120 | tf_op jit(solution)/shard_map/all_gather | solution.py:409
  168.3 99.5 %all-to-all-start = ((bf16[1,4,32,1024]{3,2,0,1:T(8,128)(2,1)}), bf16[1,4,32,1024]{3,2,0,1:T(8,128)(2,1)S(1)}, u32[]{:S(2)}, u32[]{:S(2)}) async-start(bf16[1,4,32,1024]{3,2,0,1:T(8,128)(2,1)} %bitcast.10), calls=%async_computation | async-start | bytes 524288 | tf_op jit(solution)/shard_map/all_to_all | solution.py:431
  172.0 185.4 %reduce-scatter.27.cloned.1.call-start = ((), (), s32[]{:S(2)}) async-start(), calls=%async_computation.25 | async-start | bytes 589824 | tf_op jit(solution)/shard_map/reduce_scatter | solution.py:460
  290.2 67.1 %reduce-scatter.23.cloned.1.call-start = ((), (), s32[]{:S(2)}) async-start(), calls=%async_computation.23 | async-start | bytes 1327104 | tf_op jit(solution)/shard_map/reduce_scatter | solution.py:460
  291.0 96.9 %reduce-scatter.25.cloned.1.call-start = ((), (), s32[]{:S(2)}) async-start(), calls=%async_computation.24 | async-start | bytes 1327104 | tf_op jit(solution)/shard_map/reduce_scatter | solution.py:460
  291.6 131.8 %reduce-scatter.29.cloned.1.call-start = ((), (), s32[]{:S(2)}) async-start(), calls=%async_computation.26 | async-start | bytes 1769472 | tf_op jit(solution)/shard_map/reduce_scatter | solution.py:460
  292.3 168.7 %reduce-scatter.19.cloned.1.call-start = ((), (), s32[]{:S(2)}) async-start(), calls=%async_computation.21 | async-start | bytes 2949120 | tf_op jit(solution)/shard_map/reduce_scatter | solution.py:460
  292.3 4.9 copy-start.20
  292.9 207.1 %reduce-scatter.21.cloned.1.call-start = ((), (), s32[]{:S(2)}) async-start(), calls=%async_computation.22 | async-start | bytes 2949120 | tf_op jit(solution)/shard_map/reduce_scatter | solution.py:460
  293.6 9.4 %all-to-all-start.1 = ((bf16[4,1,32,1024]{3,2,1,0:T(8,128)(2,1)}), bf16[4,1,32,1024]{3,2,1,0:T(8,128)(2,1)S(1)}, u32[]{:S(2)}, u32[]{:S(2)}) async-start(bf16[4,1,32,1024]{3,2,1,0:T(8,128)(2,1)} %bitcast.23), calls=%async_computation.1 | async-start | bytes 524288 | tf_op jit(solution)/shard_map/all_to_all | solution.py:449
  297.3 235.0 %reduce-scatter.33.cloned.1.call-start = ((), (), s32[]{:S(2)}) async-start(), calls=%async_computation.28 | async-start | bytes 294912
  298.2 265.4 %reduce-scatter.31.cloned.1.call-start = ((), (), s32[]{:S(2)}) async-start(), calls=%async_computation.27 | async-start | bytes 294912
  357.2 264.7 %all-reduce.5.cloned.1.call-start = ((), (), s32[]{:S(2)}) async-start(), calls=%async_computation.29 | async-start | bytes 2424832 | tf_op jit(solution)/shard_map/psum | solution.py:463
  500.0 179.1 %reduce-scatter.15.cloned.1.call-start = ((), (), s32[]{:S(2)}) async-start(), calls=%async_computation.13 | async-start | bytes 5308416 | tf_op jit(solution)/shard_map/reduce_scatter | solution.py:460
  500.6 234.0 %reduce-scatter.17.cloned.1.call-start = ((), (), s32[]{:S(2)}) async-start(), calls=%async_computation.14 | async-start | bytes 5308416 | tf_op jit(solution)/shard_map/reduce_scatter | solution.py:460
  501.2 41.9 %copy-start.21 = (f32[64,10]{0,1:T(8,128)S(1)}, f32[64,10]{0,1:T(8,128)}, u32[]{:S(2)}) copy-start(f32[64,10]{0,1:T(8,128)} %param.44) | copy-start | bytes 7684
  501.2 41.9 %copy-start.22 = (f32[64,10]{0,1:T(8,128)S(1)}, f32[64,10]{0,1:T(8,128)}, u32[]{:S(2)}) copy-start(f32[64,10]{0,1:T(8,128)} %param.51) | copy-start | bytes 7684
  550.8 13.6 %copy-start.24 = (f32[1,64,4]{1,2,0:T(4,128)S(1)}, f32[1,64,4]{1,2,0:T(4,128)}, u32[]{:S(2)}) copy-start(f32[1,64,4]{1,2,0:T(4,128)} %param.39) | copy-start | bytes 3076
  550.8 13.6 %copy-start.25 = (f32[1,64,4]{1,2,0:T(4,128)S(1)}, f32[1,64,4]{1,2,0:T(4,128)}, u32[]{:S(2)}) copy-start(f32[1,64,4]{1,2,0:T(4,128)} %param.46) | copy-start | bytes 3076
  550.8 71.1 %copy-start.7 = (f32[64,2,1152]{2,1,0:T(2,128)S(1)}, f32[64,2,1152]{2,1,0:T(2,128)}, u32[]{:S(2)}) copy-start(f32[64,2,1152]{2,1,0:T(2,128)} %param.41) | copy-start | bytes 1769476
  630.7 4.2 copy-start.16
  630.7 4.2 copy-start.17
  630.7 4.2 copy-start.18
  634.9 99.7 %copy-start = (f32[1,64,2,4608]{3,2,1,0:T(2,128)S(1)}, f32[1,64,2,4608]{3,2,1,0:T(2,128)}, u32[]{:S(2)}) copy-start(f32[1,64,2,4608]{3,2,1,0:T(2,128)} %param.31) | copy-start | bytes 7077892
  (16 other events, 46.0 us)
Sparse Core Ops, SparseCore 0:
  10.5 56.4 all-gather.19
  69.3 50.5 all-gather.17
  122.1 21.4 all-gather.27
  145.6 22.4 all-gather.25
  170.1 26.8 all-gather.15
  199.1 33.6 all-gather.23
  234.9 32.8 all-gather.21
  290.4 29.9 reduce-scatter.26
  323.3 30.7 reduce-scatter.22
  357.0 30.8 reduce-scatter.24
  390.9 32.4 reduce-scatter.28
  425.7 35.2 reduce-scatter.18
  463.4 36.5 reduce-scatter.20
  502.8 29.4 reduce-scatter.32
  534.9 28.5 reduce-scatter.30
  567.6 54.2 all-reduce.4
  624.1 54.9 reduce-scatter.14
  681.3 53.2 reduce-scatter.16

commit v2 on v1

v2 whole, which is shorter than its diff:
```python
import functools
import math

import jax
import jax.numpy as jnp
from jax import lax
from jax.experimental import pallas as pl
from jax.experimental.pallas import tpu as pltpu
from jax.sharding import PartitionSpec as P

TEMB = 128
GROUPS = 8
STEP = 5

norm_eps = 1e-05
beta_first = 0.5
beta_second = 0.5
adam_eps = 1e-08
rate_matrix = 0.02
rate_vector = 0.2
decay_matrix = 0.01

CH = 512
BLK = 128
ENC_GROUP = 16
f32 = jnp.float32
bf16 = jnp.bfloat16
VMEM_BYTES = 60 * 1024 * 1024

NT = (((1,), (1,)), ((), ()))
NN = (((1,), (0,)), ((), ()))
TN = (((0,), (0,)), ((), ()))


def dot(a, b, dims=NN):
    return lax.dot_general(a, b, dims, preferred_element_type=f32)


def group_ones(width, group):
    rows = lax.broadcasted_iota(jnp.int32, (width, width), 0) // group
    cols = lax.broadcasted_iota(jnp.int32, (width, width), 1) // group
    return jnp.where(rows == cols, 1.0, 0.0).astype(bf16)


def group_sum(v, ones):
    high = v.astype(bf16)
    rest = v - high.astype(f32)
    middle = rest.astype(bf16)
    low = (rest - middle.astype(f32)).astype(bf16)
    return dot(high, ones) + dot(middle, ones) + dot(low, ones)


def sigmoid(v):
    return 1.0 / (1.0 + jnp.exp(-v))


def mish_pair(v):
    e = jnp.exp(jnp.minimum(v, 20.0))
    n = e * (e + 2.0)
    inv = 1.0 / (n + 2.0)
    t = n * inv
    return v * t, t + v * (4.0 * e * (1.0 + e)) * inv * inv


def mish_value(v):
    e = jnp.exp(jnp.minimum(v, 20.0))
    n = e * (e + 2.0)
    return v * (n / (n + 2.0))


def span(i):
    return range(max(0, 1 - i), min(2, 3 - i) + 1)


MESH = pl.DeviceIdType.MESH


def batch_copy(src, dst, send_sem, recv_sem, target):
    return pltpu.make_async_remote_copy(
        src_ref=src, dst_ref=dst, send_sem=send_sem, recv_sem=recv_sem,
        device_id={"batch": target}, device_id_type=MESH,
    )


def cam_copy(src, dst, send_sem, recv_sem, target):
    return pltpu.make_async_remote_copy(
        src_ref=src, dst_ref=dst, send_sem=send_sem, recv_sem=recv_sem,
        device_id={"cam": target}, device_id_type=MESH,
    )


def line_barrier(cams, nz):
    me, cam = lax.axis_index("batch"), lax.axis_index("cam")
    zi, core = me // 2, me % 2
    barrier = pltpu.get_barrier_semaphore()
    pl.semaphore_signal(barrier, inc=1, device_id={"batch": me + 1 - 2 * core}, device_id_type=MESH)
    for step in range(1, cams):
        pl.semaphore_signal(barrier, inc=1, device_id={"cam": (cam + step) % cams}, device_id_type=MESH)

    @pl.when(zi > 0)
    def _():
        pl.semaphore_signal(barrier, inc=1, device_id={"batch": me - 2}, device_id_type=MESH)

    @pl.when(zi < nz - 1)
    def _():
        pl.semaphore_signal(barrier, inc=1, device_id={"batch": me + 2}, device_id_type=MESH)

    ends = (zi == 0).astype(jnp.int32) + (zi == nz - 1).astype(jnp.int32)
    pl.semaphore_wait(barrier, cams + 2 - ends)


def enc_fwd_kernel(
    n, cams, x_ref, own_ref,
    z1_out, r1_ref, a_out, z2_out, r2_ref, arr_ref, w_out, aff_ref,
    w_ref, z1_ref, a_ref, z2_ref, feat_ref, arr_s,
    zsend, zrecv, csend, crecv, wsem, osem, fsend, frecv,
):
    nz = n // 2
    rows = own_ref.shape[1]
    spb = BLK // rows
    n_img = x_ref.shape[0]
    me, cam = lax.axis_index("batch"), lax.axis_index("cam")
    zi, core = me // 2, me % 2
    partner = me + 1 - 2 * core
    ones = group_ones(BLK, ENC_GROUP)
    inv_n = 1.0 / (9 * ENC_GROUP)

    line_barrier(cams, nz)

    def z_copy(conv, k, way):
        ref = w_ref.at[conv, 2 * k + core]
        return batch_copy(ref, ref, zsend.at[conv, way, k], zrecv.at[conv, k], me - 2 + 4 * way)

    def core_copy(conv, k, which):
        ref = w_ref.at[conv, 2 * k + which]
        return batch_copy(ref, ref, csend.at[conv, k], crecv.at[conv, k], partner)

    def moves(s):
        low, high = zi - s, zi + s
        return (
            (high, high < nz, (high < nz) & (zi > 0), 0),
            (low, low >= 0, (low >= 0) & (zi < nz - 1), 1),
        )

    def send(conv, s):
        for k, _, passed, way in moves(s):
            @pl.when(passed)
            def _():
                z_copy(conv, k, way).start()

    def receive(conv, s):
        for k, held, _, way in moves(s):
            @pl.when(held)
            def _():
                z_copy(conv, k, way).wait_recv()
                core_copy(conv, k, core).start()

    for conv in range(2):
        w_ref[conv, me] = own_ref[conv]
    for conv in range(2):
        core_copy(conv, zi, core).start()

    def rows_of(conv, j, start, wide):
        block = w_ref[conv, pl.ds(j * spb, spb), :, start : start + wide]
        return block.reshape(BLK, wide)

    def w_save(conv, j):
        part = pl.ds(j * spb, spb)
        return pltpu.make_async_copy(w_ref.at[conv, part], w_out.at[conv, part], wsem.at[conv, j])

    def conv_norm(src_ref, conv, z_ref, r_ref, j):
        lanes = pl.ds(pl.multiple_of(j * BLK, BLK), BLK)
        total = None
        for p in range(9):
            r, c = divmod(p, 3)
            bs = span(c)
            acc = None
            for a in span(r):
                start = (3 * (r + a - 1) + c + bs[0] - 1) * CH
                wide = len(bs) * CH
                part = dot(src_ref[:, start : start + wide], rows_of(conv, j, (3 * a + bs[0]) * CH, wide), NT)
                acc = part if acc is None else acc + part
            z_ref[p, :, lanes] = acc
            total = acc if total is None else total + acc
        mean = group_sum(total, ones) * inv_n
        var = None
        for p in range(9):
            centred = z_ref[p, :, lanes] - mean
            sq = centred * centred
            var = sq if var is None else var + sq
        rstd = lax.rsqrt(group_sum(var, ones) * inv_n + norm_eps)
        r_ref[:, lanes] = rstd
        return lanes, mean, rstd

    def first(j):
        aff_ref[:, lanes_of(j)] = jnp.transpose(rows_of(0, j, 9 * CH, BLK).astype(f32))[0:8]
        lanes, mean, rstd = conv_norm(x_ref, 0, z1_ref, r1_ref, j)
        gain, offset = aff_ref[0:1, lanes], aff_ref[1:2, lanes]
        for p in range(9):
            z = (z1_ref[p, :, lanes] - mean) * rstd
            z1_ref[p, :, lanes] = z
            u = z * gain + offset
            a_ref[:, pl.ds(pl.multiple_of(p * CH + j * BLK, BLK), BLK)] = (u * sigmoid(u)).astype(bf16)

    def second(j):
        lanes, mean, rstd = conv_norm(a_ref, 1, z2_ref, r2_ref, j)
        gain, offset = aff_ref[2:3, lanes], aff_ref[3:4, lanes]
        total = None
        for p in range(9):
            z = (z2_ref[p, :, lanes] - mean) * rstd
            z2_ref[p, :, lanes] = z
            pic = x_ref[:, pl.ds(pl.multiple_of(p * CH + j * BLK, BLK), BLK)].astype(f32)
            u = z * gain + offset + pic
            act = u * sigmoid(u)
            total = act if total is None else total + act
        out = (total * (1.0 / 9.0)).astype(bf16)
        feat_ref[:, :, :, lanes] = out.reshape(feat_ref.shape[:3] + (BLK,))

    def lanes_of(j):
        return pl.ds(pl.multiple_of(j * BLK, BLK), BLK)

    def arrived(conv, k):
        core_copy(conv, k, 1 - core).wait_recv()

    def phase(conv, block):
        streaming = spb == 2

        def step(s, carry):
            if conv == 0:
                @pl.when(s < nz - 1)
                def _():
                    send(0, s)

                @pl.when(s == nz - 1)
                def _():
                    send(1, 0)
            else:
                @pl.when((s > 0) & (s < nz - 1))
                def _():
                    send(1, s)

            def side(d, carry):
                k = zi + s - 2 * s * d

                @pl.when((k >= 0) & (k < nz) & (s + 1 > d))
                def _():
                    arrived(conv, k)
                    if streaming:
                        w_save(conv, k).start()
                        block(k)
                return carry

            lax.fori_loop(0, 2, side, 0)

            @pl.when(s < nz - 1)
            def _():
                receive(conv, s + 1)
            return carry

        lax.fori_loop(0, nz, step, 0)
        if not streaming:
            def rest(j, carry):
                w_save(conv, j).start()
                block(j)
                return carry

            lax.fori_loop(0, CH // BLK, rest, 0)

    phase(0, first)
    saves = [pltpu.make_async_copy(z1_ref, z1_out, osem.at[0])]
    saves += [
        pltpu.make_async_copy(a_ref.at[:, p * CH : (p + 1) * CH], a_out.at[p], osem.at[2 + p])
        for p in range(9)
    ]
    for save in saves:
        save.start()
    phase(1, second)
    last = pltpu.make_async_copy(z2_ref, z2_out, osem.at[1])
    last.start()

    def feat_copy(to, sender):
        return cam_copy(feat_ref.at[:, to], arr_s.at[sender], fsend.at[to], frecv.at[sender], to)

    for step in range(1, cams):
        feat_copy((cam + step) % cams, cam).start()
    arr_s[cam] = feat_ref[:, cam]
    for step in range(1, cams):
        other = (cam + step) % cams
        feat_copy(other, other).wait_recv()
    arr_ref[...] = arr_s[...]
    for step in range(1, cams):
        feat_copy((cam + step) % cams, cam).wait_send()

    for conv in range(2):
        def drain(k, carry):
            s = k - zi

            @pl.when((s >= 0) & (s < nz - 1) & (zi > 0))
            def _():
                z_copy(conv, k, 0).wait_send()

            @pl.when((s <= 0) & (s > 1 - nz) & (zi < nz - 1))
            def _():
                z_copy(conv, k, 1).wait_send()

            core_copy(conv, k, core).wait_send()
            return carry

        lax.fori_loop(0, nz, drain, 0)

        def saved(j, carry):
            w_save(conv, j).wait()
            return carry

        lax.fori_loop(0, CH // BLK, saved, 0)
    for save in saves:
        save.wait()
    last.wait()


def enc_bwd_kernel(
    n, cams, x_hbm, a_hbm, w_hbm, z1_hbm, r1_ref, z2_hbm, r2_ref, aff_ref, dviews_ref,
    ig_ref, genc_ref, gaff_ref,
    x_ref, a_ref, w_ref, z1_ref, z2_ref, g_ref, gt_ref, ag_ref, gp_ref,
    dwf, core_out, core_in, slots,
    lsem, csend, crecv, zsend, zrecv, fsend, frecv,
):
    nz = n // 2
    rows = CH // n
    n_img = z1_ref.shape[1]
    me, cam = lax.axis_index("batch"), lax.axis_index("cam")
    zi, core = me // 2, me % 2
    partner = me + 1 - 2 * core
    ones = group_ones(BLK, ENC_GROUP)
    inv_n = 1.0 / (9 * ENC_GROUP)
    chunk = 3 * CH

    def load_w(conv):
        return pltpu.make_async_copy(w_hbm.at[conv, :, :, 0 : 9 * CH], w_ref, lsem.at[3])

    loads = {
        "z2": pltpu.make_async_copy(z2_hbm, z2_ref, lsem.at[0]),
        "z1": pltpu.make_async_copy(z1_hbm, z1_ref, lsem.at[1]),
        "a": pltpu.make_async_copy(a_hbm, a_ref, lsem.at[2]),
    }
    x_loads = [
        pltpu.make_async_copy(x_hbm.at[:, p * CH : (p + 1) * CH], x_ref.at[p], lsem.at[4 + p])
        for p in range(9)
    ]
    loads["z2"].start()
    for load in x_loads:
        load.start()
    loads["a"].start()
    load_w(1).start()
    loads["z1"].start()

    line_barrier(cams, nz)

    def view_copy(to, sender):
        return cam_copy(dviews_ref.at[to], gp_ref.at[:, sender], fsend.at[to], frecv.at[sender], to)

    for step in range(1, cams):
        view_copy((cam + step) % cams, cam).start()
    gp_ref[:, cam] = dviews_ref[cam]
    ag_ref[...] = jnp.zeros_like(ag_ref)
    for step in range(1, cams):
        other = (cam + step) % cams
        view_copy(other, other).wait_recv()
    for load in x_loads:
        load.wait()
    loads["z2"].wait()

    def lanes_of(j):
        return pl.ds(pl.multiple_of(j * BLK, BLK), BLK)

    def norm_back(du_ref, z_ref, r_ref, j, gain, row):
        lanes = lanes_of(j)
        s0 = jnp.zeros((n_img, BLK), f32)
        s1 = jnp.zeros((n_img, BLK), f32)
        for p in range(9):
            du = du_ref[p, :, lanes]
            s0 = s0 + du
            s1 = s1 + du * z_ref[p, :, lanes]
        ag_ref[row : row + 1, lanes] = jnp.sum(s1, axis=0, keepdims=True)
        ag_ref[row + 1 : row + 2, lanes] = jnp.sum(s0, axis=0, keepdims=True)
        m0 = group_sum(s0 * gain, ones) * inv_n
        m1 = group_sum(s1 * gain, ones) * inv_n
        rstd = r_ref[:, lanes]
        for p in range(9):
            dv = (du_ref[p, :, lanes] * gain - m0 - z_ref[p, :, lanes] * m1) * rstd
            g_ref[p, :, lanes] = dv.astype(bf16)
            gt_ref[lanes, p * n_img : (p + 1) * n_img] = jnp.transpose(dv).astype(bf16)

    def second(j, carry):
        lanes = lanes_of(j)
        gain, offset = aff_ref[2:3, lanes], aff_ref[3:4, lanes]
        pooled = gp_ref[:, :, :, lanes].reshape(n_img, BLK).astype(f32) * (1.0 / 9.0)
        for p in range(9):
            u = z2_ref[p, :, lanes] * gain + offset + x_ref[p, :, lanes].astype(f32)
            s = sigmoid(u)
            ig_ref[p, :, lanes] = pooled * (s * (1.0 + u * (1.0 - s)))
        norm_back(ig_ref, z2_ref, r2_ref, j, gain, 2)
        return carry

    def first(j, carry):
        lanes = lanes_of(j)
        gain, offset = aff_ref[0:1, lanes], aff_ref[1:2, lanes]
        for p in range(9):
            u = z1_ref[p, :, lanes] * gain + offset
            s = sigmoid(u)
            z2_ref[p, :, lanes] = z2_ref[p, :, lanes] * (s * (1.0 + u * (1.0 - s)))
        norm_back(z2_ref, z1_ref, r1_ref, j, gain, 0)
        return carry

    def width(k):
        return chunk + BLK if k == 5 else chunk

    def core_copy(k):
        cols = pl.ds(0, width(k))
        return batch_copy(
            core_out.at[k % 2, :, :, cols], core_in.at[k, :, :, cols], csend.at[k], crecv.at[k], partner
        )

    def make_chunk(k):
        src_ref = a_ref if k < 3 else x_ref
        a = k % 3
        r_lo, r_hi = max(0, 1 - a), min(2, 3 - a)
        for b in range(3):
            c_lo, c_hi = max(0, 1 - b), min(2, 3 - b)
            if b == 1:
                runs = [(3 * r_lo, 3 * (r_hi - r_lo + 1))]
            else:
                runs = [(3 * r + c_lo, c_hi - c_lo + 1) for r in range(r_lo, r_hi + 1)]
            shift = 3 * (a - 1) + b - 1
            for half in range(2):
                acc = None
                for p, m in runs:
                    part = dot(
                        gt_ref[half * 256 : half * 256 + 256, p * n_img : (p + m) * n_img],
                        src_ref[p + shift : p + shift + m].reshape(m * n_img, CH),
                    )
                    acc = part if acc is None else acc + part
                dwf[k % 2, half * n // 2 : (half + 1) * n // 2, :, b * CH : (b + 1) * CH] = acc.reshape(
                    n // 2, rows, CH
                )
        if k == 5:
            dwf[1, :, :, chunk:] = jnp.transpose(ag_ref[...]).reshape(n, rows, BLK)
        if k >= 2:
            core_copy(k - 2).wait_send()

        def pack(d, carry):
            core_out[k % 2, d, :, 0 : width(k)] = dwf[k % 2, 2 * d + 1 - core, :, 0 : width(k)].astype(bf16)
            return carry

        lax.fori_loop(0, nz, pack, 0)
        core_copy(k).start()

    def term(k, d):
        return dwf[k % 2, 2 * d + core, :, 0 : width(k)] + core_in[k, d, :, 0 : width(k)].astype(f32)

    def line_copy(k, way, s):
        cols = pl.ds(0, width(k))
        return batch_copy(
            slots.at[k, way, s - 1, :, cols], slots.at[k, way, s, :, cols],
            zsend.at[k, way, s], zrecv.at[k, way, s], me - 2 + 4 * way,
        )

    def serve(k, s):
        for way in range(2):
            ahead = zi if way else nz - 1 - zi
            d = nz - s + zi if way else s - nz + zi
            cols = pl.ds(0, width(k))

            @pl.when((ahead < nz - 1) & (s > ahead))
            def _():
                @pl.when(ahead > 0)
                def _():
                    line_copy(k, way, s - 1).wait_recv()
                    slots[k, way, s - 1, :, cols] = (
                        slots[k, way, s - 1, :, cols].astype(f32) + term(k, d)
                    ).astype(bf16)

                @pl.when(ahead == 0)
                def _():
                    slots[k, way, s - 1, :, cols] = term(k, d).astype(bf16)

                line_copy(k, way, s).start()

    def service(g):
        k, part = divmod(g, 3)
        if part == 0:
            core_copy(k).wait_recv()
        lo, hi = 1 + part * (nz - 1) // 3, 1 + (part + 1) * (nz - 1) // 3
        if hi - lo == 1:
            serve(k, lo)
        elif hi > lo:
            def body(s, carry):
                serve(k, s)
                return carry

            lax.fori_loop(lo, hi, body, 0)

    def finish(k):
        conv, a = 1 - k // 3, k % 3
        total = term(k, zi)
        cols = slice(0, width(k))

        def write(v):
            genc_ref[conv, :, a * chunk : (a + 1) * chunk] = v[:, 0:chunk]
            if k == 5:
                gaff_ref[...] = v[:, chunk:]

        last = nz - 1

        @pl.when(zi > 0)
        def _():
            line_copy(k, 1, last).wait_recv()

        @pl.when(zi < nz - 1)
        def _():
            line_copy(k, 0, last).wait_recv()

        @pl.when(zi == 0)
        def _():
            write(total + slots[k, 0, last, :, cols].astype(f32))

        @pl.when(zi == nz - 1)
        def _():
            write(total + slots[k, 1, last, :, cols].astype(f32))

        @pl.when((zi > 0) & (zi < nz - 1))
        def _():
            write(total + slots[k, 0, last, :, cols].astype(f32) + slots[k, 1, last, :, cols].astype(f32))

    def input_back(q):
        r, c = divmod(q, 3)
        acc = None
        for a in range(3):
            for b in range(3):
                pr, pc = r - a + 1, c - b + 1
                if 0 <= pr < 3 and 0 <= pc < 3:
                    t = 3 * a + b
                    w = w_ref[:, :, t * CH : (t + 1) * CH].reshape(CH, CH)
                    part = dot(g_ref[3 * pr + pc], w)
                    acc = part if acc is None else acc + part
        return acc

    def back_second(*qs):
        for q in qs:
            if q == 0:
                load_w(1).wait()
            z2_ref[q] = input_back(q)
            if q == 8:
                load_w(0).start()

    def back_first(*qs):
        for q in qs:
            if q == 0:
                load_w(0).wait()
            ig_ref[q] = ig_ref[q] + input_back(q)

    lax.fori_loop(0, CH // BLK, second, 0)
    loads["a"].wait()
    make_chunk(0)
    service(0)
    make_chunk(1)
    service(1)
    back_second(0, 1, 2)
    service(2)
    back_second(3, 4)
    service(3)
    finish(0)
    make_chunk(2)
    service(4)
    back_second(5, 6)
    service(5)
    back_second(7, 8)
    service(6)
    finish(1)
    loads["z1"].wait()
    lax.fori_loop(0, 2, first, 0)
    service(7)
    lax.fori_loop(2, 4, first, 0)
    service(8)
    make_chunk(3)
    service(9)
    finish(2)
    make_chunk(4)
    service(10)
    back_first(0, 1)
    service(11)
    back_first(2, 3)
    service(12)
    finish(3)
    make_chunk(5)
    service(13)
    back_first(4, 5)
    service(14)
    back_first(6)
    service(15)
    finish(4)
    back_first(7)
    service(16)
    back_first(8)
    service(17)
    finish(5)

    core_copy(4).wait_send()
    core_copy(5).wait_send()
    for k in range(6):
        def drain(s, carry):
            for way in range(2):
                ahead = zi if way else nz - 1 - zi

                @pl.when((ahead < nz - 1) & (s > ahead))
                def _():
                    line_copy(k, way, s).wait_send()
            return carry

        lax.fori_loop(1, nz, drain, 0)
    for step in range(1, cams):
        view_copy((cam + step) % cams, cam).wait_send()


def temporal_kernel(
    traj_ref, og_ref, arr_ref, mask_ref, emb_ref, t_ref,
    out_ref, tg_ref, dviews_ref, dt_ref,
    pad_t, pad_m, pad_h, za_ref, zb_ref, sum_ref, aff_ref, ag_ref,
):
    cond = (t_ref.shape[1] - 14 * CH - BLK) // 2
    cuts = [0]
    for wide in (5 * CH, 5 * CH, cond, cond, CH, 3 * CH, BLK):
        cuts.append(cuts[-1] + wide)
    wa_ref, wb_ref, f0_ref, f1_ref, ws_ref, wd_ref = [
        t_ref.at[:, cuts[i] : cuts[i + 1]] for i in range(6)
    ]
    dwa_ref, dwb_ref, df0_ref, df1_ref, dws_ref, dwd_ref = [
        dt_ref.at[:, cuts[i] : cuts[i + 1]] for i in range(6)
    ]
    aff_ref[...] = jnp.transpose(t_ref[:, cuts[6] :].astype(f32))
    ag_ref[...] = jnp.zeros_like(ag_ref)
    ns = mask_ref.shape[0]
    rows = traj_ref.shape[0]
    nf = rows // ns
    edge = 2 * ns
    ones = group_ones(CH, CH // GROUPS)
    inv_n = 1.0 / (nf * (CH // GROUPS))
    aff = lambda i: aff_ref[i : i + 1, :]

    def frames(v):
        return v.reshape(nf, ns, CH)

    def fill(pad_ref, v):
        pad_ref[0:edge, :] = jnp.zeros((edge, CH), bf16)
        pad_ref[edge : edge + rows, :] = v
        pad_ref[edge + rows : edge + rows + edge, :] = jnp.zeros((edge, CH), bf16)

    def conv5(pad_ref, w_ref):
        acc = None
        for t in range(5):
            part = dot(pad_ref[t * ns : t * ns + rows, :], w_ref[:, t * CH : (t + 1) * CH], NT)
            acc = part if acc is None else acc + part
        return acc

    def conv5_back(pad_ref, w_ref):
        acc = None
        for t in range(5):
            part = dot(pad_ref[(4 - t) * ns : (4 - t) * ns + rows, :], w_ref[:, t * CH : (t + 1) * CH])
            acc = part if acc is None else acc + part
        return acc

    def norm(v):
        v = frames(v)
        mean = group_sum(jnp.sum(v, axis=0), ones) * inv_n
        centred = v - mean[None]
        rstd = lax.rsqrt(group_sum(jnp.sum(centred * centred, axis=0), ones) * inv_n + norm_eps)
        return centred * rstd[None], rstd

    def norm_back(du, z, rstd, gain):
        s0 = jnp.sum(du, axis=0)
        s1 = jnp.sum(du * z, axis=0)
        m0 = group_sum(s0 * gain, ones) * inv_n
        m1 = group_sum(s1 * gain, ones) * inv_n
        dv = (du * gain[None] - m0[None] - z * m1[None]) * rstd[None]
        return dv, jnp.sum(s1, axis=0, keepdims=True), jnp.sum(s0, axis=0, keepdims=True)

    mask = mask_ref[...]
    count = jnp.sum(mask, axis=1, keepdims=True)
    cams = arr_ref.shape[0]
    obs = arr_ref.shape[1]
    conds, slopes = [], []
    for o in range(obs):
        pooled = None
        for cam in range(cams):
            part = mask[:, cam : cam + 1] * arr_ref[cam, o].astype(f32)
            pooled = part if pooled is None else pooled + part
        value, slope = mish_pair(pooled / count)
        conds.append(value.astype(bf16))
        slopes.append(slope)
    conds.append(mish_value(emb_ref[...]).astype(bf16))
    lanes = [slice(o * CH, (o + 1) * CH) for o in range(obs)] + [slice(obs * CH, cond)]
    film = []
    for i, w_ref in ((6, f0_ref), (7, f1_ref)):
        film.append(sum(dot(v, w_ref[:, cols], NT) for v, cols in zip(conds, lanes)) + aff(i))
    scale, shift = film

    fill(pad_t, traj_ref[...])
    za, rstd_a = norm(conv5(pad_t, wa_ref) + aff(4))
    za_ref[...] = za.reshape(rows, CH)
    act_a = mish_value(za * aff(0)[None] + aff(1)[None])
    fill(pad_m, (act_a * scale[None] + shift[None]).astype(bf16).reshape(rows, CH))
    zb, rstd_b = norm(conv5(pad_m, wb_ref) + aff(5))
    zb_ref[...] = zb.reshape(rows, CH)
    skip = frames(dot(traj_ref[...], ws_ref[...], NT)) + aff(8)[None]
    summed = (mish_value(zb * aff(2)[None] + aff(3)[None]) + skip).astype(bf16)
    pairs = summed.reshape(nf // 2, 2, ns, CH)
    half = rows // 2
    sum_ref[0:ns, :] = jnp.zeros((ns, CH), bf16)
    sum_ref[ns : ns + half, :] = pairs[:, 1].reshape(half, CH)
    sum_ref[ns + half : ns + 2 * half, :] = pairs[:, 0].reshape(half, CH)
    taps = (0, ns + half, ns)
    out = None
    og = og_ref[...]
    dcols = []
    for t in range(3):
        cols = sum_ref[taps[t] : taps[t] + half, :]
        w = wd_ref[:, t * CH : (t + 1) * CH]
        part = dot(cols, w, NT)
        out = part if out is None else out + part
        dcols.append(dot(og, w).reshape(nf // 2, ns, CH))
        dwd_ref[:, t * CH : (t + 1) * CH] = dot(og, cols, TN).astype(bf16)
    out_ref[...] = (out + aff(9)).astype(bf16)
    ag_ref[9:10, :] = jnp.sum(og.astype(f32), axis=0, keepdims=True)

    before = jnp.concatenate([dcols[0][1:], jnp.zeros((1, ns, CH), f32)], axis=0)
    dsum = jnp.stack([dcols[1], dcols[2] + before], axis=1).reshape(nf, ns, CH)
    ag_ref[8:9, :] = jnp.sum(dsum, axis=(0, 1)).reshape(1, CH)
    dskip = dsum.astype(bf16).reshape(rows, CH)
    dws_ref[...] = dot(dskip, traj_ref[...], TN).astype(bf16)
    tg_ref[...] = dot(dskip, ws_ref[...])
    zb = frames(zb_ref[...])
    _, slope = mish_pair(zb * aff(2)[None] + aff(3)[None])
    dhb, ag_ref[2:3, :], ag_ref[3:4, :] = norm_back(dsum * slope, zb, rstd_b, aff(2))
    ag_ref[5:6, :] = jnp.sum(dhb, axis=(0, 1)).reshape(1, CH)
    fill(pad_h, dhb.astype(bf16).reshape(rows, CH))
    hb = pad_h[edge : edge + rows, :]
    for t in range(5):
        dwb_ref[:, t * CH : (t + 1) * CH] = dot(hb, pad_m[t * ns : t * ns + rows, :], TN).astype(bf16)
    dmid = frames(conv5_back(pad_h, wb_ref))
    za = frames(za_ref[...])
    act_a, slope = mish_pair(za * aff(0)[None] + aff(1)[None])
    dscale = jnp.sum(dmid * act_a, axis=0)
    dshift = jnp.sum(dmid, axis=0)
    dha, ag_ref[0:1, :], ag_ref[1:2, :] = norm_back(dmid * scale[None] * slope, za, rstd_a, aff(0))
    ag_ref[4:5, :] = jnp.sum(dha, axis=(0, 1)).reshape(1, CH)
    ag_ref[6:7, :] = jnp.sum(dscale, axis=0, keepdims=True)
    ag_ref[7:8, :] = jnp.sum(dshift, axis=0, keepdims=True)
    fill(pad_h, dha.astype(bf16).reshape(rows, CH))
    ha = pad_h[edge : edge + rows, :]
    for t in range(5):
        dwa_ref[:, t * CH : (t + 1) * CH] = dot(ha, pad_t[t * ns : t * ns + rows, :], TN).astype(bf16)
    tg_ref[...] = tg_ref[...] + conv5_back(pad_h, wa_ref)

    lows = (dscale.astype(bf16), dshift.astype(bf16))
    for low, dw_ref in zip(lows, (df0_ref, df1_ref)):
        for v, cols in zip(conds, lanes):
            dw_ref[:, cols] = dot(low, v, TN).astype(bf16)
    for o in range(obs):
        dcond = dot(lows[0], f0_ref[:, lanes[o]]) + dot(lows[1], f1_ref[:, lanes[o]])
        dview = dcond * slopes[o] / count
        for cam in range(cams):
            dviews_ref[cam, o] = (mask[:, cam : cam + 1] * dview).astype(bf16)
    dt_ref[:, cuts[6] :] = jnp.transpose(ag_ref[...]).astype(bf16)


def call(kernel, outs, in_specs, out_specs, scratch=(), collective_id=None, cost=None):
    extra = {} if collective_id is None else dict(collective_id=collective_id, has_side_effects=True)
    return pl.pallas_call(
        kernel,
        out_shape=[jax.ShapeDtypeStruct(s, d) for s, d in outs],
        in_specs=in_specs,
        out_specs=out_specs,
        scratch_shapes=list(scratch),
        compiler_params=pltpu.CompilerParams(vmem_limit_bytes=VMEM_BYTES, **extra),
        cost_estimate=cost,
    )


def work(microseconds):
    return pl.CostEstimate(
        flops=int(microseconds * 1e9), bytes_accessed=int(microseconds * 3e6), transcendentals=0
    )


V = pl.BlockSpec(memory_space=pltpu.VMEM)
H = pl.BlockSpec(memory_space=pl.ANY)
DMA = pltpu.SemaphoreType.DMA


def time_embed(steps_given, embed_width):
    half_width = embed_width // 2
    frequency = jnp.exp(
        jnp.arange(half_width, dtype=jnp.float32) * (-math.log(10000.0) / (half_width - 1))
    )
    argument = steps_given.astype(jnp.float32)[:, None] * frequency[None, :]
    return jnp.concatenate([jnp.sin(argument), jnp.cos(argument)], axis=1)


def adamw(weight, gradient, moment_one, moment_two, step_rate, weight_decay):
    mean_new = beta_first * moment_one + (1.0 - beta_first) * gradient
    square_new = beta_second * moment_two + (1.0 - beta_second) * gradient * gradient
    mean_hat = mean_new / (1.0 - beta_first**STEP)
    square_hat = square_new / (1.0 - beta_second**STEP)
    weight_new = weight - step_rate * (
        mean_hat / (jnp.sqrt(square_hat) + adam_eps) + weight_decay * weight
    )
    return (weight_new, mean_new, square_new)


def shards(
    n, images, trajectory, view_mask, timesteps, out_grad,
    encoder_weight, encoder_affine, block_convs, film_weight, skip_weight, down_weight, block_affine,
    first_encoder, first_affine, first_convs, first_film, first_skip, first_down, first_block,
    second_encoder, second_affine, second_convs, second_film, second_skip, second_down, second_block,
):
    ns, nf, ch = trajectory.shape
    cams, obs = images.shape[1], images.shape[3]
    n_img = cams * images.shape[2] * obs
    nz, per = n // 2, ch // n
    cond = film_weight.shape[2]
    wide = 9 * ch
    rows = nf * ns

    own_t = jnp.concatenate(
        [block_convs[:, 0], block_convs[:, 1], film_weight[:, 0], film_weight[:, 1], skip_weight, down_weight,
         jnp.pad(block_affine, ((0, 0), (0, BLK - block_affine.shape[1])))],
        axis=1,
    ).astype(bf16)
    part = per // cams
    own_part = lax.dynamic_slice_in_dim(own_t, lax.axis_index("cam") * part, part, 0)
    line_t = lax.all_gather(own_part, "batch", axis=0)
    all_t = lax.all_gather(line_t, "cam", axis=1).reshape(ch, own_t.shape[1])

    own_w = jnp.concatenate(
        [jnp.transpose(encoder_weight[0], (1, 0, 2)),
         jnp.broadcast_to(jnp.pad(encoder_affine[0], ((0, 0), (0, BLK - 4)))[None], (2, per, BLK))],
        axis=2,
    ).astype(bf16)
    x = jnp.transpose(images[0], (2, 0, 1, 3, 4)).reshape(n_img, wide)
    pos = (9, n_img, ch)
    z1, r1, act, z2, r2, arrived, w_all, enc_aff = call(
        functools.partial(enc_fwd_kernel, n, cams),
        [(pos, f32), ((n_img, ch), f32), (pos, bf16), (pos, f32), ((n_img, ch), f32),
         ((cams, obs, ns, ch), bf16), ((2, n, per, wide + BLK), bf16), ((8, ch), f32)],
        [V, V],
        [H, V, H, H, V, V, H, V],
        [pltpu.VMEM((2, n, per, wide + BLK), bf16), pltpu.VMEM(pos, f32), pltpu.VMEM((n_img, wide), bf16),
         pltpu.VMEM(pos, f32), pltpu.VMEM((obs, cams, ns, ch), bf16), pltpu.VMEM((cams, obs, ns, ch), bf16),
         DMA((2, 2, nz)), DMA((2, nz)), DMA((2, nz)), DMA((2, nz)), DMA((2, ch // BLK)), DMA((11,)),
         DMA((cams,)), DMA((cams,))],
        collective_id=0,
        cost=work(90),
    )(x, own_w)

    present = view_mask.astype(f32)
    embedded = time_embed(timesteps, TEMB)
    traj_fm = jnp.transpose(trajectory, (1, 0, 2)).reshape(rows, ch)
    og_fm = jnp.transpose(out_grad, (1, 0, 2)).reshape(rows // 2, ch)
    out_fm, tg_fm, dviews, dt = call(
        temporal_kernel,
        [((rows // 2, ch), bf16), ((rows, ch), f32), ((cams, obs, ns, ch), bf16), (all_t.shape, bf16)],
        [V] * 6,
        [V] * 4,
        [pltpu.VMEM((rows + 4 * ns, ch), bf16)] * 3
        + [pltpu.VMEM((rows, ch), f32)] * 2
        + [pltpu.VMEM((rows + ns, ch), bf16)]
        + [pltpu.VMEM((BLK, ch), f32)] * 2,
        cost=work(20),
    )(traj_fm, og_fm, arrived, present, embedded, all_t)
    block_output = jnp.transpose(out_fm.reshape(nf // 2, ns, ch), (1, 0, 2))
    trajectory_grad = jnp.transpose(tg_fm.reshape(nf, ns, ch), (1, 0, 2))

    cut = lax.psum_scatter(dt.reshape(n, cams, part, -1), "cam", scatter_dimension=1, tiled=False)
    cut = lax.psum_scatter(cut, "batch", scatter_dimension=0, tiled=False)
    gt = lax.all_gather(cut, "cam", axis=0, tiled=True).astype(f32)

    chunk = 3 * ch + BLK
    ig, genc, gaff = call(
        functools.partial(enc_bwd_kernel, n, cams),
        [(pos, f32), ((2, per, wide), f32), ((per, BLK), f32)],
        [H, H, H, H, V, H, V, V, V],
        [V, V, V],
        [pltpu.VMEM(pos, bf16), pltpu.VMEM(pos, bf16), pltpu.VMEM((n, per, wide), bf16), pltpu.VMEM(pos, f32),
         pltpu.VMEM(pos, f32), pltpu.VMEM(pos, bf16), pltpu.VMEM((ch, 9 * n_img), bf16),
         pltpu.VMEM((BLK, ch), f32), pltpu.VMEM((obs, cams, ns, ch), bf16),
         pltpu.VMEM((2, n, per, chunk), f32), pltpu.VMEM((2, nz, per, chunk), bf16),
         pltpu.VMEM((6, nz, per, chunk), bf16), pltpu.VMEM((6, 2, nz, per, chunk), bf16),
         DMA((13,)), DMA((6,)), DMA((6,)), DMA((6, 2, nz)), DMA((6, 2, nz)), DMA((cams,)), DMA((cams,))],
        collective_id=1,
        cost=work(100),
    )(x, act, w_all, z1, r1, z2, r2, enc_aff, dviews)
    images_grad = jnp.transpose(ig.reshape((9, obs) + images.shape[1:3] + (ch,)), (2, 3, 1, 0, 4))[None]

    cuts = [0]
    for size in (5 * ch, 5 * ch, cond, cond, ch, 3 * ch):
        cuts.append(cuts[-1] + size)
    pieces = [gt[:, cuts[i] : cuts[i + 1]] for i in range(6)]
    convs_share = jnp.stack(pieces[0:2], axis=1)
    film_share = jnp.stack(pieces[2:4], axis=1)
    encoder_share = jnp.transpose(genc, (1, 0, 2))[None]
    upd = (
        adamw(encoder_weight, encoder_share, first_encoder, second_encoder, rate_matrix, decay_matrix),
        adamw(encoder_affine, gaff[None, :, :4], first_affine, second_affine, rate_vector, 0.0),
        adamw(block_convs, convs_share, first_convs, second_convs, rate_matrix, decay_matrix),
        adamw(film_weight, film_share, first_film, second_film, rate_matrix, decay_matrix),
        adamw(skip_weight, pieces[4], first_skip, second_skip, rate_matrix, decay_matrix),
        adamw(down_weight, pieces[5], first_down, second_down, rate_matrix, decay_matrix),
        adamw(block_affine, gt[:, cuts[6] : cuts[6] + 10], first_block, second_block, rate_vector, 0.0),
    )
    return (
        (block_output, trajectory_grad, images_grad)
        + tuple(u[0] for u in upd)
        + tuple(u[1] for u in upd)
        + tuple(u[2] for u in upd)
    )


def solution(mesh):
    sample = P(("cam", "batch"))
    params = (P("cam", "batch"), P("cam", "batch")) + (P("batch"),) * 5
    images_spec = P("cam", None, "batch")
    return jax.shard_map(
        functools.partial(shards, mesh.shape["batch"]),
        mesh=mesh,
        in_specs=(images_spec, sample, sample, sample, sample) + params * 3,
        out_specs=(sample, sample, images_spec) + params * 3,
        check_vma=False,
    )
```

time: 766 us -> 511 us (0.67)
  waiting for transfers between devices: 476 us -> 108 us
  Pallas kernels: 120 us -> 248 us
  blocking collectives: 59.1 us -> 0 us
  local copies, waits for them, and re-layouts: 63.9 us -> 105 us
  other arithmetic: 13.1 us -> 26.1 us
  starting transfers between devices: 7.95 us -> 0.2 us
    reduce_scatter x8 -> x1, waiting for transfers between devices: 240 us -> 0.02 us  [shards(): cut = lax.psum_scatter(cut, 'batch', scatter_dimension=0, tiled=False)]
    pallas_call x2, Pallas kernels: 98.5 us -> 223 us  [the longest x1 126 us: shards(): call(functools.partial(enc_bwd_kernel, n, cams), [(pos, f32), ((2, per, w...]
    all_gather x7 -> x3, waiting for transfers between devices: 139 us -> 35.3 us  [the longest x1 35.3 us: shards(): line_t = lax.all_gather(own_part, 'batch', axis=0)]
    psum x1 -> x0, waiting for transfers between devices: 56.9 us -> none  [total(): return scatter(lax.psum(v, 'cam')).astype(f32)]
    all_gather x3 -> x0, blocking collectives: 49.1 us -> none  [gather(): return lax.all_gather(v.astype(bf16), 'batch', axis=0, tiled=True)]
    unnamed x20 -> x6, waiting for transfers between devices: 35.6 us -> 72.9 us
    unnamed x76 -> x112, local copies, waits for them, and re-layouts: 43.5 us -> 73.1 us
    psum x1 -> x0, blocking collectives: 10 us -> none  [shards(): block_share = scatter(lax.psum(jnp.transpose(blk_grad[:10]), 'cam'))]
  transfers between devices with their start and end apart: 20 -> 5, of which waited for: 15 -> 2; matrix products, arithmetic and copies ran while one was open for 8% -> 14% of each run, Pallas kernels for 13% -> 45%
where the time goes in v2:
time: 511 us; the launch traced here: 501 us
  Pallas kernels  248 us (49%)
  waiting for transfers between devices  108 us (21%)
  local copies, waits for them, and re-layouts  105 us (21%)
  other arithmetic  26.1 us (5%)
  between operations  14.4 us (3%)
    pallas_call x1, Pallas kernels, shards(): call(functools.partial(enc_bwd_kernel, n, cams), [(pos, f32), ((2, per, w...  126 us
    pallas_call x1, Pallas kernels, shards(): call(functools.partial(enc_fwd_kernel, n, cams), [(pos, f32), ((n_img, ch...  97.3 us
    unnamed x112, local copies, waits for them, and re-layouts  73.1 us
    unnamed x6, waiting for transfers between devices  72.9 us
    all_gather x1, waiting for transfers between devices, shards(): line_t = lax.all_gather(own_part, 'batch', axis=0)  35.3 us
    pallas_call x1, Pallas kernels, shards(): call(temporal_kernel, [((rows // 2, ch), bf16), ((rows, ch), f32), ((cams...  24.3 us
    sub x7, other arithmetic, adamw(): weight - step_rate * (mean_hat / (jnp.sqrt(square_hat) + adam_eps) + weig...  19.5 us
  transfers between devices with their start and end apart: 5, of which 2 were waited for; matrix products, arithmetic and copies ran while one was open for 14% of the time, Pallas kernels for 45%

profile of v2, /device:TPU:0, one launch (start us, length us, event | category | flops | bytes accessed | tf_op | source)
XLA Modules:
  0.0 501.4 jit_solution(7988402868115825199)
XLA Ops:
  14.0 35.3 %all-gather.7.cloned.1.call-done = bf16[128,9600]{1,0:T(8,128)(2,1)} async-done(((bf16[16,9600]{1,0:T(8,128)(2,1)}), bf16[128,9600]{1,0:T(8,128)(2,1)}) %all-gather.7.cloned.1.call-update) | async-done | bytes 2457616 | tf_op jit(solution)/shard_map/all_gather | solution.py:841
  50.2 3.9 copy.284
  61.2 97.3 %shard_map.433 = (f32[9,256,512]{2,1,0:T(8,128)}, f32[256,512]{1,0:T(8,128)}, bf16[9,256,512]{2,1,0:T(8,128)(2,1)}, f32[9,256,512]{2,1,0:T(8,128)}, f32[256,512]...) custom-call(bf16[256,4608]{1,0:T(8,128)(2,1)} %bitcast.97, ...), custom_call_target="tpu_custom_call" | custom-call | flops 89999998976 | bytes 270000000 | tf_op jit(solution)/shard_map/pallas_call | solution.py:851
  158.5 24.3 %shard_map.434 = (bf16[256,512]{1,0:T(8,128)(2,1)}, f32[512,512]{1,0:T(8,128)}, bf16[4,2,32,512]{3,2,1,0:T(8,128)(2,1)}, bf16[512,9600]{1,0:T(8,128)(2,1)}) custom-call(bf16[512,512]{1,0:T(8,128)(2,1)} %bitcast.102, bf16[256,512]{1,0:T(8,128)(2,1)} %bitcast.107, bf16[4,2,32,512]{3,2,1,0:T(8,128)(2,1)} %get-tuple-element.39.arr_ref, f32[32,4]{1,0:T(8,128)} %copy.233.mask_ref, ...), custom_call_target="tpu_custom_call" | custom-call | flops 20000000000 | bytes 60000000 | tf_op jit(solution)/shard_map/pallas_call | solution.py:869
  182.8 8.3 %copy.248 = bf16[8,4,16,9600]{3,2,0,1:T(8,128)(2,1)} copy(bf16[8,4,16,9600]{3,2,1,0:T(8,128)(2,1)} %bitcast.88) | data formatting | bytes 19660800 | tf_op jit(solution)/shard_map/reshape | solution.py:883
  193.5 2.9 copy.252
  200.0 2.4 copy.253
  202.4 2.3 copy.254
  204.6 3.8 copy.247
  208.5 4.0 copy.250
  212.4 2.1 copy.261
  214.6 2.2 copy.262
  217.6 1.7 copy.258
  219.3 72.8 %reduce-scatter.7.cloned.1.call-done = bf16[8,1,16,9600]{3,2,0,1:T(8,128)(2,1)} async-done(((bf16[8,4,16,9600]{3,2,0,1:T(8,128)(2,1)}), bf16[8,1,16,9600]{3,2,0,1:T(8,128)(2,1)}) %reduce-scatter.7.cloned.1.call-update) | async-done | bytes 2457616
  292.2 126.0 %shard_map.435 = (f32[9,256,512]{2,1,0:T(8,128)}, f32[2,64,4608]{2,1,0:T(8,128)}, f32[64,128]{1,0:T(8,128)}) custom-call(bf16[256,4608]{1,0:T(8,128)(2,1)} %bitcast.98, bf16[9,256,512]{2,1,0:T(8,128)(2,1)} %get-tuple-element.42.a_hbm, bf16[2,8,64,4736]{3,2,1,0:T(8,128)(2,1)} %get-tuple-element.43.w_hbm, f32[9,256,512]{2,1,0:T(8,128)} %get-tuple-element.44.z1_hbm, ...), custom_call_target="tpu_custom_call" | custom-call | flops 99999997952 | bytes 300000000 | tf_op jit(solution)/shard_map/pallas_call | solution.py:888
  424.2 6.2 %multiply_subtract_fusion.1 = (f32[1,64,2,4608]{3,1,2,0:T(8,128)S(1)}, f32[1,64,2,4608]{3,1,2,0:T(8,128)S(1)}, f32[1,64,2,4608]{3,1,2,0:T(8,128)S(1)}) fusion(f32[1,64,2,4608]{3,2,1,0:T(2,128)} %param.31, f32[2,64,4608]{2,1,0:T(8,128)} %get-tuple-element.51, f32[1,64,2,4608]{3,2,1,0:T(2,128)} %param.38, f32[1,64,2,4608]{3,2,1,0:T(2,128)} %param.45), kind=kLoop, calls=%fused_computation.14 | loop fusion | flops 8257536 | bytes 16515072 | tf_op jit(solution)/shard_map/sub | solution.py:814
  430.4 3.2 copy.265
  433.6 3.2 copy.271
  436.8 3.2 copy.277
  440.1 6.0 %copy.304 = f32[9,2,4,32,512]{4,1,0,3,2:T(2,128)} copy(f32[9,2,4,32,512]{4,3,2,1,0:T(8,128)S(1)} %bitcast.93) | data formatting | bytes 9437184 | tf_op jit(solution)/shard_map/reshape | solution.py:902
  448.5 3.8 copy.249
  452.3 1.8 bitcast_convert_fusion
  455.9 2.0 copy-done
  458.8 2.5 multiply_subtract_fusion.2
  461.3 2.2 copy.268
  463.5 2.2 copy.274
  465.7 2.2 copy.280
  468.0 6.2 %multiply_subtract_fusion = (f32[64,2,2560]{0,2,1:T(8,128)}, f32[64,2,2560]{0,2,1:T(8,128)}, f32[64,2,2560]{0,2,1:T(8,128)}) fusion(f32[64,2,2560]{0,2,1:T(8,128)S(1)} %copy.252, f32[64,1,2560]{0,2,1:T(8,128)} %get-tuple-element.175, f32[64,1,2560]{0,2,1:T(8,128)} %get-tuple-element.174, f32[64,2,2560]{0,2,1:T(8,128)} %copy.247, f32[64,2,2560]{0,2,1:T(8,128)} %copy.250), kind=kLoop, calls=%fused_computation.7 | loop fusion | flops 4915200 | bytes 9175040 | tf_op jit(solution)/shard_map/sub | solution.py:814
  474.2 4.0 copy.267
  478.2 4.1 copy.273
  482.3 2.4 copy.279
  484.7 2.2 multiply_subtract_fusion.3
  (140 shorter events, 40.4 us)
Async XLA Ops:
  7.2 42.0 %all-gather.7.cloned.1.call-start = ((), (), s32[]{:S(2)}) async-start(), calls=%async_computation.3 | async-start | bytes 2764800 | tf_op jit(solution)/shard_map/all_gather | solution.py:841
  7.3 3.6 copy-start.9
  9.0 40.3 %copy-start.6 = (bf16[1,4,32,2,9,512]{5,3,4,2,1,0:T(2,128)(2,1)S(1)}, bf16[1,4,32,2,9,512]{5,3,4,2,1,0:T(2,128)(2,1)}, u32[]{:S(2)}) copy-start(bf16[1,4,32,2,9,512]{5,3,4,2,1,0:T(2,128)(2,1)} %param.26) | copy-start | bytes 7077892
  13.9 144.6 %all-gather.9.cloned.1.call-start = ((), (), s32[]{:S(2)}) async-start(), calls=%async_computation.4 | async-start | bytes 12288000 | tf_op jit(solution)/shard_map/all_gather | solution.py:842
  49.2 242.9 %reduce-scatter.7.cloned.1.call-start = ((), (), s32[]{:S(2)}) async-start(), calls=%async_computation.6 | async-start | bytes 12288000
  50.2 3.9 copy-start.28
  50.2 4.6 copy-start.2
  191.1 227.1 %reduce-scatter.5.cloned.1.call-start = ((), (), s32[]{:S(2)}) async-start(), calls=%async_computation.2 | async-start | bytes 2764800 | tf_op jit(solution)/shard_map/reduce_scatter | solution.py:884
  193.5 4.2 copy-start.15
  193.5 5.0 copy-start.31
  193.5 5.7 %copy-start.32 = (f32[1,64,4]{1,2,0:T(4,128)S(1)}, f32[1,64,4]{1,2,0:T(4,128)}, u32[]{:S(2)}) copy-start(f32[1,64,4]{1,2,0:T(4,128)} %param.46) | copy-start | bytes 3076
  208.5 8.3 %copy-start.21 = (f32[64,512]{1,0:T(8,128)S(1)}, f32[64,512]{1,0:T(8,128)}, u32[]{:S(2)}) copy-start(f32[64,512]{1,0:T(8,128)} %param.42) | copy-start | bytes 393220
  292.1 156.4 %all-gather.11.cloned.1.call-start = ((), (), s32[]{:S(2)}) async-start(), calls=%async_computation.5 | async-start | bytes 1536000 | tf_op jit(solution)/shard_map/all_gather | solution.py:885
  292.2 126.1 %copy-start.22 = (f32[1,64,4]{2,1,0:T(8,128)S(1)}, f32[1,64,4]{2,1,0:T(8,128)}, u32[]{:S(2)}) copy-start(f32[1,64,4]{2,1,0:T(8,128)} %copy.241) | copy-start | bytes 3076
  292.2 126.1 %copy-start.23 = (f32[1,64,4]{2,1,0:T(8,128)S(1)}, f32[1,64,4]{2,1,0:T(8,128)}, u32[]{:S(2)}) copy-start(f32[1,64,4]{2,1,0:T(8,128)} %copy.242) | copy-start | bytes 3076
  292.2 129.2 %copy-start.29 = (f32[1,64,4]{1,2,0:T(4,128)S(1)}, f32[1,64,4]{1,2,0:T(4,128)}, u32[]{:S(2)}) copy-start(f32[1,64,4]{1,2,0:T(4,128)} %param.32) | copy-start | bytes 3076
  292.2 129.3 %copy-start.18 = (f32[1,64,4]{2,1,0:T(8,128)S(1)}, f32[1,64,4]{2,1,0:T(8,128)}, u32[]{:S(2)}) copy-start(f32[1,64,4]{2,1,0:T(8,128)} %copy.229) | copy-start | bytes 3076
  430.4 9.7 %slice-start = ((s8[4718592]{0:T(1024)(128)(4,1)}), s8[524288]{0:T(1024)(128)(4,1)S(1)}, s32[]{:S(2)}) async-start(s8[4718592]{0:T(1024)(128)(4,1)} %bitcast.91), calls=%async_computation.7 | async-start | bytes 1048576
  433.6 6.5 %slice-start.1 = ((s8[4718592]{0:T(1024)(128)(4,1)}), s8[4194304]{0:T(1024)(128)(4,1)S(1)}, s32[]{:S(2)}) async-start(s8[4718592]{0:T(1024)(128)(4,1)} %bitcast.91), calls=%async_computation.8 | async-start | bytes 8388608
  440.1 6.0 %copy-start.13 = (f32[512,512]{1,0:T(8,128)S(1)}, f32[512,512]{1,0:T(8,128)}, u32[]{:S(2)}) copy-start(f32[512,512]{1,0:T(8,128)} %get-tuple-element.41) | copy-start | bytes 3145732
  440.1 7.6 %copy-start.20 = (bf16[256,512]{1,0:T(8,128)(2,1)S(1)}, bf16[256,512]{1,0:T(8,128)(2,1)}, u32[]{:S(2)}) copy-start(bf16[256,512]{1,0:T(8,128)(2,1)} %get-tuple-element.40) | copy-start | bytes 786436
  454.1 3.7 copy-start
  454.2 3.6 copy-start.3
  454.3 3.6 copy-start.4
  454.3 4.5 copy-start.5
  478.2 4.1 copy-start.1
  486.9 3.0 copy-start.10
  486.9 3.0 copy-start.11
  486.9 3.0 copy-start.12
  488.9 4.5 copy-start.25
  488.9 4.5 copy-start.26
  488.9 4.5 copy-start.27
  (9 other events, 16.8 us)
Sparse Core Ops, SparseCore 0:
  14.0 35.1 all-gather.6
  51.1 98.6 all-gather.8
  191.2 100.8 reduce-scatter.6
  294.3 49.6 reduce-scatter.4
  418.4 28.5 all-gather.10

commit v3 on v2

--- a/solution.py
+++ b/solution.py
@@ -319,11 +319,12 @@
 
 
 def enc_bwd_kernel(
-    n, cams, x_hbm, a_hbm, w_hbm, z1_hbm, r1_ref, z2_hbm, r2_ref, aff_ref, dviews_ref,
-    ig_ref, genc_ref, gaff_ref,
+    n, cams, cond, x_hbm, a_hbm, w_hbm, z1_hbm, r1_ref, z2_hbm, r2_ref, aff_ref, dviews_ref, dt_hbm,
+    ig_ref, genc_ref, gaff_ref, gconvs_ref, gfilm_ref, gskip_ref, gdown_ref, gblk_ref,
     x_ref, a_ref, w_ref, z1_ref, z2_ref, g_ref, gt_ref, ag_ref, gp_ref,
-    dwf, core_out, core_in, slots,
+    dwf, core_out, core_in, slots, t_own, t_sum, t_peer, t_slots, t_all,
     lsem, csend, crecv, zsend, zrecv, fsend, frecv,
+    tlsem, tcsend, tcrecv, tpsend, tprecv, tzsend, tzrecv, tfsend, tfrecv,
 ):
     nz = n // 2
     rows = CH // n
@@ -354,6 +355,11 @@
     load_w(1).start()
     loads["z1"].start()
 
+    def own_load(i):
+        return pltpu.make_async_copy(dt_hbm.at[i // cams, core, i % cams], t_own.at[i % 2], tlsem.at[i])
+
+    own_load(0).start()
+
     line_barrier(cams, nz)
 
     def view_copy(to, sender):
@@ -361,6 +367,42 @@
 
     for step in range(1, cams):
         view_copy((cam + step) % cams, cam).start()
+
+    def t_core(k):
+        return batch_copy(dt_hbm.at[k, 1 - core], t_sum.at[k], tcsend.at[k], tcrecv.at[k], partner)
+
+    def t_peers(k, step):
+        to = (cam + step) % cams
+        return cam_copy(t_sum.at[k, to], t_peer.at[step - 1, k], tpsend.at[step - 1, k], tprecv.at[step - 1, k], to)
+
+    def t_start(k, carry):
+        t_core(k).start()
+        return carry
+
+    lax.fori_loop(0, nz, t_start, 0)
+
+    def t_spread(lo, hi):
+        def body(k, carry):
+            t_core(k).wait_recv()
+
+            def quarter(q, carry):
+                i = k * cams + q
+
+                @pl.when(i + 1 < nz * cams)
+                def _():
+                    own_load(i + 1).start()
+
+                own_load(i).wait()
+                t_sum[k, q] = (t_sum[k, q].astype(f32) + t_own[i % 2].astype(f32)).astype(bf16)
+                return carry
+
+            lax.fori_loop(0, cams, quarter, 0)
+            for step in range(1, cams):
+                t_peers(k, step).start()
+            return carry
+
+        lax.fori_loop(lo, hi, body, 0)
+
     gp_ref[:, cam] = dviews_ref[cam]
     ag_ref[...] = jnp.zeros_like(ag_ref)
     for step in range(1, cams):
@@ -418,10 +460,19 @@
     def core_copy(k):
         cols = pl.ds(0, width(k))
         return batch_copy(
-            core_out.at[k % 2, :, :, cols], core_in.at[k, :, :, cols], csend.at[k], crecv.at[k], partner
+            core_out.at[k % 2, :, :, cols], core_in.at[k % 3, :, :, cols], csend.at[k], crecv.at[k], partner
         )
 
+    def keep(k, d0, lane, v):
+        count, wide = v.shape[0] // (2 * rows), v.shape[1]
+        parts = v.reshape(count, 2, rows, wide)
+        even, odd = parts[:, 0], parts[:, 1]
+        dwf[k % 2, d0 : d0 + count, :, lane : lane + wide] = jnp.where(core == 0, even, odd)
+        core_out[k % 2, d0 : d0 + count, :, lane : lane + wide] = jnp.where(core == 0, odd, even).astype(bf16)
+
     def make_chunk(k):
+        if k >= 2:
+            core_copy(k - 2).wait_send()
         src_ref = a_ref if k < 3 else x_ref
         a = k % 3
         r_lo, r_hi = max(0, 1 - a), min(2, 3 - a)
@@ -440,56 +491,56 @@
                         src_ref[p + shift : p + shift + m].reshape(m * n_img, CH),
                     )
                     acc = part if acc is None else acc + part
-                dwf[k % 2, half * n // 2 : (half + 1) * n // 2, :, b * CH : (b + 1) * CH] = acc.reshape(
-                    n // 2, rows, CH
-                )
+                keep(k, half * nz // 2, b * CH, acc)
         if k == 5:
-            dwf[1, :, :, chunk:] = jnp.transpose(ag_ref[...]).reshape(n, rows, BLK)
-        if k >= 2:
-            core_copy(k - 2).wait_send()
-
-        def pack(d, carry):
-            core_out[k % 2, d, :, 0 : width(k)] = dwf[k % 2, 2 * d + 1 - core, :, 0 : width(k)].astype(bf16)
-            return carry
-
-        lax.fori_loop(0, nz, pack, 0)
+            keep(k, 0, chunk, jnp.transpose(ag_ref[...]))
         core_copy(k).start()
 
     def term(k, d):
-        return dwf[k % 2, 2 * d + core, :, 0 : width(k)] + core_in[k, d, :, 0 : width(k)].astype(f32)
+        return dwf[k % 2, d, :, 0 : width(k)] + core_in[k % 3, d, :, 0 : width(k)].astype(f32)
 
     def line_copy(k, way, s):
+        if k == 6:
+            return batch_copy(
+                t_slots.at[way, s - 1], t_slots.at[way, s], tzsend.at[way, s], tzrecv.at[way, s], me - 2 + 4 * way
+            )
         cols = pl.ds(0, width(k))
         return batch_copy(
-            slots.at[k, way, s - 1, :, cols], slots.at[k, way, s, :, cols],
+            slots.at[k % 3, way, s - 1, :, cols], slots.at[k % 3, way, s, :, cols],
             zsend.at[k, way, s], zrecv.at[k, way, s], me - 2 + 4 * way,
         )
+
+    def slot(k, way, s):
+        return t_slots.at[way, s] if k == 6 else slots.at[k % 3, way, s, :, pl.ds(0, width(k))]
+
+    def t_term(d):
+        total = t_sum[d, cam].astype(f32)
+        for step in range(1, cams):
+            total = total + t_peer[step - 1, d].astype(f32)
+        return total
 
     def serve(k, s):
         for way in range(2):
             ahead = zi if way else nz - 1 - zi
             d = nz - s + zi if way else s - nz + zi
-            cols = pl.ds(0, width(k))
+            ref = slot(k, way, s - 1)
 
             @pl.when((ahead < nz - 1) & (s > ahead))
             def _():
+                own = t_term(d) if k == 6 else term(k, d)
+
                 @pl.when(ahead > 0)
                 def _():
                     line_copy(k, way, s - 1).wait_recv()
-                    slots[k, way, s - 1, :, cols] = (
-                        slots[k, way, s - 1, :, cols].astype(f32) + term(k, d)
-                    ).astype(bf16)
+                    ref[...] = (ref[...].astype(f32) + own).astype(bf16)
 
                 @pl.when(ahead == 0)
                 def _():
-                    slots[k, way, s - 1, :, cols] = term(k, d).astype(bf16)
+                    ref[...] = own.astype(bf16)
 
                 line_copy(k, way, s).start()
 
-    def service(g):
-        k, part = divmod(g, 3)
-        if part == 0:
-            core_copy(k).wait_recv()
+    def steps(k, part):
         lo, hi = 1 + part * (nz - 1) // 3, 1 + (part + 1) * (nz - 1) // 3
         if hi - lo == 1:
             serve(k, lo)
@@ -500,16 +551,13 @@
 
             lax.fori_loop(lo, hi, body, 0)
 
-    def finish(k):
-        conv, a = 1 - k // 3, k % 3
-        total = term(k, zi)
-        cols = slice(0, width(k))
-
-        def write(v):
-            genc_ref[conv, :, a * chunk : (a + 1) * chunk] = v[:, 0:chunk]
-            if k == 5:
-                gaff_ref[...] = v[:, chunk:]
-
+    def service(g):
+        k, part = divmod(g, 3)
+        if part == 0:
+            core_copy(k).wait_recv()
+        steps(k, part)
+
+    def collect(k, total, write):
         last = nz - 1
 
         @pl.when(zi > 0)
@@ -522,15 +570,71 @@
 
         @pl.when(zi == 0)
         def _():
-            write(total + slots[k, 0, last, :, cols].astype(f32))
+            write(total + slot(k, 0, last)[...].astype(f32))
 
         @pl.when(zi == nz - 1)
         def _():
-            write(total + slots[k, 1, last, :, cols].astype(f32))
+            write(total + slot(k, 1, last)[...].astype(f32))
 
         @pl.when((zi > 0) & (zi < nz - 1))
         def _():
-            write(total + slots[k, 0, last, :, cols].astype(f32) + slots[k, 1, last, :, cols].astype(f32))
+            write(total + slot(k, 0, last)[...].astype(f32) + slot(k, 1, last)[...].astype(f32))
+
+        def drain(s, carry):
+            for way in range(2):
+                ahead = zi if way else nz - 1 - zi
+
+                @pl.when((ahead < nz - 1) & (s > ahead))
+                def _():
+                    line_copy(k, way, s).wait_send()
+            return carry
+
+        lax.fori_loop(1, nz, drain, 0)
+
+    def finish(k):
+        def write(v):
+            genc_ref[:, 1 - k // 3, (k % 3) * chunk : (k % 3 + 1) * chunk] = v[:, 0:chunk]
+            if k == 5:
+                gaff_ref[...] = jnp.transpose(v[:, chunk:])[0 : gaff_ref.shape[0]]
+
+        collect(k, term(k, zi), write)
+
+    def t_arrived():
+        for step in range(1, cams):
+            def body(k, carry):
+                t_peers(k, step).wait_recv()
+                return carry
+
+            lax.fori_loop(0, nz, body, 0)
+
+    def t_final(to, sender):
+        return cam_copy(t_all.at[cam], t_all.at[sender], tfsend.at[to], tfrecv.at[sender], to)
+
+    def t_finish():
+        def write(v):
+            t_all[cam] = v.astype(bf16)
+
+        collect(6, t_term(zi), write)
+        for step in range(1, cams):
+            t_final((cam + step) % cams, cam).start()
+
+    def t_write():
+        for step in range(1, cams):
+            other = (cam + step) % cams
+            t_final(other, other).wait_recv()
+
+        def cut(lo, wide):
+            return t_all[:, :, lo : lo + wide].reshape(rows, wide).astype(f32)
+
+        at = 0
+        for ref, wide in ((gconvs_ref, 5 * CH), (gfilm_ref, cond)):
+            for which in range(2):
+                ref[:, which, :] = cut(at, wide)
+                at += wide
+        for ref, wide in ((gskip_ref, CH), (gdown_ref, 3 * CH)):
+            ref[...] = cut(at, wide)
+            at += wide
+        gblk_ref[...] = jnp.transpose(cut(at, BLK))[0 : gblk_ref.shape[0]]
 
     def input_back(q):
         r, c = divmod(q, 3)
@@ -563,8 +667,10 @@
     loads["a"].wait()
     make_chunk(0)
     service(0)
+    t_spread(0, nz // 2)
     make_chunk(1)
     service(1)
+    t_spread(nz // 2, nz)
     back_second(0, 1, 2)
     service(2)
     back_second(3, 4)
@@ -596,28 +702,32 @@
     service(13)
     back_first(4, 5)
     service(14)
+    t_arrived()
+    steps(6, 0)
+    finish(4)
     back_first(6)
+    steps(6, 1)
+    back_first(7)
+    steps(6, 2)
+    back_first(8)
     service(15)
-    finish(4)
-    back_first(7)
+    t_finish()
     service(16)
-    back_first(8)
     service(17)
+    t_write()
     finish(5)
 
+    def t_drain(k, carry):
+        t_core(k).wait_send()
+        for step in range(1, cams):
+            t_peers(k, step).wait_send()
+        return carry
+
+    lax.fori_loop(0, nz, t_drain, 0)
+    for step in range(1, cams):
+        t_final((cam + step) % cams, cam).wait_send()
     core_copy(4).wait_send()
     core_copy(5).wait_send()
-    for k in range(6):
-        def drain(s, carry):
-            for way in range(2):
-                ahead = zi if way else nz - 1 - zi
-
-                @pl.when((ahead < nz - 1) & (s > ahead))
-                def _():
-                    line_copy(k, way, s).wait_send()
-            return carry
-
-        lax.fori_loop(1, nz, drain, 0)
     for step in range(1, cams):
         view_copy((cam + step) % cams, cam).wait_send()
 
@@ -817,6 +927,47 @@
     return (weight_new, mean_new, square_new)
 
 
+def adam_kernel(*refs):
+    for i in range(7):
+        w_ref, m_ref, v_ref, g_ref = refs[4 * i : 4 * i + 4]
+        outs = refs[28 + 3 * i : 31 + 3 * i]
+
+        def update():
+            vector = i in (1, 6)
+            rate, decay = (rate_vector, 0.0) if vector else (rate_matrix, decay_matrix)
+            new = adamw(w_ref[...], g_ref[...], m_ref[...], v_ref[...], rate, decay)
+            for ref, value in zip(outs, new):
+                ref[...] = value
+
+        if i in (1, 6):
+            pl.when(pl.program_id(0) == 0)(update)
+        else:
+            update()
+
+
+def adam_call(shown, grads, rows):
+    step = min(rows, 8)
+
+    def spec(v):
+        if v.shape[0] != rows:
+            return pl.BlockSpec(v.shape, lambda r: (0, 0))
+        return pl.BlockSpec((step,) + v.shape[1:], lambda r: (r,) + (0,) * (v.ndim - 1))
+
+    ins = []
+    for i in range(7):
+        ins += [shown[0][i], shown[1][i], shown[2][i], grads[i]]
+    outs = [w for w in shown[0] for _ in range(3)]
+    return pl.pallas_call(
+        adam_kernel,
+        grid=(rows // step,),
+        out_shape=[jax.ShapeDtypeStruct(v.shape, f32) for v in outs],
+        in_specs=[spec(v) for v in ins],
+        out_specs=[spec(v) for v in outs],
+        compiler_params=pltpu.CompilerParams(vmem_limit_bytes=VMEM_BYTES),
+        cost_estimate=work(12),
+    )(*ins)
+
+
 def shards(
     n, images, trajectory, view_mask, timesteps, out_grad,
     encoder_weight, encoder_affine, block_convs, film_weight, skip_weight, down_weight, block_affine,
@@ -880,43 +1031,45 @@
     block_output = jnp.transpose(out_fm.reshape(nf // 2, ns, ch), (1, 0, 2))
     trajectory_grad = jnp.transpose(tg_fm.reshape(nf, ns, ch), (1, 0, 2))
 
-    cut = lax.psum_scatter(dt.reshape(n, cams, part, -1), "cam", scatter_dimension=1, tiled=False)
-    cut = lax.psum_scatter(cut, "batch", scatter_dimension=0, tiled=False)
-    gt = lax.all_gather(cut, "cam", axis=0, tiled=True).astype(f32)
-
     chunk = 3 * ch + BLK
-    ig, genc, gaff = call(
-        functools.partial(enc_bwd_kernel, n, cams),
-        [(pos, f32), ((2, per, wide), f32), ((per, BLK), f32)],
-        [H, H, H, H, V, H, V, V, V],
-        [V, V, V],
+    t_wide = all_t.shape[1]
+    ig, genc, gaff, gconvs, gfilm, gskip, gdown, gblk = call(
+        functools.partial(enc_bwd_kernel, n, cams, cond),
+        [(pos, f32), ((per, 2, wide), f32), ((4, per), f32), ((per, 2, 5 * ch), f32),
+         ((per, 2, cond), f32), ((per, ch), f32), ((per, 3 * ch), f32), ((10, per), f32)],
+        [H, H, H, H, V, H, V, V, V, H],
+        [V] * 8,
         [pltpu.VMEM(pos, bf16), pltpu.VMEM(pos, bf16), pltpu.VMEM((n, per, wide), bf16), pltpu.VMEM(pos, f32),
          pltpu.VMEM(pos, f32), pltpu.VMEM(pos, bf16), pltpu.VMEM((ch, 9 * n_img), bf16),
          pltpu.VMEM((BLK, ch), f32), pltpu.VMEM((obs, cams, ns, ch), bf16),
-         pltpu.VMEM((2, n, per, chunk), f32), pltpu.VMEM((2, nz, per, chunk), bf16),
-         pltpu.VMEM((6, nz, per, chunk), bf16), pltpu.VMEM((6, 2, nz, per, chunk), bf16),
-         DMA((13,)), DMA((6,)), DMA((6,)), DMA((6, 2, nz)), DMA((6, 2, nz)), DMA((cams,)), DMA((cams,))],
+         pltpu.VMEM((2, nz, per, chunk), f32), pltpu.VMEM((2, nz, per, chunk), bf16),
+         pltpu.VMEM((3, nz, per, chunk), bf16), pltpu.VMEM((3, 2, nz, per, chunk), bf16),
+         pltpu.VMEM((2, part, t_wide), bf16), pltpu.VMEM((nz, cams, part, t_wide), bf16),
+         pltpu.VMEM((cams - 1, nz, part, t_wide), bf16), pltpu.VMEM((2, nz, part, t_wide), bf16),
+         pltpu.VMEM((cams, part, t_wide), bf16),
+         DMA((13,)), DMA((6,)), DMA((6,)), DMA((6, 2, nz)), DMA((6, 2, nz)), DMA((cams,)), DMA((cams,)),
+         DMA((nz * cams,)), DMA((nz,)), DMA((nz,)), DMA((cams - 1, nz)), DMA((cams - 1, nz)),
+         DMA((2, nz)), DMA((2, nz)), DMA((cams,)), DMA((cams,))],
         collective_id=1,
         cost=work(100),
-    )(x, act, w_all, z1, r1, z2, r2, enc_aff, dviews)
+    )(x, act, w_all, z1, r1, z2, r2, enc_aff, dviews, dt.reshape(nz, 2, cams, part, t_wide))
     images_grad = jnp.transpose(ig.reshape((9, obs) + images.shape[1:3] + (ch,)), (2, 3, 1, 0, 4))[None]
 
-    cuts = [0]
-    for size in (5 * ch, 5 * ch, cond, cond, ch, 3 * ch):
-        cuts.append(cuts[-1] + size)
-    pieces = [gt[:, cuts[i] : cuts[i + 1]] for i in range(6)]
-    convs_share = jnp.stack(pieces[0:2], axis=1)
-    film_share = jnp.stack(pieces[2:4], axis=1)
-    encoder_share = jnp.transpose(genc, (1, 0, 2))[None]
-    upd = (
-        adamw(encoder_weight, encoder_share, first_encoder, second_encoder, rate_matrix, decay_matrix),
-        adamw(encoder_affine, gaff[None, :, :4], first_affine, second_affine, rate_vector, 0.0),
-        adamw(block_convs, convs_share, first_convs, second_convs, rate_matrix, decay_matrix),
-        adamw(film_weight, film_share, first_film, second_film, rate_matrix, decay_matrix),
-        adamw(skip_weight, pieces[4], first_skip, second_skip, rate_matrix, decay_matrix),
-        adamw(down_weight, pieces[5], first_down, second_down, rate_matrix, decay_matrix),
-        adamw(block_affine, gt[:, cuts[6] : cuts[6] + 10], first_block, second_block, rate_vector, 0.0),
-    )
+    def turned(v):
+        return jnp.transpose(v.reshape(v.shape[-2:]))
+
+    weights = (encoder_weight, encoder_affine, block_convs, film_weight, skip_weight, down_weight, block_affine)
+    firsts = (first_encoder, first_affine, first_convs, first_film, first_skip, first_down, first_block)
+    seconds = (second_encoder, second_affine, second_convs, second_film, second_skip, second_down, second_block)
+    shown = [
+        [turned(v) if i in (1, 6) else v.reshape(v.shape[-3:]) if i == 0 else v for i, v in enumerate(group)]
+        for group in (weights, firsts, seconds)
+    ]
+    news = adam_call(shown, (genc, gaff, gconvs, gfilm, gskip, gdown, gblk), per)
+    upd = [
+        tuple((turned(v) if i in (1, 6) else v).reshape(w.shape) for v in news[3 * i : 3 * i + 3])
+        for i, w in enumerate(weights)
+    ]
     return (
         (block_output, trajectory_grad, images_grad)
         + tuple(u[0] for u in upd)

time: 511 us -> 360 us (0.70)
  local copies, waits for them, and re-layouts: 105 us -> 24.8 us
  waiting for transfers between devices: 108 us -> 35.3 us
  Pallas kernels: 248 us -> 276 us
  other arithmetic: 26.1 us -> 3.49 us
    unnamed x6 -> x2, waiting for transfers between devices: 72.9 us -> 0.03 us
    unnamed x112 -> x30, local copies, waits for them, and re-layouts: 73.1 us -> 8.58 us
    pallas_call x1 -> x2, Pallas kernels: 126 us -> 154 us  [the longest x1 140 us: shards(): call(functools.partial(enc_bwd_kernel, n, cams, cond), [(pos, f32), ((per...]
    sub x7 -> x0, other arithmetic: 19.5 us -> none  [adamw(): weight - step_rate * (mean_hat / (jnp.sqrt(square_hat) + adam_eps) + weig...]
    reshape x1 -> x0, local copies, waits for them, and re-layouts: 8.25 us -> none  [shards(): dt.reshape(n, cams, part, -1)]
  transfers between devices with their start and end apart: 5 -> 2, of which waited for: 2 -> 1; matrix products, arithmetic and copies ran while one was open for 14% -> 3% of each run, Pallas kernels for 45% -> 28%
where the time goes in v3:
time: 360 us; the launch traced here: 354 us
  Pallas kernels  276 us (77%)
  waiting for transfers between devices  35.3 us (10%)
  local copies, waits for them, and re-layouts  24.8 us (7%)
  between operations  14.5 us (4%)
    pallas_call x1, Pallas kernels, shards(): call(functools.partial(enc_bwd_kernel, n, cams, cond), [(pos, f32), ((per...  140 us
    pallas_call x1, Pallas kernels, shards(): call(functools.partial(enc_fwd_kernel, n, cams), [(pos, f32), ((n_img, ch...  97.7 us
    all_gather x1, waiting for transfers between devices, shards(): line_t = lax.all_gather(own_part, 'batch', axis=0)  35.3 us
    pallas_call x1, Pallas kernels, shards(): call(temporal_kernel, [((rows // 2, ch), bf16), ((rows, ch), f32), ((cams...  24.1 us
    pallas_call x1, Pallas kernels, adam_call(): pl.pallas_call(adam_kernel, grid=(rows // step,), out_shape=[jax.ShapeDty...  14.5 us
    unnamed x30, local copies, waits for them, and re-layouts  8.58 us
    reshape x1, local copies, waits for them, and re-layouts, shards(): ig.reshape((9, obs) + images.shape[1:3] + (ch,))  8.26 us
  transfers between devices with their start and end apart: 2, of which 1 were waited for; matrix products, arithmetic and copies ran while one was open for 3% of the time, Pallas kernels for 28%

profile of v3, /device:TPU:0, one launch (start us, length us, event | category | flops | bytes accessed | tf_op | source)
XLA Modules:
  0.0 354.1 jit_solution(13911305962338849058)
XLA Ops:
  7.2 0.0 all-gather.5.cloned.1.call-start
  7.2 0.7 convert.41
  7.9 0.1 copy.85
  8.1 1.1 copy.93
  9.2 1.5 copy.92
  10.8 0.8 copy-done.7
  11.6 0.2 copy-done.4
  11.8 0.7 constant_dynamic-slice_fusion
  12.6 0.0 all-gather.5.cloned.1.call-update
  12.6 0.0 all-gather.7.cloned.1.call-start
  12.6 35.3 %all-gather.5.cloned.1.call-done = bf16[128,9600]{1,0:T(8,128)(2,1)} async-done(((bf16[16,9600]{1,0:T(8,128)(2,1)}), bf16[128,9600]{1,0:T(8,128)(2,1)}) %all-gather.5.cloned.1.call-update) | async-done | bytes 2457616 | tf_op jit(solution)/shard_map/all_gather | solution.py:992
  47.9 0.0 all-gather.7.cloned.1.call-update
  48.0 0.7 copy.81.mask_ref
  48.7 0.1 copy.76
  48.8 0.8 copy.74
  49.6 1.1 copy.73
  50.7 0.8 convert_bitcast_fusion
  51.5 1.1 pad_maximum_fusion
  52.6 1.1 copy.77.own_ref
  53.8 0.9 copy-done
  54.7 0.9 copy.75
  55.6 3.8 %copy.86 = bf16[32,8,9,512]{3,1,2,0:T(8,128)(2,1)} copy(bf16[32,8,9,512]{3,2,1,0:T(8,128)(2,1)S(1)} %bitcast.76) | data formatting | bytes 4718592
  59.5 0.1 multiply_sine_fusion
  59.6 0.7 pad_maximum_fusion.1.emb_ref
  60.3 97.7 %shard_map.433 = (f32[9,256,512]{2,1,0:T(8,128)}, f32[256,512]{1,0:T(8,128)}, bf16[9,256,512]{2,1,0:T(8,128)(2,1)}, f32[9,256,512]{2,1,0:T(8,128)}, f32[256,512]...) custom-call(bf16[256,4608]{1,0:T(8,128)(2,1)} %bitcast.81, ...), custom_call_target="tpu_custom_call" | custom-call | flops 89999998976 | bytes 270000000 | tf_op jit(solution)/shard_map/pallas_call | solution.py:1002
  158.0 0.0 all-gather.7.cloned.1.call-done
  158.0 24.1 %shard_map.434 = (bf16[256,512]{1,0:T(8,128)(2,1)}, f32[512,512]{1,0:T(8,128)}, bf16[4,2,32,512]{3,2,1,0:T(8,128)(2,1)}, bf16[512,9600]{1,0:T(8,128)(2,1)}) custom-call(bf16[512,512]{1,0:T(8,128)(2,1)} %bitcast.87, bf16[256,512]{1,0:T(8,128)(2,1)} %bitcast.90, bf16[4,2,32,512]{3,2,1,0:T(8,128)(2,1)} %get-tuple-element.65.arr_ref, f32[32,4]{1,0:T(8,128)} %copy.81.mask_ref, ...), custom_call_target="tpu_custom_call" | custom-call | flops 20000000000 | bytes 60000000 | tf_op jit(solution)/shard_map/pallas_call | solution.py:1020
  182.1 139.7 %shard_map.435 = (f32[9,256,512]{2,1,0:T(8,128)}, f32[64,2,4608]{2,1,0:T(2,128)}, f32[4,64]{1,0:T(4,128)}, f32[64,2,2560]{2,1,0:T(2,128)}, f32[64,2,1152]{2,1,0:...) custom-call(bf16[256,4608]{1,0:T(8,128)(2,1)} %bitcast.82, ...), custom_call_target="tpu_custom_call" | custom-call | flops 99999997952 | bytes 300000000 | tf_op jit(solution)/shard_map/pallas_call | solution.py:1036
  321.9 8.3 %copy.94 = f32[9,2,4,32,512]{4,1,0,3,2:T(2,128)} copy(f32[9,2,4,32,512]{4,3,2,1,0:T(8,128)} %bitcast.78) | data formatting | bytes 9437184 | tf_op jit(solution)/shard_map/reshape | solution.py:1056
  330.2 0.9 copy.96
  331.0 1.6 copy.95
  332.6 14.5 %shard_map.436 = (f32[64,2,4608]{2,1,0:T(2,128)}, f32[64,2,4608]{2,1,0:T(2,128)}, f32[64,2,4608]{2,1,0:T(2,128)}, f32[4,64]{1,0:T(4,128)}, f32[4,64]{1,0:T(4,128...) custom-call(f32[64,2,4608]{2,1,0:T(2,128)} %bitcast.83, ...), custom_call_target="tpu_custom_call" | custom-call | flops 12000000000 | bytes 36000000 | tf_op jit(solution)/shard_map/pallas_call | solution.py:960
  (31 shorter events, 0.2 us)
Async XLA Ops:
  7.2 40.7 %all-gather.5.cloned.1.call-start = ((), (), s32[]{:S(2)}) async-start(), calls=%async_computation | async-start | bytes 2764800 | tf_op jit(solution)/shard_map/all_gather | solution.py:992
  10.7 0.9 copy-start.7
  10.7 1.1 copy-start.4
  12.5 35.4 %copy-start.10 = (s32[32]{0:T(128)S(1)}, s32[32]{0:T(128)}, u32[]{:S(2)}) copy-start(s32[32]{0:T(128)} %param.29) | copy-start | bytes 388
  12.6 35.4 %copy-start.9 = (s32[32,4]{0,1:T(4,128)S(1)}, s32[32,4]{0,1:T(4,128)}, u32[]{:S(2)}) copy-start(s32[32,4]{0,1:T(4,128)} %param.28) | copy-start | bytes 1540
  12.6 36.2 %copy-start.5 = (bf16[32,8,512]{2,1,0:T(8,128)(2,1)S(1)}, bf16[32,8,512]{2,1,0:T(8,128)(2,1)}, u32[]{:S(2)}) copy-start(bf16[32,8,512]{2,1,0:T(8,128)(2,1)} %param.30) | copy-start | bytes 786436
  12.6 36.1 %copy-start.8 = (f32[1,64,4]{1,2,0:T(4,128)S(1)}, f32[1,64,4]{1,2,0:T(4,128)}, u32[]{:S(2)}) copy-start(f32[1,64,4]{1,2,0:T(4,128)} %param.32) | copy-start | bytes 3076
  12.6 145.4 %all-gather.7.cloned.1.call-start = ((), (), s32[]{:S(2)}) async-start(), calls=%async_computation.1 | async-start | bytes 12288000 | tf_op jit(solution)/shard_map/all_gather | solution.py:993
  47.9 1.7 copy-start.3
  47.9 2.8 copy-start.1
  52.6 2.1 copy-start
  321.9 8.3 %copy-start.6 = (bf16[256,512]{1,0:T(8,128)(2,1)S(1)}, bf16[256,512]{1,0:T(8,128)(2,1)}, u32[]{:S(2)}) copy-start(bf16[256,512]{1,0:T(8,128)(2,1)} %get-tuple-element.66) | copy-start | bytes 786436
  321.9 9.1 %copy-start.2 = (f32[512,512]{1,0:T(8,128)S(1)}, f32[512,512]{1,0:T(8,128)}, u32[]{:S(2)}) copy-start(f32[512,512]{1,0:T(8,128)} %get-tuple-element.67) | copy-start | bytes 3145732
Sparse Core Ops, SparseCore 0:
  12.7 35.1 all-gather.4
  49.7 98.6 all-gather.6

commit v4 on v3

--- a/solution.py
+++ b/solution.py
@@ -25,7 +25,7 @@
 ENC_GROUP = 16
 f32 = jnp.float32
 bf16 = jnp.bfloat16
-VMEM_BYTES = 60 * 1024 * 1024
+VMEM_BYTES = 61 * 1024 * 1024
 
 NT = (((1,), (1,)), ((), ()))
 NN = (((1,), (0,)), ((), ()))
@@ -109,14 +109,31 @@
     pl.semaphore_wait(barrier, cams + 2 - ends)
 
 
+PART = 5 * CH
+
+
+def pack_temporal(ref, convs_ref, film_ref, skip_ref, down_ref, ext_ref):
+    rows, cond = film_ref.shape[0], film_ref.shape[2]
+    for q in range(2):
+        ref[q] = convs_ref[:, q, :].astype(bf16)
+        ref[2, :, q * cond : (q + 1) * cond] = film_ref[:, q, :].astype(bf16)
+    ref[2, :, 2 * cond : 2 * cond + BLK] = ext_ref[...]
+    ref[2, :, 2 * cond + BLK :] = jnp.zeros((rows, PART - 2 * cond - BLK), bf16)
+    ref[3, :, 0:CH] = skip_ref[...].astype(bf16)
+    ref[3, :, CH : 4 * CH] = down_ref[...].astype(bf16)
+    ref[3, :, 4 * CH :] = jnp.zeros((rows, PART - 4 * CH), bf16)
+
+
 def enc_fwd_kernel(
-    n, cams, x_ref, own_ref,
-    z1_out, r1_ref, a_out, z2_out, r2_ref, arr_ref, w_out, aff_ref,
-    w_ref, z1_ref, a_ref, z2_ref, feat_ref, arr_s,
+    n, cams, x_ref, enc_hbm, convs_ref, film_ref, skip_ref, down_ref, ext_ref,
+    z1_out, r1_ref, a_out, z2_out, r2_ref, arr_ref, w_out, aff_ref, t_out,
+    w_ref, z1_ref, a_ref, z2_ref, feat_ref, arr_s, t_ref, enc_buf,
     zsend, zrecv, csend, crecv, wsem, osem, fsend, frecv,
+    tzsend, tzrecv, tcsend, tcrecv, tpsend, tprecv, tsem, esem,
 ):
     nz = n // 2
-    rows = own_ref.shape[1]
+    rows = ext_ref.shape[0]
+    piece = enc_buf.shape[1]
     spb = BLK // rows
     n_img = x_ref.shape[0]
     me, cam = lax.axis_index("batch"), lax.axis_index("cam")
@@ -125,7 +142,61 @@
     ones = group_ones(BLK, ENC_GROUP)
     inv_n = 1.0 / (9 * ENC_GROUP)
 
+    def enc_load(i):
+        return pltpu.make_async_copy(enc_hbm.at[pl.ds(i * piece, piece)], enc_buf.at[i % 2], esem.at[i])
+
+    enc_load(0).start()
+    pack_temporal(t_ref.at[zi, core], convs_ref, film_ref, skip_ref, down_ref, ext_ref)
+
     line_barrier(cams, nz)
+
+    def tz_copy(k, way):
+        ref = t_ref.at[k, core, cam]
+        return batch_copy(ref, ref, tzsend.at[way, k], tzrecv.at[k], me - 2 + 4 * way)
+
+    def tc_copy(k, which, q):
+        ref = t_ref.at[k, which, q]
+        return batch_copy(ref, ref, tcsend.at[k, q], tcrecv.at[k, q], partner)
+
+    def tp_copy(k, step, q):
+        ref = t_ref.at[k, core, q]
+        return cam_copy(ref, ref, tpsend.at[step - 1, k], tprecv.at[step - 1, k], (cam + step) % cams)
+
+    def t_send(s):
+        for k, _, passed, way in moves(s):
+            @pl.when(passed)
+            def _():
+                tz_copy(k, way).start()
+
+    def t_receive(s):
+        for k, held, _, way in moves(s):
+            @pl.when(held)
+            def _():
+                tz_copy(k, way).wait_recv()
+                for step in range(1, cams):
+                    tp_copy(k, step, cam).start()
+                tc_copy(k, core, cam).start()
+
+    def t_collect(d):
+        for k, held, _, _ in moves(d):
+            @pl.when(held & (d > 0))
+            def _():
+                for step in range(1, cams):
+                    q = (cam + cams - step) % cams
+                    tp_copy(k, step, q).wait_recv()
+                    tc_copy(k, core, q).start()
+
+    def t_save():
+        return pltpu.make_async_copy(t_ref, t_out, tsem)
+
+    def t_complete():
+        def body(k, carry):
+            for q in range(cams):
+                tc_copy(k, 1 - core, q).wait_recv()
+            return carry
+
+        lax.fori_loop(0, nz, body, 0)
+        t_save().start()
 
     def z_copy(conv, k, way):
         ref = w_ref.at[conv, 2 * k + core]
@@ -155,10 +226,42 @@
                 z_copy(conv, k, way).wait_recv()
                 core_copy(conv, k, core).start()
 
+    t_send(0)
+    for q in range(cams):
+        tc_copy(zi, core, q).start()
     for conv in range(2):
-        w_ref[conv, me] = own_ref[conv]
+        w_ref[conv, me, :, 9 * CH :] = ext_ref[...]
+    count = rows // piece
+
+    def pack(i, carry):
+        @pl.when(i + 1 < count)
+        def _():
+            enc_load(i + 1).start()
+
+        enc_load(i).wait()
+        for conv in range(2):
+            w_ref[conv, me, pl.ds(pl.multiple_of(i * piece, piece), piece), 0 : 9 * CH] = (
+                enc_buf[i % 2, :, conv, :].astype(bf16)
+            )
+        return carry
+
+    lax.fori_loop(0, count, pack, 0)
     for conv in range(2):
         core_copy(conv, zi, core).start()
+
+    def t_step(s, carry):
+        @pl.when(s == nz - 1)
+        def _():
+            send(0, 0)
+
+        t_receive(s)
+
+        @pl.when(s < nz - 1)
+        def _():
+            t_send(s)
+        return carry
+
+    lax.fori_loop(1, nz, t_step, 0)
 
     def rows_of(conv, j, start, wide):
         block = w_ref[conv, pl.ds(j * spb, spb), :, start : start + wide]
@@ -227,7 +330,7 @@
 
         def step(s, carry):
             if conv == 0:
-                @pl.when(s < nz - 1)
+                @pl.when((s > 0) & (s < nz - 1))
                 def _():
                     send(0, s)
 
@@ -251,6 +354,10 @@
                 return carry
 
             lax.fori_loop(0, 2, side, 0)
+            if conv == 1:
+                t_collect(2 * s)
+                t_collect(2 * s + 1)
+                pl.when(s == nz - 2)(t_complete)
 
             @pl.when(s < nz - 1)
             def _():
@@ -316,6 +423,29 @@
     for save in saves:
         save.wait()
     last.wait()
+
+    def t_drain(k, carry):
+        s = k - zi
+
+        @pl.when((s >= 0) & (s < nz - 1) & (zi > 0))
+        def _():
+            tz_copy(k, 0).wait_send()
+
+        @pl.when((s <= 0) & (s > 1 - nz) & (zi < nz - 1))
+        def _():
+            tz_copy(k, 1).wait_send()
+
+        @pl.when(s != 0)
+        def _():
+            for step in range(1, cams):
+                tp_copy(k, step, cam).wait_send()
+
+        for q in range(cams):
+            tc_copy(k, core, q).wait_send()
+        return carry
+
+    lax.fori_loop(0, nz, t_drain, 0)
+    t_save().wait()
 
 
 def enc_bwd_kernel(
@@ -623,18 +753,15 @@
             other = (cam + step) % cams
             t_final(other, other).wait_recv()
 
-        def cut(lo, wide):
-            return t_all[:, :, lo : lo + wide].reshape(rows, wide).astype(f32)
-
-        at = 0
-        for ref, wide in ((gconvs_ref, 5 * CH), (gfilm_ref, cond)):
-            for which in range(2):
-                ref[:, which, :] = cut(at, wide)
-                at += wide
-        for ref, wide in ((gskip_ref, CH), (gdown_ref, 3 * CH)):
-            ref[...] = cut(at, wide)
-            at += wide
-        gblk_ref[...] = jnp.transpose(cut(at, BLK))[0 : gblk_ref.shape[0]]
+        def cut(q, lo, wide):
+            return t_all[q, :, lo : lo + wide].astype(f32)
+
+        for which in range(2):
+            gconvs_ref[:, which, :] = cut(which, 0, PART)
+            gfilm_ref[:, which, :] = cut(2, which * cond, cond)
+        gblk_ref[...] = jnp.transpose(cut(2, 2 * cond, BLK))[0 : gblk_ref.shape[0]]
+        gskip_ref[...] = cut(3, 0, CH)
+        gdown_ref[...] = cut(3, CH, 3 * CH)
 
     def input_back(q):
         r, c = divmod(q, 3)
@@ -737,17 +864,32 @@
     out_ref, tg_ref, dviews_ref, dt_ref,
     pad_t, pad_m, pad_h, za_ref, zb_ref, sum_ref, aff_ref, ag_ref,
 ):
-    cond = (t_ref.shape[1] - 14 * CH - BLK) // 2
-    cuts = [0]
-    for wide in (5 * CH, 5 * CH, cond, cond, CH, 3 * CH, BLK):
-        cuts.append(cuts[-1] + wide)
-    wa_ref, wb_ref, f0_ref, f1_ref, ws_ref, wd_ref = [
-        t_ref.at[:, cuts[i] : cuts[i + 1]] for i in range(6)
-    ]
-    dwa_ref, dwb_ref, df0_ref, df1_ref, dws_ref, dwd_ref = [
-        dt_ref.at[:, cuts[i] : cuts[i + 1]] for i in range(6)
-    ]
-    aff_ref[...] = jnp.transpose(t_ref[:, cuts[6] :].astype(f32))
+    nz, rows_t = t_ref.shape[0], t_ref.shape[3]
+    cond = arr_ref.shape[1] * CH + emb_ref.shape[1]
+
+    class Part:
+        def __init__(self, ref, q, lo, wide):
+            self.ref, self.q, self.lo, self.wide = ref, q, lo, wide
+
+        def cols(self, key):
+            if not isinstance(key, tuple):
+                return slice(self.lo, self.lo + self.wide)
+            start, stop, _ = key[1].indices(self.wide)
+            return slice(self.lo + start, self.lo + stop)
+
+        def __getitem__(self, key):
+            v = self.ref[:, :, self.q, :, self.cols(key)]
+            return v.reshape(2 * nz * rows_t, v.shape[-1])
+
+        def __setitem__(self, key, v):
+            self.ref[:, :, self.q, :, self.cols(key)] = v.reshape(nz, 2, rows_t, v.shape[-1])
+
+    places = ((0, 0, PART), (1, 0, PART), (2, 0, cond), (2, cond, cond), (3, 0, CH), (3, CH, 3 * CH), (2, 2 * cond, BLK))
+    wa_ref, wb_ref, f0_ref, f1_ref, ws_ref, wd_ref, ext_ref = [Part(t_ref, *place) for place in places]
+    dwa_ref, dwb_ref, df0_ref, df1_ref, dws_ref, dwd_ref, dext_ref = [Part(dt_ref, *place) for place in places]
+    for q, lo in ((2, 2 * cond + BLK), (3, 4 * CH)):
+        dt_ref[:, :, q, :, lo:] = jnp.zeros((nz, 2, rows_t, PART - lo), bf16)
+    aff_ref[...] = jnp.transpose(ext_ref[...].astype(f32))
     ag_ref[...] = jnp.zeros_like(ag_ref)
     ns = mask_ref.shape[0]
     rows = traj_ref.shape[0]
@@ -755,7 +897,7 @@
     edge = 2 * ns
     ones = group_ones(CH, CH // GROUPS)
     inv_n = 1.0 / (nf * (CH // GROUPS))
-    aff = lambda i: aff_ref[i : i + 1, :]
+    aff = lambda i: aff_ref[4 + i : 5 + i, :]
 
     def frames(v):
         return v.reshape(nf, ns, CH)
@@ -880,7 +1022,7 @@
         dview = dcond * slopes[o] / count
         for cam in range(cams):
             dviews_ref[cam, o] = (mask[:, cam : cam + 1] * dview).astype(bf16)
-    dt_ref[:, cuts[6] :] = jnp.transpose(ag_ref[...]).astype(bf16)
+    dext_ref[...] = jnp.transpose(ag_ref[...]).astype(bf16)
 
 
 def call(kernel, outs, in_specs, out_specs, scratch=(), collective_id=None, cost=None):
@@ -982,36 +1124,27 @@
     wide = 9 * ch
     rows = nf * ns
 
-    own_t = jnp.concatenate(
-        [block_convs[:, 0], block_convs[:, 1], film_weight[:, 0], film_weight[:, 1], skip_weight, down_weight,
-         jnp.pad(block_affine, ((0, 0), (0, BLK - block_affine.shape[1])))],
-        axis=1,
-    ).astype(bf16)
-    part = per // cams
-    own_part = lax.dynamic_slice_in_dim(own_t, lax.axis_index("cam") * part, part, 0)
-    line_t = lax.all_gather(own_part, "batch", axis=0)
-    all_t = lax.all_gather(line_t, "cam", axis=1).reshape(ch, own_t.shape[1])
-
-    own_w = jnp.concatenate(
-        [jnp.transpose(encoder_weight[0], (1, 0, 2)),
-         jnp.broadcast_to(jnp.pad(encoder_affine[0], ((0, 0), (0, BLK - 4)))[None], (2, per, BLK))],
-        axis=2,
-    ).astype(bf16)
+    ext = jnp.concatenate([encoder_affine[0], block_affine], axis=1)
+    ext = jnp.pad(ext, ((0, 0), (0, BLK - ext.shape[1]))).astype(bf16)
     x = jnp.transpose(images[0], (2, 0, 1, 3, 4)).reshape(n_img, wide)
     pos = (9, n_img, ch)
-    z1, r1, act, z2, r2, arrived, w_all, enc_aff = call(
+    t_shape = (nz, 2, cams, per, PART)
+    z1, r1, act, z2, r2, arrived, w_all, enc_aff, all_t = call(
         functools.partial(enc_fwd_kernel, n, cams),
         [(pos, f32), ((n_img, ch), f32), (pos, bf16), (pos, f32), ((n_img, ch), f32),
-         ((cams, obs, ns, ch), bf16), ((2, n, per, wide + BLK), bf16), ((8, ch), f32)],
-        [V, V],
-        [H, V, H, H, V, V, H, V],
+         ((cams, obs, ns, ch), bf16), ((2, n, per, wide + BLK), bf16), ((8, ch), f32), (t_shape, bf16)],
+        [V, H, V, V, V, V, V],
+        [H, V, H, H, V, V, H, V, H],
         [pltpu.VMEM((2, n, per, wide + BLK), bf16), pltpu.VMEM(pos, f32), pltpu.VMEM((n_img, wide), bf16),
          pltpu.VMEM(pos, f32), pltpu.VMEM((obs, cams, ns, ch), bf16), pltpu.VMEM((cams, obs, ns, ch), bf16),
+         pltpu.VMEM(t_shape, bf16), pltpu.VMEM((2, min(per, 16), 2, wide), f32),
          DMA((2, 2, nz)), DMA((2, nz)), DMA((2, nz)), DMA((2, nz)), DMA((2, ch // BLK)), DMA((11,)),
-         DMA((cams,)), DMA((cams,))],
+         DMA((cams,)), DMA((cams,)),
+         DMA((2, nz)), DMA((nz,)), DMA((nz, cams)), DMA((nz, cams)), DMA((cams - 1, nz)), DMA((cams - 1, nz)),
+         DMA(()), DMA((max(per // 16, 1),))],
         collective_id=0,
         cost=work(90),
-    )(x, own_w)
+    )(x, encoder_weight[0], block_convs, film_weight, skip_weight, down_weight, ext)
 
     present = view_mask.astype(f32)
     embedded = time_embed(timesteps, TEMB)
@@ -1032,7 +1165,6 @@
     trajectory_grad = jnp.transpose(tg_fm.reshape(nf, ns, ch), (1, 0, 2))
 
     chunk = 3 * ch + BLK
-    t_wide = all_t.shape[1]
     ig, genc, gaff, gconvs, gfilm, gskip, gdown, gblk = call(
         functools.partial(enc_bwd_kernel, n, cams, cond),
         [(pos, f32), ((per, 2, wide), f32), ((4, per), f32), ((per, 2, 5 * ch), f32),
@@ -1044,15 +1176,15 @@
          pltpu.VMEM((BLK, ch), f32), pltpu.VMEM((obs, cams, ns, ch), bf16),
          pltpu.VMEM((2, nz, per, chunk), f32), pltpu.VMEM((2, nz, per, chunk), bf16),
          pltpu.VMEM((3, nz, per, chunk), bf16), pltpu.VMEM((3, 2, nz, per, chunk), bf16),
-         pltpu.VMEM((2, part, t_wide), bf16), pltpu.VMEM((nz, cams, part, t_wide), bf16),
-         pltpu.VMEM((cams - 1, nz, part, t_wide), bf16), pltpu.VMEM((2, nz, part, t_wide), bf16),
-         pltpu.VMEM((cams, part, t_wide), bf16),
+         pltpu.VMEM((2, per, PART), bf16), pltpu.VMEM((nz, cams, per, PART), bf16),
+         pltpu.VMEM((cams - 1, nz, per, PART), bf16), pltpu.VMEM((2, nz, per, PART), bf16),
+         pltpu.VMEM((cams, per, PART), bf16),
          DMA((13,)), DMA((6,)), DMA((6,)), DMA((6, 2, nz)), DMA((6, 2, nz)), DMA((cams,)), DMA((cams,)),
          DMA((nz * cams,)), DMA((nz,)), DMA((nz,)), DMA((cams - 1, nz)), DMA((cams - 1, nz)),
          DMA((2, nz)), DMA((2, nz)), DMA((cams,)), DMA((cams,))],
         collective_id=1,
         cost=work(100),
-    )(x, act, w_all, z1, r1, z2, r2, enc_aff, dviews, dt.reshape(nz, 2, cams, part, t_wide))
+    )(x, act, w_all, z1, r1, z2, r2, enc_aff, dviews, dt)
     images_grad = jnp.transpose(ig.reshape((9, obs) + images.shape[1:3] + (ch,)), (2, 3, 1, 0, 4))[None]
 
     def turned(v):

time: 360 us -> 334 us (0.928)
  waiting for transfers between devices: 35.3 us -> 0 us
  Pallas kernels: 276 us -> 302 us
  between operations: 14.5 us -> 0.92 us
    all_gather x2 -> x0, waiting for transfers between devices: 35.3 us -> none  [the longest x1 35.3 us: shards(): line_t = lax.all_gather(own_part, 'batch', axis=0)]
    pallas_call x1, Pallas kernels: 97.7 us -> 123 us  [shards(): call(functools.partial(enc_fwd_kernel, n, cams), [(pos, f32), ((n_img, ch...]
    unnamed x30 -> x5, local copies, waits for them, and re-layouts: 8.58 us -> 3.85 us
  transfers between devices with their start and end apart: 2 -> 0, of which waited for: 1 -> 0; matrix products, arithmetic and copies ran while one was open for 3% -> 0% of each run, Pallas kernels for 28% -> 0%
where the time goes in v4:
time: 334 us; the launch traced here: 329 us
  Pallas kernels  302 us (90%)
  local copies, waits for them, and re-layouts  22.4 us (7%)
  other arithmetic  3.57 us (1%)
    pallas_call x1, Pallas kernels, shards(): call(functools.partial(enc_bwd_kernel, n, cams, cond), [(pos, f32), ((per...  140 us
    pallas_call x1, Pallas kernels, shards(): call(functools.partial(enc_fwd_kernel, n, cams), [(pos, f32), ((n_img, ch...  123 us
    pallas_call x1, Pallas kernels, shards(): call(temporal_kernel, [((rows // 2, ch), bf16), ((rows, ch), f32), ((cams...  24.5 us
    pallas_call x1, Pallas kernels, adam_call(): pl.pallas_call(adam_kernel, grid=(rows // step,), out_shape=[jax.ShapeDty...  14.5 us
    reshape x1, local copies, waits for them, and re-layouts, shards(): ig.reshape((9, obs) + images.shape[1:3] + (ch,))  8.26 us

profile of v4, /device:TPU:0, one launch (start us, length us, event | category | flops | bytes accessed | tf_op | source)
XLA Modules:
  0.0 329.0 jit_solution(18303735018690521920)
XLA Ops:
  0.7 0.7 convert_element_type.10
  1.3 0.7 bitcast_convert_fusion
  2.0 0.7 convert_element_type.9
  2.7 0.7 convert.9
  3.4 0.1 copy.79
  3.5 0.6 pad.5.ext_ref
  4.1 0.7 copy.80.mask_ref
  4.8 0.1 multiply_sine_fusion
  5.0 0.7 pad_maximum_fusion.emb_ref
  5.7 1.7 copy.77
  7.4 2.1 copy.76
  9.5 2.6 copy.78
  12.1 3.8 %copy.84 = bf16[32,8,9,512]{3,1,2,0:T(8,128)(2,1)} copy(bf16[32,8,9,512]{3,2,1,0:T(8,128)(2,1)S(1)} %bitcast.55) | data formatting | bytes 4718592
  15.9 123.4 %shard_map.433 = (f32[9,256,512]{2,1,0:T(8,128)}, f32[256,512]{1,0:T(8,128)}, bf16[9,256,512]{2,1,0:T(8,128)(2,1)}, f32[9,256,512]{2,1,0:T(8,128)}, f32[256,512]...) custom-call(bf16[256,4608]{1,0:T(8,128)(2,1)} %bitcast.59, ...), custom_call_target="tpu_custom_call" | custom-call | flops 89999998976 | bytes 270000000 | tf_op jit(solution)/shard_map/pallas_call | solution.py:1132
  139.3 24.5 %shard_map.434 = (bf16[256,512]{1,0:T(8,128)(2,1)}, f32[512,512]{1,0:T(8,128)}, bf16[4,2,32,512]{3,2,1,0:T(8,128)(2,1)}, bf16[4,2,4,64,2560]{4,3,2,1,0:T(8,128)(2,1)}) custom-call(bf16[512,512]{1,0:T(8,128)(2,1)} %bitcast.64, bf16[256,512]{1,0:T(8,128)(2,1)} %bitcast.68, bf16[4,2,32,512]{3,2,1,0:T(8,128)(2,1)} %get-tuple-element.66.arr_ref, ...), custom_call_target="tpu_custom_call" | custom-call | flops 20000000000 | bytes 60000000 | tf_op jit(solution)/shard_map/pallas_call | solution.py:1153
  163.8 139.7 %shard_map.435 = (f32[9,256,512]{2,1,0:T(8,128)}, f32[64,2,4608]{2,1,0:T(2,128)}, f32[4,64]{1,0:T(4,128)}, f32[64,2,2560]{2,1,0:T(2,128)}, f32[64,2,1152]{2,1,0:...) custom-call(bf16[256,4608]{1,0:T(8,128)(2,1)} %bitcast.60, ...), custom_call_target="tpu_custom_call" | custom-call | flops 99999997952 | bytes 300000000 | tf_op jit(solution)/shard_map/pallas_call | solution.py:1168
  303.5 0.0 copy-start.1
  303.6 0.0 copy-start
  303.6 8.3 %copy.88 = f32[9,2,4,32,512]{4,1,0,3,2:T(2,128)} copy(f32[9,2,4,32,512]{4,3,2,1,0:T(8,128)} %bitcast.57) | data formatting | bytes 9437184 | tf_op jit(solution)/shard_map/reshape | solution.py:1188
  311.8 0.0 copy-done.1
  311.8 0.9 copy.90
  312.7 0.0 copy-done
  312.7 1.6 copy.89
  314.3 14.5 %shard_map.436 = (f32[64,2,4608]{2,1,0:T(2,128)}, f32[64,2,4608]{2,1,0:T(2,128)}, f32[64,2,4608]{2,1,0:T(2,128)}, f32[4,64]{1,0:T(4,128)}, f32[4,64]{1,0:T(4,128...) custom-call(f32[64,2,4608]{2,1,0:T(2,128)} %bitcast.72, ...), custom_call_target="tpu_custom_call" | custom-call | flops 12000000000 | bytes 36000000 | tf_op jit(solution)/shard_map/pallas_call | solution.py:1102
  (2 shorter events, 0.0 us)
Async XLA Ops:
  303.5 8.3 %copy-start.1 = (bf16[256,512]{1,0:T(8,128)(2,1)S(1)}, bf16[256,512]{1,0:T(8,128)(2,1)}, u32[]{:S(2)}) copy-start(bf16[256,512]{1,0:T(8,128)(2,1)} %get-tuple-element.68) | copy-start | bytes 786436
  303.6 9.1 %copy-start = (f32[512,512]{1,0:T(8,128)S(1)}, f32[512,512]{1,0:T(8,128)}, u32[]{:S(2)}) copy-start(f32[512,512]{1,0:T(8,128)} %get-tuple-element.69) | copy-start | bytes 3145732

commit v5 on v4

--- a/solution.py
+++ b/solution.py
@@ -125,11 +125,11 @@
 
 
 def enc_fwd_kernel(
-    n, cams, x_ref, enc_hbm, convs_ref, film_ref, skip_ref, down_ref, ext_ref,
-    z1_out, r1_ref, a_out, z2_out, r2_ref, arr_ref, w_out, aff_ref, t_out,
-    w_ref, z1_ref, a_ref, z2_ref, feat_ref, arr_s, t_ref, enc_buf,
+    n, cams, img_ref, enc_hbm, convs_ref, film_ref, skip_ref, down_ref, ext_ref,
+    z1_out, r1_ref, a_out, z2_out, r2_ref, arr_ref, w_out, aff_ref, t_out, x_out,
+    x_ref, w_ref, z1_ref, a_ref, z2_ref, feat_ref, arr_s, t_ref, enc_buf,
     zsend, zrecv, csend, crecv, wsem, osem, fsend, frecv,
-    tzsend, tzrecv, tcsend, tcrecv, tpsend, tprecv, tsem, esem,
+    tzsend, tzrecv, tcsend, tcrecv, tpsend, tprecv, tsem, esem, xsem,
 ):
     nz = n // 2
     rows = ext_ref.shape[0]
@@ -246,6 +246,16 @@
         return carry
 
     lax.fori_loop(0, count, pack, 0)
+
+    def x_save(p):
+        return pltpu.make_async_copy(x_ref.at[:, p * CH : (p + 1) * CH], x_out.at[p], xsem.at[p])
+
+    half = n_img // 2
+    for p in range(9):
+        pair = img_ref[:, p].astype(f32)
+        for o in range(2):
+            x_ref[o * half : (o + 1) * half, p * CH : (p + 1) * CH] = pair[:, o].astype(bf16)
+        x_save(p).start()
     for conv in range(2):
         core_copy(conv, zi, core).start()
 
@@ -446,6 +456,8 @@
 
     lax.fori_loop(0, nz, t_drain, 0)
     t_save().wait()
+    for p in range(9):
+        x_save(p).wait()
 
 
 def enc_bwd_kernel(
@@ -474,10 +486,7 @@
         "z1": pltpu.make_async_copy(z1_hbm, z1_ref, lsem.at[1]),
         "a": pltpu.make_async_copy(a_hbm, a_ref, lsem.at[2]),
     }
-    x_loads = [
-        pltpu.make_async_copy(x_hbm.at[:, p * CH : (p + 1) * CH], x_ref.at[p], lsem.at[4 + p])
-        for p in range(9)
-    ]
+    x_loads = [pltpu.make_async_copy(x_hbm, x_ref, lsem.at[4])]
     loads["z2"].start()
     for load in x_loads:
         load.start()
@@ -723,7 +732,7 @@
 
     def finish(k):
         def write(v):
-            genc_ref[:, 1 - k // 3, (k % 3) * chunk : (k % 3 + 1) * chunk] = v[:, 0:chunk]
+            genc_ref[1 - k // 3, :, (k % 3) * chunk : (k % 3 + 1) * chunk] = v[:, 0:chunk]
             if k == 5:
                 gaff_ref[...] = jnp.transpose(v[:, chunk:])[0 : gaff_ref.shape[0]]
 
@@ -757,8 +766,8 @@
             return t_all[q, :, lo : lo + wide].astype(f32)
 
         for which in range(2):
-            gconvs_ref[:, which, :] = cut(which, 0, PART)
-            gfilm_ref[:, which, :] = cut(2, which * cond, cond)
+            gconvs_ref[which] = cut(which, 0, PART)
+            gfilm_ref[which] = cut(2, which * cond, cond)
         gblk_ref[...] = jnp.transpose(cut(2, 2 * cond, BLK))[0 : gblk_ref.shape[0]]
         gskip_ref[...] = cut(3, 0, CH)
         gdown_ref[...] = cut(3, CH, 3 * CH)
@@ -1069,45 +1078,94 @@
     return (weight_new, mean_new, square_new)
 
 
-def adam_kernel(*refs):
+MATRIX, VECTOR = (0, 2, 3, 4, 5), (1, 6)
+
+
+def cut_of(width):
+    return next(width // d for d in (1, 2, 3) if width % (d * BLK) == 0 and width // d <= 3 * CH)
+
+
+def adam_kernel(rows, widths, *refs):
+    ins, ig_hbm = refs[0:28], refs[28]
+    outs, ig_out = refs[29:50], refs[50]
+    bufs, lsem, ssem, gsem = refs[51:71], refs[71], refs[72], refs[73]
+    half = ig_hbm.shape[1] // 2
+    moves = [
+        pltpu.make_async_copy(ig_hbm.at[p, o * half : (o + 1) * half], ig_out.at[:, p, o], gsem.at[2 * p + o])
+        for p in range(9)
+        for o in range(2)
+    ]
+
+    def place(ref, which, lo, wide):
+        cols = slice(lo, lo + wide)
+        if len(ref.shape) == 2:
+            return ref.at[:, cols]
+        return ref.at[which, :, cols] if ref.shape[0] == 2 and ref.shape[1] == rows else ref.at[:, which, cols]
+
+    chunks = []
+    for at, i in enumerate(MATRIX):
+        whiches, width = widths[at]
+        cut = cut_of(width)
+        chunks += [(at, i, which, lo, min(cut, width - lo)) for which in range(whiches) for lo in range(0, width, cut)]
+    loads, stores = [], []
+    for c, (at, i, which, lo, wide) in enumerate(chunks):
+        for j in range(4):
+            buf = bufs[4 * at + j].at[which, :, lo : lo + wide]
+            loads.append(pltpu.make_async_copy(place(ins[4 * i + j], which, lo, wide), buf, lsem.at[4 * c + j]))
+            if j < 3:
+                stores.append(pltpu.make_async_copy(buf, place(outs[3 * i + j], which, lo, wide), ssem.at[3 * c + j]))
+    for load in loads:
+        load.start()
+    for move in moves:
+        move.start()
+    for i in VECTOR:
+        w_ref, m_ref, v_ref, g_ref = ins[4 * i : 4 * i + 4]
+        new = adamw(w_ref[...], g_ref[...], m_ref[...], v_ref[...], rate_vector, 0.0)
+        for ref, value in zip(outs[3 * i : 3 * i + 3], new):
+            ref[...] = value
+    for c, (at, i, which, lo, wide) in enumerate(chunks):
+        for load in loads[4 * c : 4 * c + 4]:
+            load.wait()
+
+        def step(r, carry):
+            at_rows = pl.ds(pl.multiple_of(r * 8, 8), 8)
+            w, m, v, g = [bufs[4 * at + j][which, at_rows, lo : lo + wide] for j in range(4)]
+            for j, value in enumerate(adamw(w, g, m, v, rate_matrix, decay_matrix)):
+                bufs[4 * at + j][which, at_rows, lo : lo + wide] = value
+            return carry
+
+        lax.fori_loop(0, rows // 8, step, 0)
+        for store in stores[3 * c : 3 * c + 3]:
+            store.start()
+    for store in stores:
+        store.wait()
+    for move in moves:
+        move.wait()
+
+
+def adam_call(shown, grads, ig, ig_shape, rows):
+    ins, in_specs, outs, out_specs, bufs, widths, count = [], [], [], [], [], [], 0
     for i in range(7):
-        w_ref, m_ref, v_ref, g_ref = refs[4 * i : 4 * i + 4]
-        outs = refs[28 + 3 * i : 31 + 3 * i]
-
-        def update():
-            vector = i in (1, 6)
-            rate, decay = (rate_vector, 0.0) if vector else (rate_matrix, decay_matrix)
-            new = adamw(w_ref[...], g_ref[...], m_ref[...], v_ref[...], rate, decay)
-            for ref, value in zip(outs, new):
-                ref[...] = value
-
-        if i in (1, 6):
-            pl.when(pl.program_id(0) == 0)(update)
-        else:
-            update()
-
-
-def adam_call(shown, grads, rows):
-    step = min(rows, 8)
-
-    def spec(v):
-        if v.shape[0] != rows:
-            return pl.BlockSpec(v.shape, lambda r: (0, 0))
-        return pl.BlockSpec((step,) + v.shape[1:], lambda r: (r,) + (0,) * (v.ndim - 1))
-
-    ins = []
-    for i in range(7):
+        w = shown[0][i]
+        space = V if i in VECTOR else H
         ins += [shown[0][i], shown[1][i], shown[2][i], grads[i]]
-    outs = [w for w in shown[0] for _ in range(3)]
+        in_specs += [space] * 4
+        outs += [jax.ShapeDtypeStruct(w.shape, f32)] * 3
+        out_specs += [space] * 3
+        if i in MATRIX:
+            whiches, width = (2 if w.ndim == 3 else 1), w.shape[-1]
+            widths.append((whiches, width))
+            count += whiches * (width // cut_of(width))
+            bufs += [pltpu.VMEM((whiches, rows, width), f32)] * 4
     return pl.pallas_call(
-        adam_kernel,
-        grid=(rows // step,),
-        out_shape=[jax.ShapeDtypeStruct(v.shape, f32) for v in outs],
-        in_specs=[spec(v) for v in ins],
-        out_specs=[spec(v) for v in outs],
+        functools.partial(adam_kernel, rows, tuple(widths)),
+        out_shape=outs + [jax.ShapeDtypeStruct(ig_shape, f32)],
+        in_specs=in_specs + [H],
+        out_specs=out_specs + [H],
+        scratch_shapes=bufs + [DMA((4 * count,)), DMA((3 * count,)), DMA((18,))],
         compiler_params=pltpu.CompilerParams(vmem_limit_bytes=VMEM_BYTES),
         cost_estimate=work(12),
-    )(*ins)
+    )(*ins, ig)
 
 
 def shards(
@@ -1126,25 +1184,25 @@
 
     ext = jnp.concatenate([encoder_affine[0], block_affine], axis=1)
     ext = jnp.pad(ext, ((0, 0), (0, BLK - ext.shape[1]))).astype(bf16)
-    x = jnp.transpose(images[0], (2, 0, 1, 3, 4)).reshape(n_img, wide)
+    pairs = jnp.transpose(images[0], (0, 1, 3, 2, 4)).reshape(n_img // obs, 9, obs, ch)
     pos = (9, n_img, ch)
     t_shape = (nz, 2, cams, per, PART)
-    z1, r1, act, z2, r2, arrived, w_all, enc_aff, all_t = call(
+    z1, r1, act, z2, r2, arrived, w_all, enc_aff, all_t, x = call(
         functools.partial(enc_fwd_kernel, n, cams),
         [(pos, f32), ((n_img, ch), f32), (pos, bf16), (pos, f32), ((n_img, ch), f32),
-         ((cams, obs, ns, ch), bf16), ((2, n, per, wide + BLK), bf16), ((8, ch), f32), (t_shape, bf16)],
+         ((cams, obs, ns, ch), bf16), ((2, n, per, wide + BLK), bf16), ((8, ch), f32), (t_shape, bf16), (pos, bf16)],
         [V, H, V, V, V, V, V],
-        [H, V, H, H, V, V, H, V, H],
-        [pltpu.VMEM((2, n, per, wide + BLK), bf16), pltpu.VMEM(pos, f32), pltpu.VMEM((n_img, wide), bf16),
+        [H, V, H, H, V, V, H, V, H, H],
+        [pltpu.VMEM((n_img, wide), bf16), pltpu.VMEM((2, n, per, wide + BLK), bf16), pltpu.VMEM(pos, f32), pltpu.VMEM((n_img, wide), bf16),
          pltpu.VMEM(pos, f32), pltpu.VMEM((obs, cams, ns, ch), bf16), pltpu.VMEM((cams, obs, ns, ch), bf16),
          pltpu.VMEM(t_shape, bf16), pltpu.VMEM((2, min(per, 16), 2, wide), f32),
          DMA((2, 2, nz)), DMA((2, nz)), DMA((2, nz)), DMA((2, nz)), DMA((2, ch // BLK)), DMA((11,)),
          DMA((cams,)), DMA((cams,)),
          DMA((2, nz)), DMA((nz,)), DMA((nz, cams)), DMA((nz, cams)), DMA((cams - 1, nz)), DMA((cams - 1, nz)),
-         DMA(()), DMA((max(per // 16, 1),))],
+         DMA(()), DMA((max(per // 16, 1),)), DMA((9,))],
         collective_id=0,
         cost=work(90),
-    )(x, encoder_weight[0], block_convs, film_weight, skip_weight, down_weight, ext)
+    )(pairs, encoder_weight[0], block_convs, film_weight, skip_weight, down_weight, ext)
 
     present = view_mask.astype(f32)
     embedded = time_embed(timesteps, TEMB)
@@ -1167,8 +1225,8 @@
     chunk = 3 * ch + BLK
     ig, genc, gaff, gconvs, gfilm, gskip, gdown, gblk = call(
         functools.partial(enc_bwd_kernel, n, cams, cond),
-        [(pos, f32), ((per, 2, wide), f32), ((4, per), f32), ((per, 2, 5 * ch), f32),
-         ((per, 2, cond), f32), ((per, ch), f32), ((per, 3 * ch), f32), ((10, per), f32)],
+        [(pos, f32), ((2, per, wide), f32), ((4, per), f32), ((2, per, 5 * ch), f32),
+         ((2, per, cond), f32), ((per, ch), f32), ((per, 3 * ch), f32), ((10, per), f32)],
         [H, H, H, H, V, H, V, V, V, H],
         [V] * 8,
         [pltpu.VMEM(pos, bf16), pltpu.VMEM(pos, bf16), pltpu.VMEM((n, per, wide), bf16), pltpu.VMEM(pos, f32),
@@ -1185,8 +1243,6 @@
         collective_id=1,
         cost=work(100),
     )(x, act, w_all, z1, r1, z2, r2, enc_aff, dviews, dt)
-    images_grad = jnp.transpose(ig.reshape((9, obs) + images.shape[1:3] + (ch,)), (2, 3, 1, 0, 4))[None]
-
     def turned(v):
         return jnp.transpose(v.reshape(v.shape[-2:]))
 
@@ -1197,7 +1253,9 @@
         [turned(v) if i in (1, 6) else v.reshape(v.shape[-3:]) if i == 0 else v for i, v in enumerate(group)]
         for group in (weights, firsts, seconds)
     ]
-    news = adam_call(shown, (genc, gaff, gconvs, gfilm, gskip, gdown, gblk), per)
+    ig_shape = (n_img // obs, 9, obs, ch)
+    *news, ig_new = adam_call(shown, (genc, gaff, gconvs, gfilm, gskip, gdown, gblk), ig, ig_shape, per)
+    images_grad = jnp.transpose(ig_new.reshape(images.shape[1:3] + ig_shape[1:]), (0, 1, 3, 2, 4))[None]
     upd = [
         tuple((turned(v) if i in (1, 6) else v).reshape(w.shape) for v in news[3 * i : 3 * i + 3])
         for i, w in enumerate(weights)

time: 334 us -> 451 us (1.35)
  Pallas kernels: 302 us -> 435 us
  local copies, waits for them, and re-layouts: 22.4 us -> 7.72 us
    pallas_call x2, Pallas kernels: 154 us -> 286 us  [the longest x1 147 us: adam_call(): pl.pallas_call(functools.partial(adam_kernel, rows, tuple(widths)), out_s...]
    reshape x1 -> x0, local copies, waits for them, and re-layouts: 8.26 us -> none  [shards(): ig.reshape((9, obs) + images.shape[1:3] + (ch,))]
where the time goes in v5:
time: 451 us; the launch traced here: 447 us
  Pallas kernels  435 us (96%)
  local copies, waits for them, and re-layouts  7.72 us (2%)
    pallas_call x1, Pallas kernels, adam_call(): pl.pallas_call(functools.partial(adam_kernel, rows, tuple(widths)), out_s...  147 us
    pallas_call x1, Pallas kernels, shards(): call(functools.partial(enc_bwd_kernel, n, cams, cond), [(pos, f32), ((2,...  139 us
    pallas_call x1, Pallas kernels, shards(): call(functools.partial(enc_fwd_kernel, n, cams), [(pos, f32), ((n_img, ch...  124 us
    pallas_call x1, Pallas kernels, shards(): call(temporal_kernel, [((rows // 2, ch), bf16), ((rows, ch), f32), ((cams...  24.5 us

profile of v5, /device:TPU:0, one launch (start us, length us, event | category | flops | bytes accessed | tf_op | source)
XLA Modules:
  0.0 447.3 jit_solution(18218936391609531850)
XLA Ops:
  0.7 0.7 convert_element_type.10
  1.3 0.7 bitcast_convert_fusion
  2.0 0.7 convert_element_type.9
  2.7 0.7 convert.9
  3.4 0.1 copy.65
  3.5 0.6 pad.5.ext_ref
  4.1 0.7 copy.66.mask_ref
  4.8 0.1 multiply_sine_fusion
  5.0 0.7 pad_maximum_fusion.emb_ref
  5.7 1.7 copy.64
  7.4 2.1 copy.63
  9.5 124.3 %shard_map.433 = (f32[9,256,512]{2,1,0:T(8,128)}, f32[256,512]{1,0:T(8,128)}, bf16[9,256,512]{2,1,0:T(8,128)(2,1)}, f32[9,256,512]{2,1,0:T(8,128)}, f32[256,512]...) custom-call(bf16[128,9,2,512]{3,2,1,0:T(2,128)(2,1)} %bitcast.63, ...), custom_call_target="tpu_custom_call" | custom-call | flops 89999998976 | bytes 270000000 | tf_op jit(solution)/shard_map/pallas_call | solution.py:1190
  133.8 24.5 %shard_map.434 = (bf16[256,512]{1,0:T(8,128)(2,1)}, f32[512,512]{1,0:T(8,128)}, bf16[4,2,32,512]{3,2,1,0:T(8,128)(2,1)}, bf16[4,2,4,64,2560]{4,3,2,1,0:T(8,128)(2,1)}) custom-call(bf16[512,512]{1,0:T(8,128)(2,1)} %bitcast.56, bf16[256,512]{1,0:T(8,128)(2,1)} %bitcast.60, bf16[4,2,32,512]{3,2,1,0:T(8,128)(2,1)} %get-tuple-element.68.arr_ref, ...), custom_call_target="tpu_custom_call" | custom-call | flops 20000000000 | bytes 60000000 | tf_op jit(solution)/shard_map/pallas_call | solution.py:1211
  158.3 0.0 copy-start.1
  158.3 0.0 copy-start
  158.3 139.5 %shard_map.435 = (f32[9,256,512]{2,1,0:T(8,128)}, f32[2,64,4608]{2,1,0:T(8,128)}, f32[4,64]{1,0:T(4,128)}, f32[2,64,2560]{2,1,0:T(8,128)}, f32[2,64,1152]{2,1,0:...) custom-call(bf16[9,256,512]{2,1,0:T(8,128)(2,1)} %get-tuple-element.72.x_hbm, ...), custom_call_target="tpu_custom_call" | custom-call | flops 99999997952 | bytes 300000000 | tf_op jit(solution)/shard_map/pallas_call | solution.py:1226
  297.7 0.0 copy-done.1
  297.8 0.9 copy.72
  298.6 0.0 copy-done
  298.6 1.6 copy.71
  300.2 146.7 %shard_map.436 = (f32[64,2,4608]{2,1,0:T(2,128)}, f32[64,2,4608]{2,1,0:T(2,128)}, f32[64,2,4608]{2,1,0:T(2,128)}, f32[4,64]{1,0:T(4,128)}, f32[4,64]{1,0:T(4,128...) custom-call(f32[64,2,4608]{2,1,0:T(2,128)} %bitcast.65, ...), custom_call_target="tpu_custom_call" | custom-call | flops 12000000000 | bytes 36000000 | tf_op jit(solution)/shard_map/pallas_call | solution.py:1160
  (2 shorter events, 0.0 us)
Async XLA Ops:
  158.3 139.5 %copy-start.1 = (bf16[256,512]{1,0:T(8,128)(2,1)S(1)}, bf16[256,512]{1,0:T(8,128)(2,1)}, u32[]{:S(2)}) copy-start(bf16[256,512]{1,0:T(8,128)(2,1)} %get-tuple-element.70) | copy-start | bytes 786436
  158.3 140.3 %copy-start = (f32[512,512]{1,0:T(8,128)S(1)}, f32[512,512]{1,0:T(8,128)}, u32[]{:S(2)}) copy-start(f32[512,512]{1,0:T(8,128)} %get-tuple-element.71) | copy-start | bytes 3145732

commit v6 on v4

--- a/solution.py
+++ b/solution.py
@@ -90,6 +90,17 @@
 
 
 def line_barrier(cams, nz):
+    line_greet(cams, nz)
+    line_wait(cams, nz)
+
+
+def line_wait(cams, nz):
+    zi = lax.axis_index("batch") // 2
+    ends = (zi == 0).astype(jnp.int32) + (zi == nz - 1).astype(jnp.int32)
+    pl.semaphore_wait(pltpu.get_barrier_semaphore(), cams + 2 - ends)
+
+
+def line_greet(cams, nz):
     me, cam = lax.axis_index("batch"), lax.axis_index("cam")
     zi, core = me // 2, me % 2
     barrier = pltpu.get_barrier_semaphore()
@@ -105,34 +116,33 @@
     def _():
         pl.semaphore_signal(barrier, inc=1, device_id={"batch": me + 2}, device_id_type=MESH)
 
-    ends = (zi == 0).astype(jnp.int32) + (zi == nz - 1).astype(jnp.int32)
-    pl.semaphore_wait(barrier, cams + 2 - ends)
-
 
 PART = 5 * CH
 
 
-def pack_temporal(ref, convs_ref, film_ref, skip_ref, down_ref, ext_ref):
+def pack_temporal(ref, convs_ref, film_ref, skip_ref, down_ref, ext):
     rows, cond = film_ref.shape[0], film_ref.shape[2]
     for q in range(2):
         ref[q] = convs_ref[:, q, :].astype(bf16)
         ref[2, :, q * cond : (q + 1) * cond] = film_ref[:, q, :].astype(bf16)
-    ref[2, :, 2 * cond : 2 * cond + BLK] = ext_ref[...]
+    ref[2, :, 2 * cond : 2 * cond + BLK] = ext
     ref[2, :, 2 * cond + BLK :] = jnp.zeros((rows, PART - 2 * cond - BLK), bf16)
     ref[3, :, 0:CH] = skip_ref[...].astype(bf16)
     ref[3, :, CH : 4 * CH] = down_ref[...].astype(bf16)
     ref[3, :, 4 * CH :] = jnp.zeros((rows, PART - 4 * CH), bf16)
 
 
-def enc_fwd_kernel(
-    n, cams, x_ref, enc_hbm, convs_ref, film_ref, skip_ref, down_ref, ext_ref,
-    z1_out, r1_ref, a_out, z2_out, r2_ref, arr_ref, w_out, aff_ref, t_out,
-    w_ref, z1_ref, a_ref, z2_ref, feat_ref, arr_s, t_ref, enc_buf,
+def forward_kernel(
+    n, cams, img_ref, traj_ref, og_in, mask_ref, emb_ref, enc_hbm, convs_ref, film_ref, skip_ref, down_ref,
+    ea_ref, ba_ref,
+    z1_out, r1_ref, a_out, z2_out, r2_ref, w_out, aff_ref, x_out, out_ref, tg_ref, gp_ref, dt_out,
+    x_ref, w_ref, z1_ref, a_ref, z2_ref, feat_ref, arr_s, t_ref, enc_buf,
+    ext_s, og_ref, pad_t, pad_m, pad_h, sum_ref, taff_ref, ag_ref, rstd_ref, dviews_ref, gp_s, dt_buf,
     zsend, zrecv, csend, crecv, wsem, osem, fsend, frecv,
-    tzsend, tzrecv, tcsend, tcrecv, tpsend, tprecv, tsem, esem,
+    tzsend, tzrecv, tcsend, tcrecv, tpsend, tprecv, esem, xsem, vsend, vrecv, dsem,
 ):
     nz = n // 2
-    rows = ext_ref.shape[0]
+    rows = skip_ref.shape[0]
     piece = enc_buf.shape[1]
     spb = BLK // rows
     n_img = x_ref.shape[0]
@@ -146,7 +156,11 @@
         return pltpu.make_async_copy(enc_hbm.at[pl.ds(i * piece, piece)], enc_buf.at[i % 2], esem.at[i])
 
     enc_load(0).start()
-    pack_temporal(t_ref.at[zi, core], convs_ref, film_ref, skip_ref, down_ref, ext_ref)
+    ext_s[...] = jnp.zeros_like(ext_s)
+    ext_s[0:4] = ea_ref[...]
+    ext_s[4:14] = ba_ref[...]
+    ext = jnp.transpose(ext_s[...]).astype(bf16)
+    pack_temporal(t_ref.at[zi, core], convs_ref, film_ref, skip_ref, down_ref, ext)
 
     line_barrier(cams, nz)
 
@@ -186,9 +200,6 @@
                     tp_copy(k, step, q).wait_recv()
                     tc_copy(k, core, q).start()
 
-    def t_save():
-        return pltpu.make_async_copy(t_ref, t_out, tsem)
-
     def t_complete():
         def body(k, carry):
             for q in range(cams):
@@ -196,7 +207,203 @@
             return carry
 
         lax.fori_loop(0, nz, body, 0)
-        t_save().start()
+
+    ns, nf = traj_ref.shape[0], traj_ref.shape[1]
+    frows = ns * nf
+    obs = arr_s.shape[1]
+    cond = obs * CH + emb_ref.shape[1]
+    edge = 2 * ns
+    per_pos = frows // n_img
+    gones_shape = CH // GROUPS
+    ginv = 1.0 / (nf * gones_shape)
+
+    class Part:
+        def __init__(self, ref, index, lo, wide):
+            self.ref, self.index, self.lo, self.wide = ref, index, lo, wide
+
+        def where(self, key):
+            if not isinstance(key, tuple):
+                return self.index(slice(self.lo, self.lo + self.wide))
+            start, stop, _ = key[1].indices(self.wide)
+            return self.index(slice(self.lo + start, self.lo + stop))
+
+        def __getitem__(self, key):
+            v = self.ref[self.where(key)]
+            return v.reshape(CH, v.shape[-1])
+
+        def __setitem__(self, key, v):
+            self.ref[self.where(key)] = v.reshape(nz, 2, rows, v.shape[-1])
+
+    def weight(q, lo, wide):
+        return Part(t_ref, lambda cols: (slice(None), slice(None), q, slice(None), cols), lo, wide)
+
+    def grad(buf, lo, wide):
+        return Part(dt_buf, lambda cols: (buf, slice(None), slice(None), slice(None), cols), lo, wide)
+
+    wa, wb = weight(0, 0, PART), weight(1, 0, PART)
+    f0, f1, wext = weight(2, 0, cond), weight(2, cond, cond), weight(2, 2 * cond, BLK)
+    ws, wd = weight(3, 0, CH), weight(3, CH, 3 * CH)
+
+    def dt_save(q, buf):
+        return pltpu.make_async_copy(dt_buf.at[buf], dt_out.at[:, :, q], dsem.at[q])
+
+    def blank(buf, lo):
+        dt_buf[buf, :, :, :, lo:] = jnp.zeros((nz, 2, rows, PART - lo), bf16)
+
+    def tail(i):
+        return taff_ref[4 + i : 5 + i, :]
+
+    def frames(v):
+        return v.reshape(nf, ns, CH)
+
+    def keep(i, v):
+        z1_ref[per_pos * i : per_pos * (i + 1)] = v.reshape(per_pos, n_img, CH)
+
+    def kept(i):
+        return z1_ref[per_pos * i : per_pos * (i + 1)].reshape(nf, ns, CH)
+
+    def fill_edges(pad_ref):
+        pad_ref[0:edge, :] = jnp.zeros((edge, CH), bf16)
+        pad_ref[edge + frows : edge + frows + edge, :] = jnp.zeros((edge, CH), bf16)
+
+    def fill(pad_ref, v):
+        fill_edges(pad_ref)
+        pad_ref[edge : edge + frows, :] = v.astype(bf16).reshape(frows, CH)
+
+    def conv5(pad_ref, w):
+        return sum(
+            dot(pad_ref[t * ns : t * ns + frows, :], w[:, t * CH : (t + 1) * CH], NT) for t in range(5)
+        )
+
+    def conv5_back(pad_ref, w):
+        return sum(
+            dot(pad_ref[(4 - t) * ns : (4 - t) * ns + frows, :], w[:, t * CH : (t + 1) * CH]) for t in range(5)
+        )
+
+    def gsum(v):
+        return group_sum(v, group_ones(CH, gones_shape)) * ginv
+
+    def norm(v):
+        v = frames(v)
+        centred = v - gsum(jnp.sum(v, axis=0))[None]
+        rstd = lax.rsqrt(gsum(jnp.sum(centred * centred, axis=0)) + norm_eps)
+        return centred * rstd[None], rstd
+
+    def norm_back(du, z, rstd, gain):
+        s0 = jnp.sum(du, axis=0)
+        s1 = jnp.sum(du * z, axis=0)
+        dv = (du * gain[None] - gsum(s0 * gain)[None] - z * gsum(s1 * gain)[None]) * rstd[None]
+        return dv, jnp.sum(s1, axis=0, keepdims=True), jnp.sum(s0, axis=0, keepdims=True)
+
+    def total(v):
+        return jnp.sum(v, axis=(0, 1)).reshape(1, CH)
+
+    def temporal_early():
+        taff_ref[...] = jnp.transpose(wext[...].astype(f32))
+        ag_ref[...] = jnp.zeros_like(ag_ref)
+        traj = pad_t[edge : edge + frows, :]
+        za, rstd = norm(conv5(pad_t, wa) + tail(4))
+        rstd_ref[...] = rstd
+        keep(0, za)
+        keep(1, dot(traj, ws[...], NT) + tail(8))
+        og = og_ref[...]
+        dcols = [dot(og, wd[:, t * CH : (t + 1) * CH]).reshape(nf // 2, ns, CH) for t in range(3)]
+        before = jnp.concatenate([dcols[0][1:], jnp.zeros((1, ns, CH), f32)], axis=0)
+        dsum = jnp.stack([dcols[1], dcols[2] + before], axis=1).reshape(nf, ns, CH)
+        keep(2, dsum)
+        ag_ref[8:9, :] = total(dsum)
+        ag_ref[9:10, :] = jnp.sum(og.astype(f32), axis=0, keepdims=True)
+        dskip = dsum.astype(bf16).reshape(frows, CH)
+        grad(0, 0, CH)[...] = dot(dskip, traj, TN).astype(bf16)
+        blank(0, 4 * CH)
+        tg_ref[...] = dot(dskip, ws[...])
+
+    def view_copy(to, sender):
+        return cam_copy(dviews_ref.at[to], gp_s.at[:, sender], vsend.at[to], vrecv.at[sender], to)
+
+    def temporal_rest():
+        mask = mask_ref[...]
+        seen = jnp.sum(mask, axis=1, keepdims=True)
+        conds, slopes = [], []
+        for o in range(obs):
+            pooled = sum(mask[:, c : c + 1] * arr_s[c, o].astype(f32) for c in range(cams))
+            value, slope = mish_pair(pooled / seen)
+            conds.append(value.astype(bf16))
+            slopes.append(slope)
+        conds.append(mish_value(emb_ref[...]).astype(bf16))
+        lanes = [slice(o * CH, (o + 1) * CH) for o in range(obs)] + [slice(obs * CH, cond)]
+        scale, shift = [
+            sum(dot(v, w[:, cols], NT) for v, cols in zip(conds, lanes)) + tail(i) for i, w in ((6, f0), (7, f1))
+        ]
+        za = kept(0)
+        fill(pad_m, mish_value(za * tail(0)[None] + tail(1)[None]) * scale[None] + shift[None])
+        zb, rstd_b = norm(conv5(pad_m, wb) + tail(5))
+        act_b, slope = mish_pair(zb * tail(2)[None] + tail(3)[None])
+        keep(3, act_b + kept(1))
+        dhb, ag_ref[2:3, :], ag_ref[3:4, :] = norm_back(kept(2) * slope, zb, rstd_b, tail(2))
+        ag_ref[5:6, :] = total(dhb)
+        fill(pad_h, dhb)
+        dmid = frames(conv5_back(pad_h, wb))
+        za = kept(0)
+        act_a, slope = mish_pair(za * tail(0)[None] + tail(1)[None])
+        dscale = jnp.sum(dmid * act_a, axis=0)
+        dshift = jnp.sum(dmid, axis=0)
+        lows = (dscale.astype(bf16), dshift.astype(bf16))
+        for o in range(obs):
+            dcond = dot(lows[0], f0[:, lanes[o]]) + dot(lows[1], f1[:, lanes[o]])
+            dview = dcond * slopes[o] / seen
+            for c in range(cams):
+                dviews_ref[c, o] = (mask[:, c : c + 1] * dview).astype(bf16)
+        for step in range(1, cams):
+            view_copy((cam + step) % cams, cam).start()
+        gp_s[:, cam] = dviews_ref[cam]
+
+        dha, ag_ref[0:1, :], ag_ref[1:2, :] = norm_back(dmid * scale[None] * slope, za, rstd_ref[...], tail(0))
+        ag_ref[4:5, :] = total(dha)
+        ag_ref[6:7, :] = jnp.sum(dscale, axis=0, keepdims=True)
+        ag_ref[7:8, :] = jnp.sum(dshift, axis=0, keepdims=True)
+        dwb = grad(1, 0, PART)
+        hb = pad_h[edge : edge + frows, :]
+        for t in range(5):
+            dwb[:, t * CH : (t + 1) * CH] = dot(hb, pad_m[t * ns : t * ns + frows, :], TN).astype(bf16)
+        dt_save(1, 1).start()
+        pairs = kept(3).astype(bf16).reshape(nf // 2, 2, ns, CH)
+        half = frows // 2
+        sum_ref[0:ns, :] = jnp.zeros((ns, CH), bf16)
+        sum_ref[ns : ns + half, :] = pairs[:, 1].reshape(half, CH)
+        sum_ref[ns + half : ns + 2 * half, :] = pairs[:, 0].reshape(half, CH)
+        og = og_ref[...]
+        dwd = grad(0, CH, 3 * CH)
+        out = None
+        for t, at in enumerate((0, ns + half, ns)):
+            cols = sum_ref[at : at + half, :]
+            part = dot(cols, wd[:, t * CH : (t + 1) * CH], NT)
+            out = part if out is None else out + part
+            dwd[:, t * CH : (t + 1) * CH] = dot(og, cols, TN).astype(bf16)
+        dt_save(3, 0).start()
+        out_ref[...] = (out + tail(9)).astype(bf16)
+        fill(pad_h, dha)
+        tg_ref[...] = tg_ref[...] + conv5_back(pad_h, wa)
+        dt_save(1, 1).wait()
+        for base, low in zip((0, cond), lows):
+            dw = grad(1, base, cond)
+            for v, cols in zip(conds, lanes):
+                dw[:, cols] = dot(low, v, TN).astype(bf16)
+        grad(1, 2 * cond, BLK)[...] = jnp.transpose(ag_ref[...]).astype(bf16)
+        blank(1, 2 * cond + BLK)
+        dt_save(2, 1).start()
+        dt_save(3, 0).wait()
+        dwa = grad(0, 0, PART)
+        ha = pad_h[edge : edge + frows, :]
+        for t in range(5):
+            dwa[:, t * CH : (t + 1) * CH] = dot(ha, pad_t[t * ns : t * ns + frows, :], TN).astype(bf16)
+        dt_save(0, 0).start()
+        for step in range(1, cams):
+            other = (cam + step) % cams
+            view_copy(other, other).wait_recv()
+        gp_ref[...] = gp_s[...]
+        dt_save(2, 1).wait()
+        dt_save(0, 0).wait()
 
     def z_copy(conv, k, way):
         ref = w_ref.at[conv, 2 * k + core]
@@ -230,7 +437,7 @@
     for q in range(cams):
         tc_copy(zi, core, q).start()
     for conv in range(2):
-        w_ref[conv, me, :, 9 * CH :] = ext_ref[...]
+        w_ref[conv, me, :, 9 * CH :] = ext
     count = rows // piece
 
     def pack(i, carry):
@@ -246,6 +453,23 @@
         return carry
 
     lax.fori_loop(0, count, pack, 0)
+
+    def x_save(p):
+        return pltpu.make_async_copy(x_ref.at[:, p * CH : (p + 1) * CH], x_out.at[p], xsem.at[p])
+
+    fill_edges(pad_t)
+    moved = traj_ref[...].astype(f32)
+    for f in range(nf):
+        pad_t[edge + f * ns : edge + (f + 1) * ns, :] = moved[:, f].astype(bf16)
+    moved = og_in[...].astype(f32)
+    for f in range(nf // 2):
+        og_ref[f * ns : (f + 1) * ns, :] = moved[:, f].astype(bf16)
+    half = n_img // 2
+    for p in range(9):
+        pair = img_ref[:, p].astype(f32)
+        for o in range(2):
+            x_ref[o * half : (o + 1) * half, p * CH : (p + 1) * CH] = pair[:, o].astype(bf16)
+        x_save(p).start()
     for conv in range(2):
         core_copy(conv, zi, core).start()
 
@@ -357,7 +581,12 @@
             if conv == 1:
                 t_collect(2 * s)
                 t_collect(2 * s + 1)
-                pl.when(s == nz - 2)(t_complete)
+
+                @pl.when(s == nz - 2)
+                def _():
+                    t_complete()
+                    saves[0].wait()
+                    temporal_early()
 
             @pl.when(s < nz - 1)
             def _():
@@ -394,7 +623,7 @@
     for step in range(1, cams):
         other = (cam + step) % cams
         feat_copy(other, other).wait_recv()
-    arr_ref[...] = arr_s[...]
+    temporal_rest()
     for step in range(1, cams):
         feat_copy((cam + step) % cams, cam).wait_send()
 
@@ -420,7 +649,7 @@
             return carry
 
         lax.fori_loop(0, CH // BLK, saved, 0)
-    for save in saves:
+    for save in saves[1:]:
         save.wait()
     last.wait()
 
@@ -445,15 +674,18 @@
         return carry
 
     lax.fori_loop(0, nz, t_drain, 0)
-    t_save().wait()
+    for p in range(9):
+        x_save(p).wait()
+    for step in range(1, cams):
+        view_copy((cam + step) % cams, cam).wait_send()
 
 
 def enc_bwd_kernel(
-    n, cams, cond, x_hbm, a_hbm, w_hbm, z1_hbm, r1_ref, z2_hbm, r2_ref, aff_ref, dviews_ref, dt_hbm,
+    n, cams, cond, x_hbm, a_hbm, w_hbm, z1_hbm, r1_ref, z2_hbm, r2_ref, aff_ref, gp_ref, dt_hbm,
     ig_ref, genc_ref, gaff_ref, gconvs_ref, gfilm_ref, gskip_ref, gdown_ref, gblk_ref,
-    x_ref, a_ref, w_ref, z1_ref, z2_ref, g_ref, gt_ref, ag_ref, gp_ref,
+    x_ref, a_ref, w_ref, z1_ref, z2_ref, g_ref, gt_ref, ag_ref,
     dwf, core_out, core_in, slots, t_own, t_sum, t_peer, t_slots, t_all,
-    lsem, csend, crecv, zsend, zrecv, fsend, frecv,
+    lsem, csend, crecv, zsend, zrecv,
     tlsem, tcsend, tcrecv, tpsend, tprecv, tzsend, tzrecv, tfsend, tfrecv,
 ):
     nz = n // 2
@@ -474,10 +706,7 @@
         "z1": pltpu.make_async_copy(z1_hbm, z1_ref, lsem.at[1]),
         "a": pltpu.make_async_copy(a_hbm, a_ref, lsem.at[2]),
     }
-    x_loads = [
-        pltpu.make_async_copy(x_hbm.at[:, p * CH : (p + 1) * CH], x_ref.at[p], lsem.at[4 + p])
-        for p in range(9)
-    ]
+    x_loads = [pltpu.make_async_copy(x_hbm, x_ref, lsem.at[4])]
     loads["z2"].start()
     for load in x_loads:
         load.start()
@@ -490,13 +719,7 @@
 
     own_load(0).start()
 
-    line_barrier(cams, nz)
-
-    def view_copy(to, sender):
-        return cam_copy(dviews_ref.at[to], gp_ref.at[:, sender], fsend.at[to], frecv.at[sender], to)
-
-    for step in range(1, cams):
-        view_copy((cam + step) % cams, cam).start()
+    line_greet(cams, nz)
 
     def t_core(k):
         return batch_copy(dt_hbm.at[k, 1 - core], t_sum.at[k], tcsend.at[k], tcrecv.at[k], partner)
@@ -508,8 +731,6 @@
     def t_start(k, carry):
         t_core(k).start()
         return carry
-
-    lax.fori_loop(0, nz, t_start, 0)
 
     def t_spread(lo, hi):
         def body(k, carry):
@@ -533,11 +754,7 @@
 
         lax.fori_loop(lo, hi, body, 0)
 
-    gp_ref[:, cam] = dviews_ref[cam]
     ag_ref[...] = jnp.zeros_like(ag_ref)
-    for step in range(1, cams):
-        other = (cam + step) % cams
-        view_copy(other, other).wait_recv()
     for load in x_loads:
         load.wait()
     loads["z2"].wait()
@@ -790,7 +1007,10 @@
                 load_w(0).wait()
             ig_ref[q] = ig_ref[q] + input_back(q)
 
-    lax.fori_loop(0, CH // BLK, second, 0)
+    lax.fori_loop(0, 1, second, 0)
+    line_wait(cams, nz)
+    lax.fori_loop(0, nz, t_start, 0)
+    lax.fori_loop(1, CH // BLK, second, 0)
     loads["a"].wait()
     make_chunk(0)
     service(0)
@@ -855,174 +1075,6 @@
         t_final((cam + step) % cams, cam).wait_send()
     core_copy(4).wait_send()
     core_copy(5).wait_send()
-    for step in range(1, cams):
-        view_copy((cam + step) % cams, cam).wait_send()
-
-
-def temporal_kernel(
-    traj_ref, og_ref, arr_ref, mask_ref, emb_ref, t_ref,
-    out_ref, tg_ref, dviews_ref, dt_ref,
-    pad_t, pad_m, pad_h, za_ref, zb_ref, sum_ref, aff_ref, ag_ref,
-):
-    nz, rows_t = t_ref.shape[0], t_ref.shape[3]
-    cond = arr_ref.shape[1] * CH + emb_ref.shape[1]
-
-    class Part:
-        def __init__(self, ref, q, lo, wide):
-            self.ref, self.q, self.lo, self.wide = ref, q, lo, wide
-
-        def cols(self, key):
-            if not isinstance(key, tuple):
-                return slice(self.lo, self.lo + self.wide)
-            start, stop, _ = key[1].indices(self.wide)
-            return slice(self.lo + start, self.lo + stop)
-
-        def __getitem__(self, key):
-            v = self.ref[:, :, self.q, :, self.cols(key)]
-            return v.reshape(2 * nz * rows_t, v.shape[-1])
-
-        def __setitem__(self, key, v):
-            self.ref[:, :, self.q, :, self.cols(key)] = v.reshape(nz, 2, rows_t, v.shape[-1])
-
-    places = ((0, 0, PART), (1, 0, PART), (2, 0, cond), (2, cond, cond), (3, 0, CH), (3, CH, 3 * CH), (2, 2 * cond, BLK))
-    wa_ref, wb_ref, f0_ref, f1_ref, ws_ref, wd_ref, ext_ref = [Part(t_ref, *place) for place in places]
-    dwa_ref, dwb_ref, df0_ref, df1_ref, dws_ref, dwd_ref, dext_ref = [Part(dt_ref, *place) for place in places]
-    for q, lo in ((2, 2 * cond + BLK), (3, 4 * CH)):
-        dt_ref[:, :, q, :, lo:] = jnp.zeros((nz, 2, rows_t, PART - lo), bf16)
-    aff_ref[...] = jnp.transpose(ext_ref[...].astype(f32))
-    ag_ref[...] = jnp.zeros_like(ag_ref)
-    ns = mask_ref.shape[0]
-    rows = traj_ref.shape[0]
-    nf = rows // ns
-    edge = 2 * ns
-    ones = group_ones(CH, CH // GROUPS)
-    inv_n = 1.0 / (nf * (CH // GROUPS))
-    aff = lambda i: aff_ref[4 + i : 5 + i, :]
-
-    def frames(v):
-        return v.reshape(nf, ns, CH)
-
-    def fill(pad_ref, v):
-        pad_ref[0:edge, :] = jnp.zeros((edge, CH), bf16)
-        pad_ref[edge : edge + rows, :] = v
-        pad_ref[edge + rows : edge + rows + edge, :] = jnp.zeros((edge, CH), bf16)
-
-    def conv5(pad_ref, w_ref):
-        acc = None
-        for t in range(5):
-            part = dot(pad_ref[t * ns : t * ns + rows, :], w_ref[:, t * CH : (t + 1) * CH], NT)
-            acc = part if acc is None else acc + part
-        return acc
-
-    def conv5_back(pad_ref, w_ref):
-        acc = None
-        for t in range(5):
-            part = dot(pad_ref[(4 - t) * ns : (4 - t) * ns + rows, :], w_ref[:, t * CH : (t + 1) * CH])
-            acc = part if acc is None else acc + part
-        return acc
-
-    def norm(v):
-        v = frames(v)
-        mean = group_sum(jnp.sum(v, axis=0), ones) * inv_n
-        centred = v - mean[None]
-        rstd = lax.rsqrt(group_sum(jnp.sum(centred * centred, axis=0), ones) * inv_n + norm_eps)
-        return centred * rstd[None], rstd
-
-    def norm_back(du, z, rstd, gain):
-        s0 = jnp.sum(du, axis=0)
-        s1 = jnp.sum(du * z, axis=0)
-        m0 = group_sum(s0 * gain, ones) * inv_n
-        m1 = group_sum(s1 * gain, ones) * inv_n
-        dv = (du * gain[None] - m0[None] - z * m1[None]) * rstd[None]
-        return dv, jnp.sum(s1, axis=0, keepdims=True), jnp.sum(s0, axis=0, keepdims=True)
-
-    mask = mask_ref[...]
-    count = jnp.sum(mask, axis=1, keepdims=True)
-    cams = arr_ref.shape[0]
-    obs = arr_ref.shape[1]
-    conds, slopes = [], []
-    for o in range(obs):
-        pooled = None
-        for cam in range(cams):
-            part = mask[:, cam : cam + 1] * arr_ref[cam, o].astype(f32)
-            pooled = part if pooled is None else pooled + part
-        value, slope = mish_pair(pooled / count)
-        conds.append(value.astype(bf16))
-        slopes.append(slope)
-    conds.append(mish_value(emb_ref[...]).astype(bf16))
-    lanes = [slice(o * CH, (o + 1) * CH) for o in range(obs)] + [slice(obs * CH, cond)]
-    film = []
-    for i, w_ref in ((6, f0_ref), (7, f1_ref)):
-        film.append(sum(dot(v, w_ref[:, cols], NT) for v, cols in zip(conds, lanes)) + aff(i))
-    scale, shift = film
-
-    fill(pad_t, traj_ref[...])
-    za, rstd_a = norm(conv5(pad_t, wa_ref) + aff(4))
-    za_ref[...] = za.reshape(rows, CH)
-    act_a = mish_value(za * aff(0)[None] + aff(1)[None])
-    fill(pad_m, (act_a * scale[None] + shift[None]).astype(bf16).reshape(rows, CH))
-    zb, rstd_b = norm(conv5(pad_m, wb_ref) + aff(5))
-    zb_ref[...] = zb.reshape(rows, CH)
-    skip = frames(dot(traj_ref[...], ws_ref[...], NT)) + aff(8)[None]
-    summed = (mish_value(zb * aff(2)[None] + aff(3)[None]) + skip).astype(bf16)
-    pairs = summed.reshape(nf // 2, 2, ns, CH)
-    half = rows // 2
-    sum_ref[0:ns, :] = jnp.zeros((ns, CH), bf16)
-    sum_ref[ns : ns + half, :] = pairs[:, 1].reshape(half, CH)
-    sum_ref[ns + half : ns + 2 * half, :] = pairs[:, 0].reshape(half, CH)
-    taps = (0, ns + half, ns)
-    out = None
-    og = og_ref[...]
-    dcols = []
-    for t in range(3):
-        cols = sum_ref[taps[t] : taps[t] + half, :]
-        w = wd_ref[:, t * CH : (t + 1) * CH]
-        part = dot(cols, w, NT)
-        out = part if out is None else out + part
-        dcols.append(dot(og, w).reshape(nf // 2, ns, CH))
-        dwd_ref[:, t * CH : (t + 1) * CH] = dot(og, cols, TN).astype(bf16)
-    out_ref[...] = (out + aff(9)).astype(bf16)
-    ag_ref[9:10, :] = jnp.sum(og.astype(f32), axis=0, keepdims=True)
-
-    before = jnp.concatenate([dcols[0][1:], jnp.zeros((1, ns, CH), f32)], axis=0)
-    dsum = jnp.stack([dcols[1], dcols[2] + before], axis=1).reshape(nf, ns, CH)
-    ag_ref[8:9, :] = jnp.sum(dsum, axis=(0, 1)).reshape(1, CH)
-    dskip = dsum.astype(bf16).reshape(rows, CH)
-    dws_ref[...] = dot(dskip, traj_ref[...], TN).astype(bf16)
-    tg_ref[...] = dot(dskip, ws_ref[...])
-    zb = frames(zb_ref[...])
-    _, slope = mish_pair(zb * aff(2)[None] + aff(3)[None])
-    dhb, ag_ref[2:3, :], ag_ref[3:4, :] = norm_back(dsum * slope, zb, rstd_b, aff(2))
-    ag_ref[5:6, :] = jnp.sum(dhb, axis=(0, 1)).reshape(1, CH)
-    fill(pad_h, dhb.astype(bf16).reshape(rows, CH))
-    hb = pad_h[edge : edge + rows, :]
-    for t in range(5):
-        dwb_ref[:, t * CH : (t + 1) * CH] = dot(hb, pad_m[t * ns : t * ns + rows, :], TN).astype(bf16)
-    dmid = frames(conv5_back(pad_h, wb_ref))
-    za = frames(za_ref[...])
-    act_a, slope = mish_pair(za * aff(0)[None] + aff(1)[None])
-    dscale = jnp.sum(dmid * act_a, axis=0)
-    dshift = jnp.sum(dmid, axis=0)
-    dha, ag_ref[0:1, :], ag_ref[1:2, :] = norm_back(dmid * scale[None] * slope, za, rstd_a, aff(0))
-    ag_ref[4:5, :] = jnp.sum(dha, axis=(0, 1)).reshape(1, CH)
-    ag_ref[6:7, :] = jnp.sum(dscale, axis=0, keepdims=True)
-    ag_ref[7:8, :] = jnp.sum(dshift, axis=0, keepdims=True)
-    fill(pad_h, dha.astype(bf16).reshape(rows, CH))
-    ha = pad_h[edge : edge + rows, :]
-    for t in range(5):
-        dwa_ref[:, t * CH : (t + 1) * CH] = dot(ha, pad_t[t * ns : t * ns + rows, :], TN).astype(bf16)
-    tg_ref[...] = tg_ref[...] + conv5_back(pad_h, wa_ref)
-
-    lows = (dscale.astype(bf16), dshift.astype(bf16))
-    for low, dw_ref in zip(lows, (df0_ref, df1_ref)):
-        for v, cols in zip(conds, lanes):
-            dw_ref[:, cols] = dot(low, v, TN).astype(bf16)
-    for o in range(obs):
-        dcond = dot(lows[0], f0_ref[:, lanes[o]]) + dot(lows[1], f1_ref[:, lanes[o]])
-        dview = dcond * slopes[o] / count
-        for cam in range(cams):
-            dviews_ref[cam, o] = (mask[:, cam : cam + 1] * dview).astype(bf16)
-    dext_ref[...] = jnp.transpose(ag_ref[...]).astype(bf16)
 
 
 def call(kernel, outs, in_specs, out_specs, scratch=(), collective_id=None, cost=None):
@@ -1124,43 +1176,36 @@
     wide = 9 * ch
     rows = nf * ns
 
-    ext = jnp.concatenate([encoder_affine[0], block_affine], axis=1)
-    ext = jnp.pad(ext, ((0, 0), (0, BLK - ext.shape[1]))).astype(bf16)
-    x = jnp.transpose(images[0], (2, 0, 1, 3, 4)).reshape(n_img, wide)
+    def turned(v):
+        return jnp.transpose(v.reshape(v.shape[-2:]))
+
+    pairs = jnp.transpose(images[0], (0, 1, 3, 2, 4)).reshape(n_img // obs, 9, obs, ch)
     pos = (9, n_img, ch)
     t_shape = (nz, 2, cams, per, PART)
-    z1, r1, act, z2, r2, arrived, w_all, enc_aff, all_t = call(
-        functools.partial(enc_fwd_kernel, n, cams),
-        [(pos, f32), ((n_img, ch), f32), (pos, bf16), (pos, f32), ((n_img, ch), f32),
-         ((cams, obs, ns, ch), bf16), ((2, n, per, wide + BLK), bf16), ((8, ch), f32), (t_shape, bf16)],
-        [V, H, V, V, V, V, V],
-        [H, V, H, H, V, V, H, V, H],
-        [pltpu.VMEM((2, n, per, wide + BLK), bf16), pltpu.VMEM(pos, f32), pltpu.VMEM((n_img, wide), bf16),
-         pltpu.VMEM(pos, f32), pltpu.VMEM((obs, cams, ns, ch), bf16), pltpu.VMEM((cams, obs, ns, ch), bf16),
-         pltpu.VMEM(t_shape, bf16), pltpu.VMEM((2, min(per, 16), 2, wide), f32),
+    wcols = wide + BLK
+    z1, r1, act, z2, r2, w_all, enc_aff, x, out_fm, tg_fm, gp, dt = call(
+        functools.partial(forward_kernel, n, cams),
+        [(pos, f32), ((n_img, ch), f32), (pos, bf16), (pos, f32), ((n_img, ch), f32), ((2, n, per, wcols), bf16),
+         ((8, ch), f32), (pos, bf16), ((rows // 2, ch), bf16), ((rows, ch), f32), ((obs, cams, ns, ch), bf16),
+         (t_shape, bf16)],
+        [V, V, V, V, V, H, V, V, V, V, V, V],
+        [H, V, H, H, V, H, V, H, V, V, V, H],
+        [pltpu.VMEM((n_img, wide), bf16), pltpu.VMEM((2, n, per, wcols), bf16), pltpu.VMEM(pos, f32),
+         pltpu.VMEM((n_img, wide), bf16), pltpu.VMEM(pos, f32), pltpu.VMEM((obs, cams, ns, ch), bf16),
+         pltpu.VMEM((cams, obs, ns, ch), bf16), pltpu.VMEM(t_shape, bf16), pltpu.VMEM((2, min(per, 16), 2, wide), f32),
+         pltpu.VMEM((BLK, per), f32), pltpu.VMEM((rows // 2, ch), bf16), pltpu.VMEM((rows + 4 * ns, ch), bf16),
+         pltpu.VMEM((rows + 4 * ns, ch), bf16), pltpu.VMEM((rows + 4 * ns, ch), bf16), pltpu.VMEM((rows + ns, ch), bf16),
+         pltpu.VMEM((BLK, ch), f32), pltpu.VMEM((BLK, ch), f32), pltpu.VMEM((ns, ch), f32),
+         pltpu.VMEM((cams, obs, ns, ch), bf16), pltpu.VMEM((obs, cams, ns, ch), bf16),
+         pltpu.VMEM((2, nz, 2, per, PART), bf16),
          DMA((2, 2, nz)), DMA((2, nz)), DMA((2, nz)), DMA((2, nz)), DMA((2, ch // BLK)), DMA((11,)),
          DMA((cams,)), DMA((cams,)),
          DMA((2, nz)), DMA((nz,)), DMA((nz, cams)), DMA((nz, cams)), DMA((cams - 1, nz)), DMA((cams - 1, nz)),
-         DMA(()), DMA((max(per // 16, 1),))],
+         DMA((max(per // 16, 1),)), DMA((9,)), DMA((cams,)), DMA((cams,)), DMA((4,))],
         collective_id=0,
-        cost=work(90),
-    )(x, encoder_weight[0], block_convs, film_weight, skip_weight, down_weight, ext)
-
-    present = view_mask.astype(f32)
-    embedded = time_embed(timesteps, TEMB)
-    traj_fm = jnp.transpose(trajectory, (1, 0, 2)).reshape(rows, ch)
-    og_fm = jnp.transpose(out_grad, (1, 0, 2)).reshape(rows // 2, ch)
-    out_fm, tg_fm, dviews, dt = call(
-        temporal_kernel,
-        [((rows // 2, ch), bf16), ((rows, ch), f32), ((cams, obs, ns, ch), bf16), (all_t.shape, bf16)],
-        [V] * 6,
-        [V] * 4,
-        [pltpu.VMEM((rows + 4 * ns, ch), bf16)] * 3
-        + [pltpu.VMEM((rows, ch), f32)] * 2
-        + [pltpu.VMEM((rows + ns, ch), bf16)]
-        + [pltpu.VMEM((BLK, ch), f32)] * 2,
-        cost=work(20),
-    )(traj_fm, og_fm, arrived, present, embedded, all_t)
+        cost=work(130),
+    )(pairs, trajectory, out_grad, view_mask.astype(f32), time_embed(timesteps, TEMB), encoder_weight[0], block_convs,
+      film_weight, skip_weight, down_weight, turned(encoder_affine), turned(block_affine))
     block_output = jnp.transpose(out_fm.reshape(nf // 2, ns, ch), (1, 0, 2))
     trajectory_grad = jnp.transpose(tg_fm.reshape(nf, ns, ch), (1, 0, 2))
 
@@ -1173,22 +1218,19 @@
         [V] * 8,
         [pltpu.VMEM(pos, bf16), pltpu.VMEM(pos, bf16), pltpu.VMEM((n, per, wide), bf16), pltpu.VMEM(pos, f32),
          pltpu.VMEM(pos, f32), pltpu.VMEM(pos, bf16), pltpu.VMEM((ch, 9 * n_img), bf16),
-         pltpu.VMEM((BLK, ch), f32), pltpu.VMEM((obs, cams, ns, ch), bf16),
+         pltpu.VMEM((BLK, ch), f32),
          pltpu.VMEM((2, nz, per, chunk), f32), pltpu.VMEM((2, nz, per, chunk), bf16),
          pltpu.VMEM((3, nz, per, chunk), bf16), pltpu.VMEM((3, 2, nz, per, chunk), bf16),
          pltpu.VMEM((2, per, PART), bf16), pltpu.VMEM((nz, cams, per, PART), bf16),
          pltpu.VMEM((cams - 1, nz, per, PART), bf16), pltpu.VMEM((2, nz, per, PART), bf16),
          pltpu.VMEM((cams, per, PART), bf16),
-         DMA((13,)), DMA((6,)), DMA((6,)), DMA((6, 2, nz)), DMA((6, 2, nz)), DMA((cams,)), DMA((cams,)),
+         DMA((13,)), DMA((6,)), DMA((6,)), DMA((6, 2, nz)), DMA((6, 2, nz)),
          DMA((nz * cams,)), DMA((nz,)), DMA((nz,)), DMA((cams - 1, nz)), DMA((cams - 1, nz)),
          DMA((2, nz)), DMA((2, nz)), DMA((cams,)), DMA((cams,))],
         collective_id=1,
         cost=work(100),
-    )(x, act, w_all, z1, r1, z2, r2, enc_aff, dviews, dt)
+    )(x, act, w_all, z1, r1, z2, r2, enc_aff, gp, dt)
     images_grad = jnp.transpose(ig.reshape((9, obs) + images.shape[1:3] + (ch,)), (2, 3, 1, 0, 4))[None]
-
-    def turned(v):
-        return jnp.transpose(v.reshape(v.shape[-2:]))
 
     weights = (encoder_weight, encoder_affine, block_convs, film_weight, skip_weight, down_weight, block_affine)
     firsts = (first_encoder, first_affine, first_convs, first_film, first_skip, first_down, first_block)

time: 334 us -> 318 us (0.952)
  local copies, waits for them, and re-layouts: 22.4 us -> 13.5 us
  Pallas kernels: 302 us -> 296 us
    transpose x3 -> x0, local copies, waits for them, and re-layouts: 6.42 us -> none  [the longest x1 2.56 us: shards(): x = jnp.transpose(images[0], (2, 0, 1, 3, 4)).reshape(n_img, wide)]
    pallas_call x1, Pallas kernels: 140 us -> 135 us  [shards(): call(functools.partial(enc_bwd_kernel, n, cams, cond), [(pos, f32), ((per...]
    unnamed x5 -> x0, local copies, waits for them, and re-layouts: 3.85 us -> none
    pallas_call x2 -> x1, Pallas kernels: 148 us -> 146 us  [shards(): call(functools.partial(forward_kernel, n, cams), [(pos, f32), ((n_img, ch...]
where the time goes in v6:
time: 318 us; the launch traced here: 312 us
  Pallas kernels  296 us (93%)
  local copies, waits for them, and re-layouts  13.5 us (4%)
    pallas_call x1, Pallas kernels, shards(): call(functools.partial(forward_kernel, n, cams), [(pos, f32), ((n_img, ch...  146 us
    pallas_call x1, Pallas kernels, shards(): call(functools.partial(enc_bwd_kernel, n, cams, cond), [(pos, f32), ((per...  135 us
    pallas_call x1, Pallas kernels, adam_call(): pl.pallas_call(adam_kernel, grid=(rows // step,), out_shape=[jax.ShapeDty...  14.5 us
    reshape x1, local copies, waits for them, and re-layouts, shards(): ig.reshape((9, obs) + images.shape[1:3] + (ch,))  8.16 us

profile of v6, /device:TPU:0, one launch (start us, length us, event | category | flops | bytes accessed | tf_op | source)
XLA Modules:
  0.0 312.4 jit_solution(17250223597046459907)
XLA Ops:
  0.7 0.7 convert_element_type.7
  1.3 0.7 convert_element_type.6
  2.0 0.7 copy.54.mask_ref
  2.7 0.1 multiply_sine_fusion
  2.9 0.7 pad_maximum_fusion.emb_ref
  3.5 146.1 %shard_map.433 = (f32[9,256,512]{2,1,0:T(8,128)}, f32[256,512]{1,0:T(8,128)}, bf16[9,256,512]{2,1,0:T(8,128)(2,1)}, f32[9,256,512]{2,1,0:T(8,128)}, f32[256,512]...) custom-call(bf16[128,9,2,512]{3,2,1,0:T(2,128)(2,1)} %bitcast.55, ...), custom_call_target="tpu_custom_call" | custom-call | flops 130000003072 | bytes 390000000 | tf_op jit(solution)/shard_map/pallas_call | solution.py:1186
  149.7 1.8 copy.63
  151.5 2.8 copy.62
  154.3 135.2 %shard_map.434 = (f32[9,256,512]{2,1,0:T(8,128)}, f32[64,2,4608]{2,1,0:T(2,128)}, f32[4,64]{1,0:T(4,128)}, f32[64,2,2560]{2,1,0:T(2,128)}, f32[64,2,1152]{2,1,0:...) custom-call(bf16[9,256,512]{2,1,0:T(8,128)(2,1)} %get-tuple-element.67.x_hbm, ...), custom_call_target="tpu_custom_call" | custom-call | flops 99999997952 | bytes 300000000 | tf_op jit(solution)/shard_map/pallas_call | solution.py:1213
  289.5 8.2 %copy.61 = f32[9,2,4,32,512]{4,1,0,3,2:T(2,128)} copy(f32[9,2,4,32,512]{4,3,2,1,0:T(8,128)} %bitcast.50) | data formatting | bytes 9437184 | tf_op jit(solution)/shard_map/reshape | solution.py:1233
  297.7 14.5 %shard_map.435 = (f32[64,2,4608]{2,1,0:T(2,128)}, f32[64,2,4608]{2,1,0:T(2,128)}, f32[64,2,4608]{2,1,0:T(2,128)}, f32[4,64]{1,0:T(4,128)}, f32[4,64]{1,0:T(4,128...) custom-call(f32[64,2,4608]{2,1,0:T(2,128)} %bitcast.57, ...), custom_call_target="tpu_custom_call" | custom-call | flops 12000000000 | bytes 36000000 | tf_op jit(solution)/shard_map/pallas_call | solution.py:1154
  (1 shorter events, 0.0 us)

commit v7 on v6

--- a/solution.py
+++ b/solution.py
@@ -298,6 +298,9 @@
     def total(v):
         return jnp.sum(v, axis=(0, 1)).reshape(1, CH)
 
+    def across(v):
+        return jnp.transpose(v.reshape(frows, CH)).astype(bf16)
+
     def temporal_early():
         taff_ref[...] = jnp.transpose(wext[...].astype(f32))
         ag_ref[...] = jnp.zeros_like(ag_ref)
@@ -314,7 +317,7 @@
         ag_ref[8:9, :] = total(dsum)
         ag_ref[9:10, :] = jnp.sum(og.astype(f32), axis=0, keepdims=True)
         dskip = dsum.astype(bf16).reshape(frows, CH)
-        grad(0, 0, CH)[...] = dot(dskip, traj, TN).astype(bf16)
+        grad(0, 0, CH)[...] = dot(across(dsum), traj).astype(bf16)
         blank(0, 4 * CH)
         tg_ref[...] = dot(dskip, ws[...])
 
@@ -363,23 +366,23 @@
         ag_ref[6:7, :] = jnp.sum(dscale, axis=0, keepdims=True)
         ag_ref[7:8, :] = jnp.sum(dshift, axis=0, keepdims=True)
         dwb = grad(1, 0, PART)
-        hb = pad_h[edge : edge + frows, :]
+        hb = across(dhb)
         for t in range(5):
-            dwb[:, t * CH : (t + 1) * CH] = dot(hb, pad_m[t * ns : t * ns + frows, :], TN).astype(bf16)
+            dwb[:, t * CH : (t + 1) * CH] = dot(hb, pad_m[t * ns : t * ns + frows, :]).astype(bf16)
         dt_save(1, 1).start()
         pairs = kept(3).astype(bf16).reshape(nf // 2, 2, ns, CH)
         half = frows // 2
         sum_ref[0:ns, :] = jnp.zeros((ns, CH), bf16)
         sum_ref[ns : ns + half, :] = pairs[:, 1].reshape(half, CH)
         sum_ref[ns + half : ns + 2 * half, :] = pairs[:, 0].reshape(half, CH)
-        og = og_ref[...]
+        og = jnp.transpose(og_ref[...].astype(f32)).astype(bf16)
         dwd = grad(0, CH, 3 * CH)
         out = None
         for t, at in enumerate((0, ns + half, ns)):
             cols = sum_ref[at : at + half, :]
             part = dot(cols, wd[:, t * CH : (t + 1) * CH], NT)
             out = part if out is None else out + part
-            dwd[:, t * CH : (t + 1) * CH] = dot(og, cols, TN).astype(bf16)
+            dwd[:, t * CH : (t + 1) * CH] = dot(og, cols).astype(bf16)
         dt_save(3, 0).start()
         out_ref[...] = (out + tail(9)).astype(bf16)
         fill(pad_h, dha)
@@ -394,9 +397,9 @@
         dt_save(2, 1).start()
         dt_save(3, 0).wait()
         dwa = grad(0, 0, PART)
-        ha = pad_h[edge : edge + frows, :]
+        ha = across(dha)
         for t in range(5):
-            dwa[:, t * CH : (t + 1) * CH] = dot(ha, pad_t[t * ns : t * ns + frows, :], TN).astype(bf16)
+            dwa[:, t * CH : (t + 1) * CH] = dot(ha, pad_t[t * ns : t * ns + frows, :]).astype(bf16)
         dt_save(0, 0).start()
         for step in range(1, cams):
             other = (cam + step) % cams
@@ -1113,18 +1116,32 @@
 def adamw(weight, gradient, moment_one, moment_two, step_rate, weight_decay):
     mean_new = beta_first * moment_one + (1.0 - beta_first) * gradient
     square_new = beta_second * moment_two + (1.0 - beta_second) * gradient * gradient
-    mean_hat = mean_new / (1.0 - beta_first**STEP)
-    square_hat = square_new / (1.0 - beta_second**STEP)
-    weight_new = weight - step_rate * (
-        mean_hat / (jnp.sqrt(square_hat) + adam_eps) + weight_decay * weight
+    square_hat = square_new * (1.0 / (1.0 - beta_second**STEP))
+    root = square_hat * lax.rsqrt(square_hat)
+    weight_new = (1.0 - step_rate * weight_decay) * weight - (step_rate / (1.0 - beta_first**STEP)) * (
+        mean_new / (root + adam_eps)
     )
     return (weight_new, mean_new, square_new)
 
 
-def adam_kernel(*refs):
+def last_kernel(*refs):
+    tg_ref, out_ref, ig_ref = refs[28:31]
+    tg_new, out_new, ig_new, turn_ref = refs[52:56]
+    for p in range(ig_ref.shape[0]):
+        for o in range(ig_ref.shape[1]):
+            ig_new[:, p, o, :] = ig_ref[p, o]
+
+    @pl.when(pl.program_id(0) == 0)
+    def _():
+        for f in range(tg_ref.shape[0]):
+            tg_new[:, f, :] = tg_ref[f]
+        for u in range(out_ref.shape[0]):
+            turn_ref[:, u, :] = out_ref[u].astype(f32)
+        out_new[...] = turn_ref[...].astype(bf16)
+
     for i in range(7):
         w_ref, m_ref, v_ref, g_ref = refs[4 * i : 4 * i + 4]
-        outs = refs[28 + 3 * i : 31 + 3 * i]
+        outs = refs[31 + 3 * i : 34 + 3 * i]
 
         def update():
             vector = i in (1, 6)
@@ -1139,27 +1156,39 @@
             update()
 
 
-def adam_call(shown, grads, rows):
+def last_call(shown, grads, tg, out, ig, rows):
     step = min(rows, 8)
+    steps = rows // step
+
+    def whole(shape):
+        return pl.BlockSpec(shape, lambda r: (0,) * len(shape))
 
     def spec(v):
         if v.shape[0] != rows:
-            return pl.BlockSpec(v.shape, lambda r: (0, 0))
+            return whole(v.shape)
         return pl.BlockSpec((step,) + v.shape[1:], lambda r: (r,) + (0,) * (v.ndim - 1))
 
     ins = []
     for i in range(7):
         ins += [shown[0][i], shown[1][i], shown[2][i], grads[i]]
     outs = [w for w in shown[0] for _ in range(3)]
+    pos, obs, count, ch = ig.shape
+    part = count // steps
+    turned = [(v.shape[1], v.shape[0], v.shape[2]) for v in (tg, out)]
     return pl.pallas_call(
-        adam_kernel,
-        grid=(rows // step,),
-        out_shape=[jax.ShapeDtypeStruct(v.shape, f32) for v in outs],
-        in_specs=[spec(v) for v in ins],
-        out_specs=[spec(v) for v in outs],
+        last_kernel,
+        grid=(steps,),
+        out_shape=[jax.ShapeDtypeStruct(v.shape, f32) for v in outs]
+        + [jax.ShapeDtypeStruct(turned[0], f32), jax.ShapeDtypeStruct(turned[1], bf16),
+           jax.ShapeDtypeStruct((count, pos, obs, ch), f32)],
+        in_specs=[spec(v) for v in ins]
+        + [whole(tg.shape), whole(out.shape), pl.BlockSpec((pos, obs, part, ch), lambda r: (0, 0, r, 0))],
+        out_specs=[spec(v) for v in outs]
+        + [whole(turned[0]), whole(turned[1]), pl.BlockSpec((part, pos, obs, ch), lambda r: (r, 0, 0, 0))],
+        scratch_shapes=[pltpu.VMEM(turned[1], f32)],
         compiler_params=pltpu.CompilerParams(vmem_limit_bytes=VMEM_BYTES),
-        cost_estimate=work(12),
-    )(*ins)
+        cost_estimate=work(15),
+    )(*ins, tg, out, ig)
 
 
 def shards(
@@ -1206,9 +1235,6 @@
         cost=work(130),
     )(pairs, trajectory, out_grad, view_mask.astype(f32), time_embed(timesteps, TEMB), encoder_weight[0], block_convs,
       film_weight, skip_weight, down_weight, turned(encoder_affine), turned(block_affine))
-    block_output = jnp.transpose(out_fm.reshape(nf // 2, ns, ch), (1, 0, 2))
-    trajectory_grad = jnp.transpose(tg_fm.reshape(nf, ns, ch), (1, 0, 2))
-
     chunk = 3 * ch + BLK
     ig, genc, gaff, gconvs, gfilm, gskip, gdown, gblk = call(
         functools.partial(enc_bwd_kernel, n, cams, cond),
@@ -1230,8 +1256,6 @@
         collective_id=1,
         cost=work(100),
     )(x, act, w_all, z1, r1, z2, r2, enc_aff, gp, dt)
-    images_grad = jnp.transpose(ig.reshape((9, obs) + images.shape[1:3] + (ch,)), (2, 3, 1, 0, 4))[None]
-
     weights = (encoder_weight, encoder_affine, block_convs, film_weight, skip_weight, down_weight, block_affine)
     firsts = (first_encoder, first_affine, first_convs, first_film, first_skip, first_down, first_block)
     seconds = (second_encoder, second_affine, second_convs, second_film, second_skip, second_down, second_block)
@@ -1239,7 +1263,11 @@
         [turned(v) if i in (1, 6) else v.reshape(v.shape[-3:]) if i == 0 else v for i, v in enumerate(group)]
         for group in (weights, firsts, seconds)
     ]
-    news = adam_call(shown, (genc, gaff, gconvs, gfilm, gskip, gdown, gblk), per)
+    *news, trajectory_grad, block_output, ig_new = last_call(
+        shown, (genc, gaff, gconvs, gfilm, gskip, gdown, gblk),
+        tg_fm.reshape(nf, ns, ch), out_fm.reshape(nf // 2, ns, ch), ig.reshape(9, obs, n_img // obs, ch), per,
+    )
+    images_grad = jnp.transpose(ig_new.reshape(images.shape[1:3] + ig_new.shape[1:]), (0, 1, 3, 2, 4))[None]
     upd = [
         tuple((turned(v) if i in (1, 6) else v).reshape(w.shape) for v in news[3 * i : 3 * i + 3])
         for i, w in enumerate(weights)

time: 318 us -> 308 us (0.969)
  local copies, waits for them, and re-layouts: 13.5 us -> 0.69 us
  Pallas kernels: 296 us -> 300 us
    reshape x3 -> x0, local copies, waits for them, and re-layouts: 12.8 us -> none  [the longest x1 8.16 us: shards(): ig.reshape((9, obs) + images.shape[1:3] + (ch,))]
    pallas_call x1, Pallas kernels: 14.5 us -> 18.2 us  [last_call(): pl.pallas_call(last_kernel, grid=(steps,), out_shape=[jax.ShapeDtypeStruc...]
where the time goes in v7:
time: 308 us; the launch traced here: 304 us
  Pallas kernels  300 us (97%)
    pallas_call x1, Pallas kernels, shards(): call(functools.partial(forward_kernel, n, cams), [(pos, f32), ((n_img, ch...  146 us
    pallas_call x1, Pallas kernels, shards(): call(functools.partial(enc_bwd_kernel, n, cams, cond), [(pos, f32), ((per...  136 us
    pallas_call x1, Pallas kernels, last_call(): pl.pallas_call(last_kernel, grid=(steps,), out_shape=[jax.ShapeDtypeStruc...  18.2 us

profile of v7, /device:TPU:0, one launch (start us, length us, event | category | flops | bytes accessed | tf_op | source)
XLA Modules:
  0.0 303.8 jit_solution(9841156789912103745)
XLA Ops:
  0.7 0.7 convert_element_type.7
  1.3 0.7 convert_element_type.6
  2.0 0.7 copy.51.mask_ref
  2.7 0.1 multiply_sine_fusion
  2.9 0.7 pad_maximum_fusion.emb_ref
  3.5 146.0 %shard_map.433 = (f32[9,256,512]{2,1,0:T(8,128)}, f32[256,512]{1,0:T(8,128)}, bf16[9,256,512]{2,1,0:T(8,128)(2,1)}, f32[9,256,512]{2,1,0:T(8,128)}, f32[256,512]...) custom-call(bf16[128,9,2,512]{3,2,1,0:T(2,128)(2,1)} %bitcast.43, ...), custom_call_target="tpu_custom_call" | custom-call | flops 130000003072 | bytes 390000000 | tf_op jit(solution)/shard_map/pallas_call | solution.py:1215
  149.5 135.6 %shard_map.434 = (f32[9,256,512]{2,1,0:T(8,128)}, f32[64,2,4608]{2,1,0:T(2,128)}, f32[4,64]{1,0:T(4,128)}, f32[64,2,2560]{2,1,0:T(2,128)}, f32[64,2,1152]{2,1,0:...) custom-call(bf16[9,256,512]{2,1,0:T(8,128)(2,1)} %get-tuple-element.68.x_hbm, ...), custom_call_target="tpu_custom_call" | custom-call | flops 99999997952 | bytes 300000000 | tf_op jit(solution)/shard_map/pallas_call | solution.py:1239
  285.1 18.2 %shard_map.435 = (f32[64,2,4608]{2,1,0:T(2,128)}, f32[64,2,4608]{2,1,0:T(2,128)}, f32[64,2,4608]{2,1,0:T(2,128)}, f32[4,64]{1,0:T(4,128)}, f32[4,64]{1,0:T(4,128...) custom-call(f32[64,2,4608]{2,1,0:T(2,128)} %bitcast.45, ...), custom_call_target="tpu_custom_call" | custom-call | flops 15000000512 | bytes 45000000 | tf_op jit(solution)/shard_map/pallas_call | solution.py:1178
  (1 shorter events, 0.0 us)

commit v8 on v7

--- a/solution.py
+++ b/solution.py
@@ -133,10 +133,10 @@
 
 
 def forward_kernel(
-    n, cams, img_ref, traj_ref, og_in, mask_ref, emb_ref, enc_hbm, convs_ref, film_ref, skip_ref, down_ref,
+    n, cams, img_hbm, traj_ref, og_in, mask_ref, emb_ref, enc_hbm, convs_ref, film_ref, skip_ref, down_ref,
     ea_ref, ba_ref,
     z1_out, r1_ref, a_out, z2_out, r2_ref, w_out, aff_ref, x_out, out_ref, tg_ref, gp_ref, dt_out,
-    x_ref, w_ref, z1_ref, a_ref, z2_ref, feat_ref, arr_s, t_ref, enc_buf,
+    img_ref, x_ref, w_ref, z1_ref, a_ref, z2_ref, feat_ref, arr_s, t_ref, enc_buf,
     ext_s, og_ref, pad_t, pad_m, pad_h, sum_ref, taff_ref, ag_ref, rstd_ref, dviews_ref, gp_s, dt_buf,
     zsend, zrecv, csend, crecv, wsem, osem, fsend, frecv,
     tzsend, tzrecv, tcsend, tcrecv, tpsend, tprecv, esem, xsem, vsend, vrecv, dsem,
@@ -156,6 +156,8 @@
         return pltpu.make_async_copy(enc_hbm.at[pl.ds(i * piece, piece)], enc_buf.at[i % 2], esem.at[i])
 
     enc_load(0).start()
+    img_load = pltpu.make_async_copy(img_hbm, img_ref, xsem.at[9])
+    img_load.start()
     ext_s[...] = jnp.zeros_like(ext_s)
     ext_s[0:4] = ea_ref[...]
     ext_s[4:14] = ba_ref[...]
@@ -468,6 +470,7 @@
     for f in range(nf // 2):
         og_ref[f * ns : (f + 1) * ns, :] = moved[:, f].astype(bf16)
     half = n_img // 2
+    img_load.wait()
     for p in range(9):
         pair = img_ref[:, p].astype(f32)
         for o in range(2):
@@ -685,10 +688,10 @@
 
 def enc_bwd_kernel(
     n, cams, cond, x_hbm, a_hbm, w_hbm, z1_hbm, r1_ref, z2_hbm, r2_ref, aff_ref, gp_ref, dt_hbm,
-    ig_ref, genc_ref, gaff_ref, gconvs_ref, gfilm_ref, gskip_ref, gdown_ref, gblk_ref,
-    x_ref, a_ref, w_ref, z1_ref, z2_ref, g_ref, gt_ref, ag_ref,
+    ig_out, genc_ref, gaff_ref, gconvs_ref, gfilm_ref, gskip_ref, gdown_ref, gblk_ref,
+    ig_ref, x_ref, a_ref, w_ref, z1_ref, z2_ref, g_ref, gt_ref, ag_ref,
     dwf, core_out, core_in, slots, t_own, t_sum, t_peer, t_slots, t_all,
-    lsem, csend, crecv, zsend, zrecv,
+    lsem, bsem, isem, csend, crecv, zsend, zrecv,
     tlsem, tcsend, tcrecv, tpsend, tprecv, tzsend, tzrecv, tfsend, tfrecv,
 ):
     nz = n // 2
@@ -704,18 +707,23 @@
     def load_w(conv):
         return pltpu.make_async_copy(w_hbm.at[conv, :, :, 0 : 9 * CH], w_ref, lsem.at[3])
 
+    def lanes_of(j):
+        return pl.ds(pl.multiple_of(j * BLK, BLK), BLK)
+
+    def block_loads(j):
+        cols = lanes_of(j)
+        return (
+            pltpu.make_async_copy(z2_hbm.at[:, :, cols], z2_ref.at[:, :, cols], bsem.at[0, j]),
+            pltpu.make_async_copy(x_hbm.at[:, :, cols], x_ref.at[:, :, cols], bsem.at[1, j]),
+        )
+
     loads = {
-        "z2": pltpu.make_async_copy(z2_hbm, z2_ref, lsem.at[0]),
         "z1": pltpu.make_async_copy(z1_hbm, z1_ref, lsem.at[1]),
         "a": pltpu.make_async_copy(a_hbm, a_ref, lsem.at[2]),
     }
-    x_loads = [pltpu.make_async_copy(x_hbm, x_ref, lsem.at[4])]
-    loads["z2"].start()
-    for load in x_loads:
-        load.start()
-    loads["a"].start()
-    load_w(1).start()
-    loads["z1"].start()
+    for j in range(CH // BLK):
+        for load in block_loads(j):
+            load.start()
 
     def own_load(i):
         return pltpu.make_async_copy(dt_hbm.at[i // cams, core, i % cams], t_own.at[i % 2], tlsem.at[i])
@@ -758,12 +766,6 @@
         lax.fori_loop(lo, hi, body, 0)
 
     ag_ref[...] = jnp.zeros_like(ag_ref)
-    for load in x_loads:
-        load.wait()
-    loads["z2"].wait()
-
-    def lanes_of(j):
-        return pl.ds(pl.multiple_of(j * BLK, BLK), BLK)
 
     def norm_back(du_ref, z_ref, r_ref, j, gain, row):
         lanes = lanes_of(j)
@@ -785,6 +787,8 @@
 
     def second(j, carry):
         lanes = lanes_of(j)
+        for load in block_loads(j):
+            load.wait()
         gain, offset = aff_ref[2:3, lanes], aff_ref[3:4, lanes]
         pooled = gp_ref[:, :, :, lanes].reshape(n_img, BLK).astype(f32) * (1.0 / 9.0)
         for p in range(9):
@@ -1004,30 +1008,48 @@
             if q == 8:
                 load_w(0).start()
 
+    def ig_save(q):
+        return pltpu.make_async_copy(ig_ref.at[q], ig_out.at[q], isem.at[q])
+
     def back_first(*qs):
         for q in qs:
             if q == 0:
                 load_w(0).wait()
             ig_ref[q] = ig_ref[q] + input_back(q)
+            ig_save(q).start()
+
+    def quarter_of(i):
+        return i * nz // 4, (i + 1) * nz // 4
+
+    def t_go(i):
+        lax.fori_loop(*quarter_of(i), t_start, 0)
 
     lax.fori_loop(0, 1, second, 0)
+    loads["a"].start()
     line_wait(cams, nz)
-    lax.fori_loop(0, nz, t_start, 0)
     lax.fori_loop(1, CH // BLK, second, 0)
+    load_w(1).start()
     loads["a"].wait()
     make_chunk(0)
     service(0)
-    t_spread(0, nz // 2)
+    t_go(0)
     make_chunk(1)
     service(1)
-    t_spread(nz // 2, nz)
+    t_go(1)
+    t_spread(*quarter_of(0))
+    loads["z1"].start()
     back_second(0, 1, 2)
     service(2)
+    t_go(2)
+    t_spread(*quarter_of(1))
     back_second(3, 4)
     service(3)
     finish(0)
+    t_go(3)
+    t_spread(*quarter_of(2))
     make_chunk(2)
     service(4)
+    t_spread(*quarter_of(3))
     back_second(5, 6)
     service(5)
     back_second(7, 8)
@@ -1067,6 +1089,9 @@
     t_write()
     finish(5)
 
+    for q in range(9):
+        ig_save(q).wait()
+
     def t_drain(k, carry):
         t_core(k).wait_send()
         for step in range(1, cams):
@@ -1217,9 +1242,9 @@
         [(pos, f32), ((n_img, ch), f32), (pos, bf16), (pos, f32), ((n_img, ch), f32), ((2, n, per, wcols), bf16),
          ((8, ch), f32), (pos, bf16), ((rows // 2, ch), bf16), ((rows, ch), f32), ((obs, cams, ns, ch), bf16),
          (t_shape, bf16)],
-        [V, V, V, V, V, H, V, V, V, V, V, V],
+        [H, V, V, V, V, H, V, V, V, V, V, V],
         [H, V, H, H, V, H, V, H, V, V, V, H],
-        [pltpu.VMEM((n_img, wide), bf16), pltpu.VMEM((2, n, per, wcols), bf16), pltpu.VMEM(pos, f32),
+        [pltpu.VMEM((n_img // obs, 9, obs, ch), bf16), pltpu.VMEM((n_img, wide), bf16), pltpu.VMEM((2, n, per, wcols), bf16), pltpu.VMEM(pos, f32),
          pltpu.VMEM((n_img, wide), bf16), pltpu.VMEM(pos, f32), pltpu.VMEM((obs, cams, ns, ch), bf16),
          pltpu.VMEM((cams, obs, ns, ch), bf16), pltpu.VMEM(t_shape, bf16), pltpu.VMEM((2, min(per, 16), 2, wide), f32),
          pltpu.VMEM((BLK, per), f32), pltpu.VMEM((rows // 2, ch), bf16), pltpu.VMEM((rows + 4 * ns, ch), bf16),
@@ -1230,7 +1255,7 @@
          DMA((2, 2, nz)), DMA((2, nz)), DMA((2, nz)), DMA((2, nz)), DMA((2, ch // BLK)), DMA((11,)),
          DMA((cams,)), DMA((cams,)),
          DMA((2, nz)), DMA((nz,)), DMA((nz, cams)), DMA((nz, cams)), DMA((cams - 1, nz)), DMA((cams - 1, nz)),
-         DMA((max(per // 16, 1),)), DMA((9,)), DMA((cams,)), DMA((cams,)), DMA((4,))],
+         DMA((max(per // 16, 1),)), DMA((10,)), DMA((cams,)), DMA((cams,)), DMA((4,))],
         collective_id=0,
         cost=work(130),
     )(pairs, trajectory, out_grad, view_mask.astype(f32), time_embed(timesteps, TEMB), encoder_weight[0], block_convs,
@@ -1241,8 +1266,8 @@
         [(pos, f32), ((per, 2, wide), f32), ((4, per), f32), ((per, 2, 5 * ch), f32),
          ((per, 2, cond), f32), ((per, ch), f32), ((per, 3 * ch), f32), ((10, per), f32)],
         [H, H, H, H, V, H, V, V, V, H],
-        [V] * 8,
-        [pltpu.VMEM(pos, bf16), pltpu.VMEM(pos, bf16), pltpu.VMEM((n, per, wide), bf16), pltpu.VMEM(pos, f32),
+        [H] + [V] * 7,
+        [pltpu.VMEM(pos, f32), pltpu.VMEM(pos, bf16), pltpu.VMEM(pos, bf16), pltpu.VMEM((n, per, wide), bf16), pltpu.VMEM(pos, f32),
          pltpu.VMEM(pos, f32), pltpu.VMEM(pos, bf16), pltpu.VMEM((ch, 9 * n_img), bf16),
          pltpu.VMEM((BLK, ch), f32),
          pltpu.VMEM((2, nz, per, chunk), f32), pltpu.VMEM((2, nz, per, chunk), bf16),
@@ -1250,7 +1275,7 @@
          pltpu.VMEM((2, per, PART), bf16), pltpu.VMEM((nz, cams, per, PART), bf16),
          pltpu.VMEM((cams - 1, nz, per, PART), bf16), pltpu.VMEM((2, nz, per, PART), bf16),
          pltpu.VMEM((cams, per, PART), bf16),
-         DMA((13,)), DMA((6,)), DMA((6,)), DMA((6, 2, nz)), DMA((6, 2, nz)),
+         DMA((4,)), DMA((2, ch // BLK)), DMA((9,)), DMA((6,)), DMA((6,)), DMA((6, 2, nz)), DMA((6, 2, nz)),
          DMA((nz * cams,)), DMA((nz,)), DMA((nz,)), DMA((cams - 1, nz)), DMA((cams - 1, nz)),
          DMA((2, nz)), DMA((2, nz)), DMA((cams,)), DMA((cams,))],
         collective_id=1,

time: 308 us -> 302 us (0.981)
  Pallas kernels: 300 us -> 294 us
    pallas_call x1, Pallas kernels: 136 us -> 130 us  [shards(): call(functools.partial(enc_bwd_kernel, n, cams, cond), [(pos, f32), ((per...]
where the time goes in v8:
time: 302 us; the launch traced here: 298 us
  Pallas kernels  294 us (97%)
    pallas_call x1, Pallas kernels, shards(): call(functools.partial(forward_kernel, n, cams), [(pos, f32), ((n_img, ch...  145 us
    pallas_call x1, Pallas kernels, shards(): call(functools.partial(enc_bwd_kernel, n, cams, cond), [(pos, f32), ((per...  130 us
    pallas_call x1, Pallas kernels, last_call(): pl.pallas_call(last_kernel, grid=(steps,), out_shape=[jax.ShapeDtypeStruc...  18.2 us

profile of v8, /device:TPU:0, one launch (start us, length us, event | category | flops | bytes accessed | tf_op | source)
XLA Modules:
  0.0 297.9 jit_solution(2467063854029515602)
XLA Ops:
  0.7 0.7 convert_element_type.7
  1.3 0.7 convert_element_type.6
  2.0 0.7 copy.51.mask_ref
  2.7 0.1 multiply_sine_fusion
  2.9 0.7 pad_maximum_fusion.emb_ref
  3.5 145.2 %shard_map.433 = (f32[9,256,512]{2,1,0:T(8,128)}, f32[256,512]{1,0:T(8,128)}, bf16[9,256,512]{2,1,0:T(8,128)(2,1)}, f32[9,256,512]{2,1,0:T(8,128)}, f32[256,512]...) custom-call(bf16[128,9,2,512]{3,2,1,0:T(2,128)(2,1)} %bitcast.43, ...), custom_call_target="tpu_custom_call" | custom-call | flops 130000003072 | bytes 390000000 | tf_op jit(solution)/shard_map/pallas_call | solution.py:1240
  148.8 130.4 %shard_map.434 = (f32[9,256,512]{2,1,0:T(8,128)}, f32[64,2,4608]{2,1,0:T(2,128)}, f32[4,64]{1,0:T(4,128)}, f32[64,2,2560]{2,1,0:T(2,128)}, f32[64,2,1152]{2,1,0:...) custom-call(bf16[9,256,512]{2,1,0:T(8,128)(2,1)} %get-tuple-element.68.x_hbm, ...), custom_call_target="tpu_custom_call" | custom-call | flops 99999997952 | bytes 300000000 | tf_op jit(solution)/shard_map/pallas_call | solution.py:1264
  279.2 18.2 %shard_map.435 = (f32[64,2,4608]{2,1,0:T(2,128)}, f32[64,2,4608]{2,1,0:T(2,128)}, f32[64,2,4608]{2,1,0:T(2,128)}, f32[4,64]{1,0:T(4,128)}, f32[4,64]{1,0:T(4,128...) custom-call(f32[64,2,4608]{2,1,0:T(2,128)} %bitcast.45, ...), custom_call_target="tpu_custom_call" | custom-call | flops 15000000512 | bytes 45000000 | tf_op jit(solution)/shard_map/pallas_call | solution.py:1203
  (1 shorter events, 0.0 us)

commit v9 on v8

--- a/solution.py
+++ b/solution.py
@@ -89,11 +89,6 @@
     )
 
 
-def line_barrier(cams, nz):
-    line_greet(cams, nz)
-    line_wait(cams, nz)
-
-
 def line_wait(cams, nz):
     zi = lax.axis_index("batch") // 2
     ends = (zi == 0).astype(jnp.int32) + (zi == nz - 1).astype(jnp.int32)
@@ -120,24 +115,27 @@
 PART = 5 * CH
 
 
-def pack_temporal(ref, convs_ref, film_ref, skip_ref, down_ref, ext):
+def pack_part(q, ref, convs_ref, film_ref, skip_ref, down_ref, ext):
     rows, cond = film_ref.shape[0], film_ref.shape[2]
-    for q in range(2):
+    if q < 2:
         ref[q] = convs_ref[:, q, :].astype(bf16)
-        ref[2, :, q * cond : (q + 1) * cond] = film_ref[:, q, :].astype(bf16)
-    ref[2, :, 2 * cond : 2 * cond + BLK] = ext
-    ref[2, :, 2 * cond + BLK :] = jnp.zeros((rows, PART - 2 * cond - BLK), bf16)
-    ref[3, :, 0:CH] = skip_ref[...].astype(bf16)
-    ref[3, :, CH : 4 * CH] = down_ref[...].astype(bf16)
-    ref[3, :, 4 * CH :] = jnp.zeros((rows, PART - 4 * CH), bf16)
+    elif q == 2:
+        for which in range(2):
+            ref[2, :, which * cond : (which + 1) * cond] = film_ref[:, which, :].astype(bf16)
+        ref[2, :, 2 * cond : 2 * cond + BLK] = ext
+        ref[2, :, 2 * cond + BLK :] = jnp.zeros((rows, PART - 2 * cond - BLK), bf16)
+    else:
+        ref[3, :, 0:CH] = skip_ref[...].astype(bf16)
+        ref[3, :, CH : 4 * CH] = down_ref[...].astype(bf16)
+        ref[3, :, 4 * CH :] = jnp.zeros((rows, PART - 4 * CH), bf16)
 
 
 def forward_kernel(
-    n, cams, img_hbm, traj_ref, og_in, mask_ref, emb_ref, enc_hbm, convs_ref, film_ref, skip_ref, down_ref,
+    n, cams, img_hbm, traj_ref, og_in, mask_in, emb_ref, enc_hbm, convs_ref, film_ref, skip_ref, down_ref,
     ea_ref, ba_ref,
-    z1_out, r1_ref, a_out, z2_out, r2_ref, w_out, aff_ref, x_out, out_ref, tg_ref, gp_ref, dt_out,
+    z1_out, r1_ref, a_out, z2_out, r2_ref, w_out, aff_ref, x_out, slope_out, out_ref, tg_ref, gp_ref, dt_out,
     img_ref, x_ref, w_ref, z1_ref, a_ref, z2_ref, feat_ref, arr_s, t_ref, enc_buf,
-    ext_s, og_ref, pad_t, pad_m, pad_h, sum_ref, taff_ref, ag_ref, rstd_ref, dviews_ref, gp_s, dt_buf,
+    mask_s, ext_s, og_ref, pad_t, pad_m, pad_h, sum_ref, taff_ref, ag_ref, rstd_ref, dviews_ref, gp_s, dt_buf,
     zsend, zrecv, csend, crecv, wsem, osem, fsend, frecv,
     tzsend, tzrecv, tcsend, tcrecv, tpsend, tprecv, esem, xsem, vsend, vrecv, dsem,
 ):
@@ -162,9 +160,14 @@
     ext_s[0:4] = ea_ref[...]
     ext_s[4:14] = ba_ref[...]
     ext = jnp.transpose(ext_s[...]).astype(bf16)
-    pack_temporal(t_ref.at[zi, core], convs_ref, film_ref, skip_ref, down_ref, ext)
-
-    line_barrier(cams, nz)
+    line_greet(cams, nz)
+
+    def pack_own(q):
+        pack_part(q, t_ref.at[zi, core], convs_ref, film_ref, skip_ref, down_ref, ext)
+
+    for q in range(cams):
+        pl.when(cam == q)(functools.partial(pack_own, q))
+    line_wait(cams, nz)
 
     def tz_copy(k, way):
         ref = t_ref.at[k, core, cam]
@@ -327,7 +330,9 @@
         return cam_copy(dviews_ref.at[to], gp_s.at[:, sender], vsend.at[to], vrecv.at[sender], to)
 
     def temporal_rest():
-        mask = mask_ref[...]
+        mask_s[...] = jnp.zeros_like(mask_s)
+        mask_s[0:cams, 0:ns] = mask_in[...].astype(f32)
+        mask = jnp.transpose(mask_s[...])[0:ns, 0:cams]
         seen = jnp.sum(mask, axis=1, keepdims=True)
         conds, slopes = [], []
         for o in range(obs):
@@ -440,6 +445,8 @@
 
     t_send(0)
     for q in range(cams):
+        pl.when(cam != q)(functools.partial(pack_own, q))
+    for q in range(cams):
         tc_copy(zi, core, q).start()
     for conv in range(2):
         w_ref[conv, me, :, 9 * CH :] = ext
@@ -542,9 +549,11 @@
         for p in range(9):
             z = (z2_ref[p, :, lanes] - mean) * rstd
             z2_ref[p, :, lanes] = z
-            pic = x_ref[:, pl.ds(pl.multiple_of(p * CH + j * BLK, BLK), BLK)].astype(f32)
-            u = z * gain + offset + pic
-            act = u * sigmoid(u)
+            cols = pl.ds(pl.multiple_of(p * CH + j * BLK, BLK), BLK)
+            u = z * gain + offset + x_ref[:, cols].astype(f32)
+            s = sigmoid(u)
+            act = u * s
+            x_ref[:, cols] = (s + act * (1.0 - s)).astype(bf16)
             total = act if total is None else total + act
         out = (total * (1.0 / 9.0)).astype(bf16)
         feat_ref[:, :, :, lanes] = out.reshape(feat_ref.shape[:3] + (BLK,))
@@ -616,9 +625,17 @@
     ]
     for save in saves:
         save.start()
+    for p in range(9):
+        x_save(p).wait()
     phase(1, second)
     last = pltpu.make_async_copy(z2_ref, z2_out, osem.at[1])
     last.start()
+
+    def slope_save(p):
+        return pltpu.make_async_copy(x_ref.at[:, p * CH : (p + 1) * CH], slope_out.at[p], xsem.at[p])
+
+    for p in range(9):
+        slope_save(p).start()
 
     def feat_copy(to, sender):
         return cam_copy(feat_ref.at[:, to], arr_s.at[sender], fsend.at[to], frecv.at[sender], to)
@@ -681,13 +698,13 @@
 
     lax.fori_loop(0, nz, t_drain, 0)
     for p in range(9):
-        x_save(p).wait()
+        slope_save(p).wait()
     for step in range(1, cams):
         view_copy((cam + step) % cams, cam).wait_send()
 
 
 def enc_bwd_kernel(
-    n, cams, cond, x_hbm, a_hbm, w_hbm, z1_hbm, r1_ref, z2_hbm, r2_ref, aff_ref, gp_ref, dt_hbm,
+    n, cams, cond, x_hbm, slope_hbm, a_hbm, w_hbm, z1_hbm, r1_ref, z2_hbm, r2_ref, aff_ref, gp_ref, dt_hbm,
     ig_out, genc_ref, gaff_ref, gconvs_ref, gfilm_ref, gskip_ref, gdown_ref, gblk_ref,
     ig_ref, x_ref, a_ref, w_ref, z1_ref, z2_ref, g_ref, gt_ref, ag_ref,
     dwf, core_out, core_in, slots, t_own, t_sum, t_peer, t_slots, t_all,
@@ -714,12 +731,13 @@
         cols = lanes_of(j)
         return (
             pltpu.make_async_copy(z2_hbm.at[:, :, cols], z2_ref.at[:, :, cols], bsem.at[0, j]),
-            pltpu.make_async_copy(x_hbm.at[:, :, cols], x_ref.at[:, :, cols], bsem.at[1, j]),
+            pltpu.make_async_copy(slope_hbm.at[:, :, cols], g_ref.at[:, :, cols], bsem.at[1, j]),
         )
 
     loads = {
         "z1": pltpu.make_async_copy(z1_hbm, z1_ref, lsem.at[1]),
         "a": pltpu.make_async_copy(a_hbm, a_ref, lsem.at[2]),
+        "x": pltpu.make_async_copy(x_hbm, x_ref, lsem.at[0]),
     }
     for j in range(CH // BLK):
         for load in block_loads(j):
@@ -789,13 +807,10 @@
         lanes = lanes_of(j)
         for load in block_loads(j):
             load.wait()
-        gain, offset = aff_ref[2:3, lanes], aff_ref[3:4, lanes]
         pooled = gp_ref[:, :, :, lanes].reshape(n_img, BLK).astype(f32) * (1.0 / 9.0)
         for p in range(9):
-            u = z2_ref[p, :, lanes] * gain + offset + x_ref[p, :, lanes].astype(f32)
-            s = sigmoid(u)
-            ig_ref[p, :, lanes] = pooled * (s * (1.0 + u * (1.0 - s)))
-        norm_back(ig_ref, z2_ref, r2_ref, j, gain, 2)
+            ig_ref[p, :, lanes] = pooled * g_ref[p, :, lanes].astype(f32)
+        norm_back(ig_ref, z2_ref, r2_ref, j, aff_ref[2:3, lanes], 2)
         return carry
 
     def first(j, carry):
@@ -1009,13 +1024,13 @@
                 load_w(0).start()
 
     def ig_save(q):
-        return pltpu.make_async_copy(ig_ref.at[q], ig_out.at[q], isem.at[q])
+        return pltpu.make_async_copy(a_ref.at[q], ig_out.at[q], isem.at[q])
 
     def back_first(*qs):
         for q in qs:
             if q == 0:
                 load_w(0).wait()
-            ig_ref[q] = ig_ref[q] + input_back(q)
+            a_ref[q] = (ig_ref[q] + input_back(q)).astype(bf16)
             ig_save(q).start()
 
     def quarter_of(i):
@@ -1038,6 +1053,7 @@
     t_go(1)
     t_spread(*quarter_of(0))
     loads["z1"].start()
+    loads["x"].start()
     back_second(0, 1, 2)
     service(2)
     t_go(2)
@@ -1056,6 +1072,7 @@
     service(6)
     finish(1)
     loads["z1"].wait()
+    loads["x"].wait()
     lax.fori_loop(0, 2, first, 0)
     service(7)
     lax.fori_loop(2, 4, first, 0)
@@ -1154,7 +1171,7 @@
     tg_new, out_new, ig_new, turn_ref = refs[52:56]
     for p in range(ig_ref.shape[0]):
         for o in range(ig_ref.shape[1]):
-            ig_new[:, p, o, :] = ig_ref[p, o]
+            ig_new[:, p, o, :] = ig_ref[p, o].astype(f32)
 
     @pl.when(pl.program_id(0) == 0)
     def _():
@@ -1237,17 +1254,17 @@
     pos = (9, n_img, ch)
     t_shape = (nz, 2, cams, per, PART)
     wcols = wide + BLK
-    z1, r1, act, z2, r2, w_all, enc_aff, x, out_fm, tg_fm, gp, dt = call(
+    z1, r1, act, z2, r2, w_all, enc_aff, x, slope, out_fm, tg_fm, gp, dt = call(
         functools.partial(forward_kernel, n, cams),
         [(pos, f32), ((n_img, ch), f32), (pos, bf16), (pos, f32), ((n_img, ch), f32), ((2, n, per, wcols), bf16),
-         ((8, ch), f32), (pos, bf16), ((rows // 2, ch), bf16), ((rows, ch), f32), ((obs, cams, ns, ch), bf16),
+         ((8, ch), f32), (pos, bf16), (pos, bf16), ((rows // 2, ch), bf16), ((rows, ch), f32), ((obs, cams, ns, ch), bf16),
          (t_shape, bf16)],
         [H, V, V, V, V, H, V, V, V, V, V, V],
-        [H, V, H, H, V, H, V, H, V, V, V, H],
+        [H, V, H, H, V, H, V, H, H, V, V, V, H],
         [pltpu.VMEM((n_img // obs, 9, obs, ch), bf16), pltpu.VMEM((n_img, wide), bf16), pltpu.VMEM((2, n, per, wcols), bf16), pltpu.VMEM(pos, f32),
          pltpu.VMEM((n_img, wide), bf16), pltpu.VMEM(pos, f32), pltpu.VMEM((obs, cams, ns, ch), bf16),
          pltpu.VMEM((cams, obs, ns, ch), bf16), pltpu.VMEM(t_shape, bf16), pltpu.VMEM((2, min(per, 16), 2, wide), f32),
-         pltpu.VMEM((BLK, per), f32), pltpu.VMEM((rows // 2, ch), bf16), pltpu.VMEM((rows + 4 * ns, ch), bf16),
+         pltpu.VMEM((BLK, BLK), f32), pltpu.VMEM((BLK, per), f32), pltpu.VMEM((rows // 2, ch), bf16), pltpu.VMEM((rows + 4 * ns, ch), bf16),
          pltpu.VMEM((rows + 4 * ns, ch), bf16), pltpu.VMEM((rows + 4 * ns, ch), bf16), pltpu.VMEM((rows + ns, ch), bf16),
          pltpu.VMEM((BLK, ch), f32), pltpu.VMEM((BLK, ch), f32), pltpu.VMEM((ns, ch), f32),
          pltpu.VMEM((cams, obs, ns, ch), bf16), pltpu.VMEM((obs, cams, ns, ch), bf16),
@@ -1258,14 +1275,14 @@
          DMA((max(per // 16, 1),)), DMA((10,)), DMA((cams,)), DMA((cams,)), DMA((4,))],
         collective_id=0,
         cost=work(130),
-    )(pairs, trajectory, out_grad, view_mask.astype(f32), time_embed(timesteps, TEMB), encoder_weight[0], block_convs,
+    )(pairs, trajectory, out_grad, jnp.transpose(view_mask), time_embed(timesteps, TEMB), encoder_weight[0], block_convs,
       film_weight, skip_weight, down_weight, turned(encoder_affine), turned(block_affine))
     chunk = 3 * ch + BLK
     ig, genc, gaff, gconvs, gfilm, gskip, gdown, gblk = call(
         functools.partial(enc_bwd_kernel, n, cams, cond),
-        [(pos, f32), ((per, 2, wide), f32), ((4, per), f32), ((per, 2, 5 * ch), f32),
+        [(pos, bf16), ((per, 2, wide), f32), ((4, per), f32), ((per, 2, 5 * ch), f32),
          ((per, 2, cond), f32), ((per, ch), f32), ((per, 3 * ch), f32), ((10, per), f32)],
-        [H, H, H, H, V, H, V, V, V, H],
+        [H, H, H, H, H, V, H, V, V, V, H],
         [H] + [V] * 7,
         [pltpu.VMEM(pos, f32), pltpu.VMEM(pos, bf16), pltpu.VMEM(pos, bf16), pltpu.VMEM((n, per, wide), bf16), pltpu.VMEM(pos, f32),
          pltpu.VMEM(pos, f32), pltpu.VMEM(pos, bf16), pltpu.VMEM((ch, 9 * n_img), bf16),
@@ -1280,7 +1297,7 @@
          DMA((2, nz)), DMA((2, nz)), DMA((cams,)), DMA((cams,))],
         collective_id=1,
         cost=work(100),
-    )(x, act, w_all, z1, r1, z2, r2, enc_aff, gp, dt)
+    )(x, slope, act, w_all, z1, r1, z2, r2, enc_aff, gp, dt)
     weights = (encoder_weight, encoder_affine, block_convs, film_weight, skip_weight, down_weight, block_affine)
     firsts = (first_encoder, first_affine, first_convs, first_film, first_skip, first_down, first_block)
     seconds = (second_encoder, second_affine, second_convs, second_film, second_skip, second_down, second_block)

time: 302 us -> 297 us (0.983)
  no operation moved by 1% of the time
where the time goes in v9:
time: 297 us; the launch traced here: 293 us
  Pallas kernels  291 us (98%)
    pallas_call x1, Pallas kernels, shards(): call(functools.partial(forward_kernel, n, cams), [(pos, f32), ((n_img, ch...  144 us
    pallas_call x1, Pallas kernels, shards(): call(functools.partial(enc_bwd_kernel, n, cams, cond), [(pos, bf16), ((pe...  129 us
    pallas_call x1, Pallas kernels, last_call(): pl.pallas_call(last_kernel, grid=(steps,), out_shape=[jax.ShapeDtypeStruc...  17.8 us

profile of v9, /device:TPU:0, one launch (start us, length us, event | category | flops | bytes accessed | tf_op | source)
XLA Modules:
  0.0 293.2 jit_solution(5715414845067335736)
XLA Ops:
  0.7 0.7 convert_element_type.3
  1.3 0.1 multiply_sine_fusion
  1.5 0.7 pad_maximum_fusion.emb_ref
  2.2 144.2 %shard_map.433 = (f32[9,256,512]{2,1,0:T(8,128)}, f32[256,512]{1,0:T(8,128)}, bf16[9,256,512]{2,1,0:T(8,128)(2,1)}, f32[9,256,512]{2,1,0:T(8,128)}, f32[256,512]...) custom-call(bf16[128,9,2,512]{3,2,1,0:T(2,128)(2,1)} %bitcast.44, ...), custom_call_target="tpu_custom_call" | custom-call | flops 130000003072 | bytes 390000000 | tf_op jit(solution)/shard_map/pallas_call | solution.py:1257
  146.4 128.5 %shard_map.434 = (bf16[9,256,512]{2,1,0:T(8,128)(2,1)}, f32[64,2,4608]{2,1,0:T(2,128)}, f32[4,64]{1,0:T(4,128)}, f32[64,2,2560]{2,1,0:T(2,128)}, f32[64,2,1152]{...) custom-call(bf16[9,256,512]{2,1,0:T(8,128)(2,1)} %get-tuple-element.69.x_hbm, ...), custom_call_target="tpu_custom_call" | custom-call | flops 99999997952 | bytes 300000000 | tf_op jit(solution)/shard_map/pallas_call | solution.py:1281
  274.9 17.8 %shard_map.435 = (f32[64,2,4608]{2,1,0:T(2,128)}, f32[64,2,4608]{2,1,0:T(2,128)}, f32[64,2,4608]{2,1,0:T(2,128)}, f32[4,64]{1,0:T(4,128)}, f32[4,64]{1,0:T(4,128...) custom-call(f32[64,2,4608]{2,1,0:T(2,128)} %bitcast.46, ...), custom_call_target="tpu_custom_call" | custom-call | flops 15000000512 | bytes 45000000 | tf_op jit(solution)/shard_map/pallas_call | solution.py:1220
  (1 shorter events, 0.0 us)

commit v10 on v9

--- a/solution.py
+++ b/solution.py
@@ -466,6 +466,23 @@
 
     lax.fori_loop(0, count, pack, 0)
 
+    for conv in range(2):
+        core_copy(conv, zi, core).start()
+
+    def t_step(s, carry):
+        @pl.when(s == nz - 1)
+        def _():
+            send(0, 0)
+
+        t_receive(s)
+
+        @pl.when(s < nz - 1)
+        def _():
+            t_send(s)
+        return carry
+
+    lax.fori_loop(1, nz, t_step, 0)
+
     def x_save(p):
         return pltpu.make_async_copy(x_ref.at[:, p * CH : (p + 1) * CH], x_out.at[p], xsem.at[p])
 
@@ -483,22 +500,6 @@
         for o in range(2):
             x_ref[o * half : (o + 1) * half, p * CH : (p + 1) * CH] = pair[:, o].astype(bf16)
         x_save(p).start()
-    for conv in range(2):
-        core_copy(conv, zi, core).start()
-
-    def t_step(s, carry):
-        @pl.when(s == nz - 1)
-        def _():
-            send(0, 0)
-
-        t_receive(s)
-
-        @pl.when(s < nz - 1)
-        def _():
-            t_send(s)
-        return carry
-
-    lax.fori_loop(1, nz, t_step, 0)
 
     def rows_of(conv, j, start, wide):
         block = w_ref[conv, pl.ds(j * spb, spb), :, start : start + wide]
@@ -1046,6 +1047,7 @@
     load_w(1).start()
     loads["a"].wait()
     make_chunk(0)
+    back_second(0)
     service(0)
     t_go(0)
     make_chunk(1)
@@ -1054,7 +1056,7 @@
     t_spread(*quarter_of(0))
     loads["z1"].start()
     loads["x"].start()
-    back_second(0, 1, 2)
+    back_second(1, 2)
     service(2)
     t_go(2)
     t_spread(*quarter_of(1))

time: 297 us -> 293 us (0.987)
  Pallas kernels: 291 us -> 286 us
    pallas_call x1, Pallas kernels: 144 us -> 140 us  [shards(): call(functools.partial(forward_kernel, n, cams), [(pos, f32), ((n_img, ch...]
where the time goes in v10:
time: 293 us; the launch traced here: 289 us
  Pallas kernels  286 us (98%)
    pallas_call x1, Pallas kernels, shards(): call(functools.partial(forward_kernel, n, cams), [(pos, f32), ((n_img, ch...  140 us
    pallas_call x1, Pallas kernels, shards(): call(functools.partial(enc_bwd_kernel, n, cams, cond), [(pos, bf16), ((pe...  128 us
    pallas_call x1, Pallas kernels, last_call(): pl.pallas_call(last_kernel, grid=(steps,), out_shape=[jax.ShapeDtypeStruc...  17.8 us

profile of v10, /device:TPU:0, one launch (start us, length us, event | category | flops | bytes accessed | tf_op | source)
XLA Modules:
  0.0 288.7 jit_solution(6264939777929138125)
XLA Ops:
  0.7 0.7 convert_element_type.3
  1.3 0.1 multiply_sine_fusion
  1.5 0.7 pad_maximum_fusion.emb_ref
  2.2 140.0 %shard_map.433 = (f32[9,256,512]{2,1,0:T(8,128)}, f32[256,512]{1,0:T(8,128)}, bf16[9,256,512]{2,1,0:T(8,128)(2,1)}, f32[9,256,512]{2,1,0:T(8,128)}, f32[256,512]...) custom-call(bf16[128,9,2,512]{3,2,1,0:T(2,128)(2,1)} %bitcast.44, ...), custom_call_target="tpu_custom_call" | custom-call | flops 130000003072 | bytes 390000000 | tf_op jit(solution)/shard_map/pallas_call | solution.py:1259
  142.2 128.3 %shard_map.434 = (bf16[9,256,512]{2,1,0:T(8,128)(2,1)}, f32[64,2,4608]{2,1,0:T(2,128)}, f32[4,64]{1,0:T(4,128)}, f32[64,2,2560]{2,1,0:T(2,128)}, f32[64,2,1152]{...) custom-call(bf16[9,256,512]{2,1,0:T(8,128)(2,1)} %get-tuple-element.69.x_hbm, ...), custom_call_target="tpu_custom_call" | custom-call | flops 99999997952 | bytes 300000000 | tf_op jit(solution)/shard_map/pallas_call | solution.py:1283
  270.5 17.8 %shard_map.435 = (f32[64,2,4608]{2,1,0:T(2,128)}, f32[64,2,4608]{2,1,0:T(2,128)}, f32[64,2,4608]{2,1,0:T(2,128)}, f32[4,64]{1,0:T(4,128)}, f32[4,64]{1,0:T(4,128...) custom-call(f32[64,2,4608]{2,1,0:T(2,128)} %bitcast.46, ...), custom_call_target="tpu_custom_call" | custom-call | flops 15000000512 | bytes 45000000 | tf_op jit(solution)/shard_map/pallas_call | solution.py:1222
  (1 shorter events, 0.0 us)

commit v11 on v10

--- a/solution.py
+++ b/solution.py
@@ -392,8 +392,6 @@
             dwd[:, t * CH : (t + 1) * CH] = dot(og, cols).astype(bf16)
         dt_save(3, 0).start()
         out_ref[...] = (out + tail(9)).astype(bf16)
-        fill(pad_h, dha)
-        tg_ref[...] = tg_ref[...] + conv5_back(pad_h, wa)
         dt_save(1, 1).wait()
         for base, low in zip((0, cond), lows):
             dw = grad(1, base, cond)
@@ -408,6 +406,8 @@
         for t in range(5):
             dwa[:, t * CH : (t + 1) * CH] = dot(ha, pad_t[t * ns : t * ns + frows, :]).astype(bf16)
         dt_save(0, 0).start()
+        fill(pad_h, dha)
+        tg_ref[...] = tg_ref[...] + conv5_back(pad_h, wa)
         for step in range(1, cams):
             other = (cam + step) % cams
             view_copy(other, other).wait_recv()

time: 293 us -> 292 us (level)
  no operation moved by 1% of the time
where the time goes in v11:
time: 292 us; the launch traced here: 288 us
  Pallas kernels  286 us (98%)
    pallas_call x1, Pallas kernels, shards(): call(functools.partial(forward_kernel, n, cams), [(pos, f32), ((n_img, ch...  140 us
    pallas_call x1, Pallas kernels, shards(): call(functools.partial(enc_bwd_kernel, n, cams, cond), [(pos, bf16), ((pe...  128 us
    pallas_call x1, Pallas kernels, last_call(): pl.pallas_call(last_kernel, grid=(steps,), out_shape=[jax.ShapeDtypeStruc...  17.8 us

profile of v11, /device:TPU:0, one launch (start us, length us, event | category | flops | bytes accessed | tf_op | source)
XLA Modules:
  0.0 288.2 jit_solution(167646244790215333)
XLA Ops:
  0.7 0.7 convert_element_type.3
  1.3 0.1 multiply_sine_fusion
  1.5 0.7 pad_maximum_fusion.emb_ref
  2.2 139.6 %shard_map.433 = (f32[9,256,512]{2,1,0:T(8,128)}, f32[256,512]{1,0:T(8,128)}, bf16[9,256,512]{2,1,0:T(8,128)(2,1)}, f32[9,256,512]{2,1,0:T(8,128)}, f32[256,512]...) custom-call(bf16[128,9,2,512]{3,2,1,0:T(2,128)(2,1)} %bitcast.44, ...), custom_call_target="tpu_custom_call" | custom-call | flops 130000003072 | bytes 390000000 | tf_op jit(solution)/shard_map/pallas_call | solution.py:1259
  141.7 128.2 %shard_map.434 = (bf16[9,256,512]{2,1,0:T(8,128)(2,1)}, f32[64,2,4608]{2,1,0:T(2,128)}, f32[4,64]{1,0:T(4,128)}, f32[64,2,2560]{2,1,0:T(2,128)}, f32[64,2,1152]{...) custom-call(bf16[9,256,512]{2,1,0:T(8,128)(2,1)} %get-tuple-element.69.x_hbm, ...), custom_call_target="tpu_custom_call" | custom-call | flops 99999997952 | bytes 300000000 | tf_op jit(solution)/shard_map/pallas_call | solution.py:1283
  270.0 17.8 %shard_map.435 = (f32[64,2,4608]{2,1,0:T(2,128)}, f32[64,2,4608]{2,1,0:T(2,128)}, f32[64,2,4608]{2,1,0:T(2,128)}, f32[4,64]{1,0:T(4,128)}, f32[4,64]{1,0:T(4,128...) custom-call(f32[64,2,4608]{2,1,0:T(2,128)} %bitcast.46, ...), custom_call_target="tpu_custom_call" | custom-call | flops 15000000512 | bytes 45000000 | tf_op jit(solution)/shard_map/pallas_call | solution.py:1222
  (1 shorter events, 0.0 us)
